TPU v7x, 32 devices: a whole 2x2x4 slice. The times are simulated.
32 devices in a mesh: dp: 8 (over z, core), seq: 4 (over y, x).
Axes of the slice: x: 2, y: 2, z: 4, core: 2. Of those that a mesh axis runs over, the one named last changes fastest.
Arguments:
- token_ids: int32 [16, 1024], P('dp', 'seq'), may hold values from 0 to 127
- target_ids: int32 [16, 1024], P('dp', 'seq'), may hold values from 0 to 127
- prefix_lengths: int32 [16], P('dp'), may hold values from 128 to 960, as said below
- cluster_ids: int32 [16], P('dp'), may hold values from 0 to 63
- cluster_counts: int32 [64], replicated, may hold values from 1 to 8
- embedding: bfloat16 [128, 2048], P(('dp', 'seq')), may hold values from -0.25 to 0.25
- qkv_weight: bfloat16 [2048, 6144], P(('dp', 'seq')), may hold values from -4 to 4
- out_weight: bfloat16 [2048, 2048], P(('dp', 'seq')), may hold values from -0.375 to 0.375
- norm1_gain: bfloat16 [2048], P(('dp', 'seq')), may hold values from 0.5 to 1.5
- norm1_bias: bfloat16 [2048], P(('dp', 'seq')), may hold values from -1.25 to 1.25
- gate_weight: bfloat16 [2048, 5461], P(('dp', 'seq')), may hold values from -0.125 to 0.125
- up_weight: bfloat16 [2048, 5461], P(('dp', 'seq')), may hold values from -0.125 to 0.125
- down_weight: bfloat16 [2048, 5461], P(('dp', 'seq')), may hold values from -0.4375 to 0.4375
- norm2_gain: bfloat16 [2048], P(('dp', 'seq')), may hold values from 0.5 to 1.5
- norm2_bias: bfloat16 [2048], P(('dp', 'seq')), may hold values from -1.25 to 1.25
Outputs:
- activations: bfloat16 [16, 1024, 2048], P('dp', 'seq')
- input_grad: float32 [16, 1024, 2048], P('dp', 'seq')
- embedding_grad: float32 [128, 2048], P(('dp', 'seq'))
- qkv_grad: float32 [2048, 6144], P(('dp', 'seq'))
- out_grad: float32 [2048, 2048], P(('dp', 'seq'))
- norm1_gain_grad: float32 [2048], P(('dp', 'seq'))
- norm1_bias_grad: float32 [2048], P(('dp', 'seq'))
- gate_grad: float32 [2048, 5461], P(('dp', 'seq'))
- up_grad: float32 [2048, 5461], P(('dp', 'seq'))
- down_grad: float32 [2048, 5461], P(('dp', 'seq'))
- norm2_gain_grad: float32 [2048], P(('dp', 'seq'))
- norm2_bias_grad: float32 [2048], P(('dp', 'seq'))
Inputs may be any that keep to these rules, and one draw needn't show every extreme that they name: `prefix_lengths`: one sequence of the batch has a prefix of exactly 960 residues.
All inputs are finite; a program needn't handle non-finite values.
Results may differ from a plain program's by a relative error of at most 0.015.
Values may be sent and summed in bfloat16 or wider, within the bound.
No kernel may reach another device: no remote copies, remote signals or barrier semaphores. Data moves between devices by JAX's collectives and lax.ppermute only.
A program may use at most 448 MiB of HBM per device.

v0:
```python
import math

import jax
import jax.numpy as jnp
from jax import lax
from jax.sharding import PartitionSpec as P

HEADS = 16
HEAD = 128


deep_alpha = math.sqrt(48.0)
loss_scale = 1024.0
norm_epsilon = 1e-05
lookup_scale = 0.1


def layer_norm(inputs_row, gain_row, bias_row):
    centred = inputs_row - jnp.mean(inputs_row, axis=-1, keepdims=True)
    spread_sq = jnp.mean(centred * centred, axis=-1, keepdims=True)
    return centred * lax.rsqrt(spread_sq + norm_epsilon) * gain_row + bias_row


def rotary_angles(positions, head_size):
    halves = head_size // 2
    freqs = jnp.power(
        jnp.float32(10000.0), -2.0 * jnp.arange(halves, dtype=jnp.float32) / head_size
    )
    return positions.astype(jnp.float32)[:, None] * freqs[None, :]


def rotate(field, angles):
    halves = field.shape[-1] // 2
    cosine = jnp.cos(angles)[:, None, :]
    sine = jnp.sin(angles)[:, None, :]
    first_half = field[..., :halves]
    second_half = field[..., halves:]
    return jnp.concatenate(
        [first_half * cosine - second_half * sine, second_half * cosine + first_half * sine],
        axis=-1,
    )


def unrotate(grads, angles):
    halves = grads.shape[-1] // 2
    cosine = jnp.cos(angles)[:, None, :]
    sine = jnp.sin(angles)[:, None, :]
    first_half = grads[..., :halves]
    second_half = grads[..., halves:]
    return jnp.concatenate(
        [first_half * cosine + second_half * sine, second_half * cosine - first_half * sine],
        axis=-1,
    )


def gated_gelu(gate_in, up_in):
    return jax.nn.gelu(gate_in, approximate=True) * up_in


def weighted_head(
    activations,
    embed_table,
    target_ids,
    prefix_lengths,
    cluster_ids,
    cluster_counts,
    positions,
    seq_len,
    vocab_ids,
):
    contract_rows = (((0,), (0,)), ((), ()))
    contract_last = (((1,), (1,)), ((), ()))
    row_count = activations.shape[0]
    logits = lax.dot_general(
        activations, embed_table, contract_last, preferred_element_type=jnp.float32
    )
    cluster_hot = (
        cluster_ids[:, None] == jnp.arange(cluster_counts.shape[0], dtype=jnp.int32)[None, :]
    )
    seq_weight = 1.0 / jnp.sum(jnp.where(cluster_hot, cluster_counts[None, :], 0), axis=1).astype(
        jnp.float32
    )
    counted = (positions[None, :] >= prefix_lengths[:, None]).astype(jnp.float32)
    coefs = (
        loss_scale
        * seq_weight[:, None]
        / (seq_len - prefix_lengths)[:, None].astype(jnp.float32)
        * counted
    )
    logit_top = jnp.max(logits, axis=-1, keepdims=True)
    logit_exp = jnp.exp(logits - logit_top)
    logit_probs = logit_exp / jnp.sum(logit_exp, axis=-1, keepdims=True)
    target_hot = (target_ids.reshape(row_count)[:, None] == vocab_ids[None, :]).astype(jnp.float32)
    d_logits = (coefs.reshape(row_count, 1) * (logit_probs - target_hot)).astype(jnp.bfloat16)
    head_grad = lax.dot_general(
        d_logits, activations, contract_rows, preferred_element_type=jnp.float32
    )
    d_normed = jnp.dot(d_logits, embed_table, preferred_element_type=jnp.float32)
    return (head_grad, d_normed)


def on_device(
    token_ids,
    target_ids,
    prefix_lengths,
    cluster_ids,
    cluster_counts,
    embedding,
    qkv_weight,
    out_weight,
    norm1_gain,
    norm1_bias,
    gate_weight,
    up_weight,
    down_weight,
    norm2_gain,
    norm2_bias,
):
    seqs_here, local_len = token_ids.shape
    row_count = seqs_here * local_len
    seq_len = local_len * lax.axis_size("seq")
    first_pos = lax.axis_index("seq") * local_len
    positions = first_pos + jnp.arange(local_len, dtype=jnp.int32)
    angles = rotary_angles(positions, HEAD)
    score_scale = 1.0 / math.sqrt(HEAD)
    contract_rows = (((0,), (0,)), ((), ()))
    contract_last = (((1,), (1,)), ((), ()))
    qkv_full, out_full, gain_one, bias_one, embed_table = (
        lax.all_gather(qkv_weight, ("dp", "seq"), axis=0, tiled=True),
        lax.all_gather(out_weight, ("dp", "seq"), axis=0, tiled=True),
        lax.all_gather(norm1_gain, ("dp", "seq"), axis=0, tiled=True),
        lax.all_gather(norm1_bias, ("dp", "seq"), axis=0, tiled=True),
        lax.all_gather(embedding, ("dp", "seq"), axis=0, tiled=True),
    )
    vocab_ids = jnp.arange(embed_table.shape[0], dtype=jnp.int32)
    token_hot = token_ids.reshape(row_count)[:, None] == vocab_ids[None, :]
    inputs_low = jnp.dot(
        token_hot.astype(jnp.bfloat16), embed_table, preferred_element_type=jnp.float32
    ).astype(jnp.bfloat16)
    inputs_full = inputs_low.astype(jnp.float32)
    width = inputs_low.shape[1]
    qkv_value = jnp.dot(inputs_low, qkv_full, preferred_element_type=jnp.float32).reshape(
        seqs_here, local_len, 3, HEADS, HEAD
    )
    queries = rotate(qkv_value[:, :, 0], angles).astype(jnp.bfloat16)
    keys_local = rotate(qkv_value[:, :, 1], angles).astype(jnp.bfloat16)
    values_local = qkv_value[:, :, 2].astype(jnp.bfloat16)
    keys_all, values_all = (
        lax.all_gather(keys_local, "seq", axis=1, tiled=True),
        lax.all_gather(values_local, "seq", axis=1, tiled=True),
    )
    key_pos = jnp.arange(seq_len, dtype=jnp.int32)
    visible = (key_pos[None, None, :] < prefix_lengths[:, None, None]) | (
        key_pos[None, None, :] <= positions[None, :, None]
    )
    visible = visible[:, None]

    def masked_scores(keys_in):
        raw_scores = (
            jnp.einsum("sqhe,skhe->shqk", queries, keys_in, preferred_element_type=jnp.float32)
            * score_scale
        )
        return jnp.where(visible, raw_scores, -1e30)

    scores = masked_scores(keys_all)
    top_score = jnp.max(scores, axis=-1, keepdims=True)
    expo = jnp.exp(scores - top_score)
    row_total = jnp.sum(expo, axis=-1, keepdims=True)
    log_total = top_score + jnp.log(row_total)
    probs_low = (expo / row_total).astype(jnp.bfloat16)
    context = jnp.einsum(
        "shqk,skhe->sqhe", probs_low, values_all, preferred_element_type=jnp.float32
    )
    context = context.reshape(row_count, width).astype(jnp.bfloat16)
    attention = jnp.dot(context, out_full, preferred_element_type=jnp.float32)
    hidden, norm_one_pull = jax.vjp(
        layer_norm,
        deep_alpha * inputs_full + attention,
        gain_one.astype(jnp.float32),
        bias_one.astype(jnp.float32),
    )
    gate_full, up_full, down_full, gain_two, bias_two = (
        lax.all_gather(gate_weight, ("dp", "seq"), axis=0, tiled=True),
        lax.all_gather(up_weight, ("dp", "seq"), axis=0, tiled=True),
        lax.all_gather(down_weight, ("dp", "seq"), axis=0, tiled=True),
        lax.all_gather(norm2_gain, ("dp", "seq"), axis=0, tiled=True),
        lax.all_gather(norm2_bias, ("dp", "seq"), axis=0, tiled=True),
    )
    hidden_low = hidden.astype(jnp.bfloat16)
    gate_value = jnp.dot(hidden_low, gate_full, preferred_element_type=jnp.float32)
    up_value = jnp.dot(hidden_low, up_full, preferred_element_type=jnp.float32)
    product_full, gelu_pull = jax.vjp(gated_gelu, gate_value, up_value)
    product = product_full.astype(jnp.bfloat16)
    branch = lax.dot_general(product, down_full, contract_last, preferred_element_type=jnp.float32)
    normed, norm_two_pull = jax.vjp(
        layer_norm,
        deep_alpha * hidden + branch,
        gain_two.astype(jnp.float32),
        bias_two.astype(jnp.float32),
    )
    activations = normed.astype(jnp.bfloat16)
    head_grad, d_normed = weighted_head(
        activations,
        embed_table,
        target_ids,
        prefix_lengths,
        cluster_ids,
        cluster_counts,
        positions,
        seq_len,
        vocab_ids,
    )
    back_gate, back_up, back_down = (
        lax.all_gather(gate_weight, ("dp", "seq"), axis=0, tiled=True),
        lax.all_gather(up_weight, ("dp", "seq"), axis=0, tiled=True),
        lax.all_gather(down_weight, ("dp", "seq"), axis=0, tiled=True),
    )
    d_second, d_gain_two, d_bias_two = norm_two_pull(d_normed)
    d_branch = d_second.astype(jnp.bfloat16)
    down_grad_part = lax.dot_general(
        d_branch, product, contract_rows, preferred_element_type=jnp.float32
    )
    d_product = jnp.dot(d_branch, back_down, preferred_element_type=jnp.float32)
    d_gate, d_up = gelu_pull(d_product)
    d_gate_low = d_gate.astype(jnp.bfloat16)
    d_up_low = d_up.astype(jnp.bfloat16)
    gate_grad_part = lax.dot_general(
        hidden_low, d_gate_low, contract_rows, preferred_element_type=jnp.float32
    )
    up_grad_part = lax.dot_general(
        hidden_low, d_up_low, contract_rows, preferred_element_type=jnp.float32
    )
    d_hidden = deep_alpha * d_second
    d_hidden = d_hidden + lax.dot_general(
        d_gate_low, back_gate, contract_last, preferred_element_type=jnp.float32
    )
    d_hidden = d_hidden + lax.dot_general(
        d_up_low, back_up, contract_last, preferred_element_type=jnp.float32
    )
    gate_grad, up_grad, down_grad, norm2_gain_grad, norm2_bias_grad = (
        lax.psum_scatter(gate_grad_part, ("dp", "seq"), scatter_dimension=0, tiled=True),
        lax.psum_scatter(up_grad_part, ("dp", "seq"), scatter_dimension=0, tiled=True),
        lax.psum_scatter(down_grad_part, ("dp", "seq"), scatter_dimension=0, tiled=True),
        lax.psum_scatter(d_gain_two, ("dp", "seq"), scatter_dimension=0, tiled=True),
        lax.psum_scatter(d_bias_two, ("dp", "seq"), scatter_dimension=0, tiled=True),
    )
    back_qkv, back_out = (
        lax.all_gather(qkv_weight, ("dp", "seq"), axis=0, tiled=True),
        lax.all_gather(out_weight, ("dp", "seq"), axis=0, tiled=True),
    )
    d_first, d_gain_one, d_bias_one = norm_one_pull(d_hidden)
    d_attention = d_first.astype(jnp.bfloat16)
    out_grad_part = lax.dot_general(
        context, d_attention, contract_rows, preferred_element_type=jnp.float32
    )
    d_context = lax.dot_general(
        d_attention, back_out, contract_last, preferred_element_type=jnp.float32
    )
    d_context = d_context.astype(jnp.bfloat16).reshape(seqs_here, local_len, HEADS, HEAD)
    keys_back, values_back = (keys_all, values_all)
    probs_again = jnp.exp(masked_scores(keys_back) - log_total)
    probs_again_low = probs_again.astype(jnp.bfloat16)
    d_probs = jnp.einsum(
        "sqhe,skhe->shqk", d_context, values_back, preferred_element_type=jnp.float32
    )
    inner = jnp.sum(probs_again * d_probs, axis=-1, keepdims=True)
    d_scores = (probs_again * (d_probs - inner)).astype(jnp.bfloat16)
    d_queries = (
        jnp.einsum("shqk,skhe->sqhe", d_scores, keys_back, preferred_element_type=jnp.float32)
        * score_scale
    )
    d_keys_part = (
        jnp.einsum("shqk,sqhe->skhe", d_scores, queries, preferred_element_type=jnp.float32)
        * score_scale
    )
    d_values_part = jnp.einsum(
        "shqk,sqhe->skhe", probs_again_low, d_context, preferred_element_type=jnp.float32
    )
    d_keys, d_values = (
        lax.psum_scatter(
            d_keys_part.astype(jnp.bfloat16), "seq", scatter_dimension=1, tiled=True
        ).astype(jnp.float32),
        lax.psum_scatter(
            d_values_part.astype(jnp.bfloat16), "seq", scatter_dimension=1, tiled=True
        ).astype(jnp.float32),
    )
    d_qkv = jnp.stack([unrotate(d_queries, angles), unrotate(d_keys, angles), d_values], axis=2)
    d_qkv = d_qkv.reshape(row_count, 3 * width).astype(jnp.bfloat16)
    qkv_grad_part = lax.dot_general(
        inputs_low, d_qkv, contract_rows, preferred_element_type=jnp.float32
    )
    input_grad = deep_alpha * d_first + lax.dot_general(
        d_qkv, back_qkv, contract_last, preferred_element_type=jnp.float32
    )
    lookup_grad = lax.dot_general(
        token_hot.astype(jnp.float32),
        input_grad,
        contract_rows,
        precision=lax.Precision.HIGHEST,
        preferred_element_type=jnp.float32,
    )
    embed_grad_part = lookup_scale * lookup_grad + head_grad
    embedding_grad, qkv_grad, out_grad, norm1_gain_grad, norm1_bias_grad = (
        lax.psum_scatter(embed_grad_part, ("dp", "seq"), scatter_dimension=0, tiled=True),
        lax.psum_scatter(qkv_grad_part, ("dp", "seq"), scatter_dimension=0, tiled=True),
        lax.psum_scatter(out_grad_part, ("dp", "seq"), scatter_dimension=0, tiled=True),
        lax.psum_scatter(d_gain_one, ("dp", "seq"), scatter_dimension=0, tiled=True),
        lax.psum_scatter(d_bias_one, ("dp", "seq"), scatter_dimension=0, tiled=True),
    )
    return (
        activations.reshape(seqs_here, local_len, width),
        input_grad.reshape(seqs_here, local_len, width),
        embedding_grad,
        qkv_grad,
        out_grad,
        norm1_gain_grad,
        norm1_bias_grad,
        gate_grad,
        up_grad,
        down_grad,
        norm2_gain_grad,
        norm2_bias_grad,
    )


def solution(mesh):
    return jax.shard_map(
        on_device,
        mesh=mesh,
        in_specs=(
            P("dp", "seq"),
            P("dp", "seq"),
            P("dp"),
            P("dp"),
            P(),
            P(("dp", "seq"), None),
            P(("dp", "seq"), None),
            P(("dp", "seq"), None),
            P(("dp", "seq")),
            P(("dp", "seq")),
            P(("dp", "seq"), None),
            P(("dp", "seq"), None),
            P(("dp", "seq"), None),
            P(("dp", "seq")),
            P(("dp", "seq")),
        ),
        out_specs=(
            P("dp", "seq", None),
            P("dp", "seq", None),
            P(("dp", "seq"), None),
            P(("dp", "seq"), None),
            P(("dp", "seq"), None),
            P(("dp", "seq")),
            P(("dp", "seq")),
            P(("dp", "seq"), None),
            P(("dp", "seq"), None),
            P(("dp", "seq"), None),
            P(("dp", "seq")),
            P(("dp", "seq")),
        ),
        check_vma=False,
    )
```

profile of v0, /device:TPU:9, one launch (start us, length us, event | category | flops | bytes accessed | tf_op | source)
XLA Modules:
  0.0 5107.0 jit_solution(17225579147689738112)
XLA Ops:
  8.6 58.7 %all-gather.1 = bf16[32,4,2048]{2,1,0:T(4,128)(2,1)S(1)} all-gather(bf16[1,4,2048]{2,1,0:T(4,128)(2,1)} %bitcast.101), channel_id=1, replica_groups=mesh['dp'=8,'seq'=4] {'dp','seq'}, dimensions={0}, use_global_device_ids=true | all-gather | bytes 540672 | tf_op jit(solution)/shard_map/all_gather | solution.py:133
  68.9 101.0 %all-gather.10.cloned.1.call-done = bf16[2048,6144]{1,0:T(8,128)(2,1)} async-done(((bf16[64,6144]{1,0:T(8,128)(2,1)}), bf16[2048,6144]{1,0:T(8,128)(2,1)}) %all-gather.10.cloned.1.call-update) | async-done | bytes 25165840 | tf_op jit(solution)/shard_map/all_gather | solution.py:129
  169.9 20.6 convolution_bitcast_fusion
  190.6 11.8 copy.87
  202.4 4.1 fusion.43
  206.5 2.6 copy_bitcast_fusion
  209.1 15.5 subtract_convert_fusion.3
  224.6 2.5 pad_maximum_fusion.2
  227.2 3.8 slice.45
  231.0 4.4 copy.85
  240.5 40.7 all-reduce.10
  282.9 32.9 all-gather.12.cloned.1.call-done
  315.8 19.4 fusion.44
  335.2 14.3 fusion
  349.5 55.6 %all-gather.22.cloned.1.call-done = bf16[2,1024,1,16,128]{1,4,3,0,2:T(8,128)(2,1)} async-done(((bf16[2,256,1,16,128]{1,4,3,0,2:T(8,128)(2,1)}), bf16[2,1024,1,16,128]{1,4,3,0,2:T(8,128)(2,1)}) %all-gather.22.cloned.1.call-update) | async-done | bytes 8388624 | tf_op jit(solution)/shard_map/all_gather | solution.py:150
  405.1 17.1 convert_bitcast_fusion.1
  422.2 4.6 copy.67
  426.9 58.8 %all-gather.14.cloned.1.call-done = bf16[2048,2048]{1,0:T(8,128)(2,1)} async-done(((bf16[64,2048]{1,0:T(8,128)(2,1)}), bf16[2048,2048]{1,0:T(8,128)(2,1)}) %all-gather.14.cloned.1.call-update) | async-done | bytes 8388624 | tf_op jit(solution)/shard_map/all_gather | solution.py:130
  485.7 7.7 fusion.45
  496.2 131.1 %all-gather.16.cloned.1.call-done = bf16[2048,5461]{1,0:T(8,128)(2,1)} async-done(((bf16[64,5461]{1,0:T(8,128)(2,1)}), bf16[2048,5461]{1,0:T(8,128)(2,1)}) %all-gather.16.cloned.1.call-update) | async-done | bytes 22368272 | tf_op jit(solution)/shard_map/all_gather | solution.py:183
  627.3 18.8 fusion.48
  646.1 124.2 %all-gather.18.cloned.1.call-done = bf16[2048,5461]{1,0:T(8,128)(2,1)} async-done(((bf16[64,5461]{1,0:T(8,128)(2,1)}), bf16[2048,5461]{1,0:T(8,128)(2,1)}) %all-gather.18.cloned.1.call-update) | async-done | bytes 22368272 | tf_op jit(solution)/shard_map/all_gather | solution.py:184
  770.3 30.5 multiply_convert_fusion.3
  800.9 112.6 %all-gather.20.cloned.1.call-done = bf16[2048,5461]{1,0:T(8,128)(2,1)} async-done(((bf16[64,5461]{1,0:T(8,128)(2,1)}), bf16[2048,5461]{1,0:T(8,128)(2,1)}) %all-gather.20.cloned.1.call-update) | async-done | bytes 22368272 | tf_op jit(solution)/shard_map/all_gather | solution.py:185
  913.4 21.0 fusion.46
  934.4 2.9 multiply_reduce_fusion.5
  939.6 2.1 multiply_reduce_fusion.1
  942.9 29.3 multiply_convert_fusion.2
  972.3 19.6 fusion.49
  991.8 21.0 multiply_reduce_fusion.2
  1014.1 9.8 fusion.27
  1023.9 2.0 copy.91
  1025.9 3.0 copy.74
  1028.9 25.4 multiply_reduce_fusion
  1054.3 27.8 multiply_convert_fusion
  1082.1 14.1 fusion.13
  1096.3 16.8 convert_bitcast_fusion
  1113.2 15.5 multiply_bitcast_fusion
  1128.7 53.5 %reduce-scatter.8.cloned.1.call-done = bf16[2,256,16,128]{3,1,2,0:T(8,128)(2,1)} async-done(((bf16[2,1024,16,128]{3,1,2,0:T(8,128)(2,1)}), bf16[2,256,16,128]{3,1,2,0:T(8,128)(2,1)}) %reduce-scatter.8.cloned.1.call-update) | async-done | bytes 2097168 | tf_op jit(solution)/shard_map/reduce_scatter | solution.py:280
  1182.3 2.2 convert_element_type.136
  1185.1 3.2 add_convert_fusion.1
  1189.5 2.5 maximum_bitcast_fusion.1
  1192.0 80.1 %reduce-scatter.10.cloned.1.call-done = bf16[2,256,16,128]{3,1,2,0:T(8,128)(2,1)} async-done(((bf16[2,1024,16,128]{3,1,2,0:T(8,128)(2,1)}), bf16[2,256,16,128]{3,1,2,0:T(8,128)(2,1)}) %reduce-scatter.10.cloned.1.call-update) | async-done | bytes 2097168 | tf_op jit(solution)/shard_map/reduce_scatter | solution.py:283
  1272.1 3.4 pad_maximum_fusion
  1275.4 6.6 copy.76
  1282.1 10.1 convert_element_type.140
  1292.2 19.2 multiply_add_fusion
  1311.3 2.0 copy-done.9
  1313.4 1.8 convolution_multiply_fusion
  1315.2 1.5 convolution_add_fusion
  1316.8 13.3 fusion.20
  1330.2 1.5 copy-done.17
  1331.7 22.6 fusion.50
  1355.0 23.3 fusion.39
  1378.3 1.5 copy-done.19
  1379.9 20.6 fusion.52
  1400.6 20.8 fusion.51
  1422.1 41.5 all-reduce.9
  1466.0 1.5 constant_dynamic-slice_fusion
  1467.4 339.4 %reduce-scatter.14.cloned.1.call-done = f32[64,2048]{1,0:T(8,128)} async-done(((f32[2048,2048]{1,0:T(8,128)}), f32[64,2048]{1,0:T(8,128)}) %reduce-scatter.14.cloned.1.call-update) | async-done | bytes 524304 | tf_op jit(solution)/shard_map/reduce_scatter | solution.py:306
  1806.8 439.6 %reduce-scatter.12.cloned.1.call-done = f32[64,6144]{1,0:T(8,128)} async-done(((f32[2048,6144]{1,0:T(8,128)}), f32[64,6144]{1,0:T(8,128)}) %reduce-scatter.12.cloned.1.call-update) | async-done | bytes 1572880 | tf_op jit(solution)/shard_map/reduce_scatter | solution.py:305
  2246.3 950.1 %reduce-scatter.20.cloned.1.call-done = f32[64,5461]{1,0:T(8,128)} async-done(((f32[2048,5461]{1,0:T(8,128)}), f32[64,5461]{1,0:T(8,128)}) %reduce-scatter.20.cloned.1.call-update) | async-done | bytes 1398032 | tf_op jit(solution)/shard_map/reduce_scatter | solution.py:243
  3196.5 951.9 %reduce-scatter.18.cloned.1.call-done = f32[64,5461]{1,0:T(8,128)} async-done(((f32[2048,5461]{1,0:T(8,128)}), f32[64,5461]{1,0:T(8,128)}) %reduce-scatter.18.cloned.1.call-update) | async-done | bytes 1398032 | tf_op jit(solution)/shard_map/reduce_scatter | solution.py:242
  4148.4 951.9 %reduce-scatter.16.cloned.1.call-done = f32[64,5461]{1,0:T(8,128)} async-done(((f32[2048,5461]{1,0:T(8,128)}), f32[64,5461]{1,0:T(8,128)}) %reduce-scatter.16.cloned.1.call-update) | async-done | bytes 1398032 | tf_op jit(solution)/shard_map/reduce_scatter | solution.py:241
  (179 shorter events, 22.9 us)
Async XLA Ops:
  7.2 162.7 %all-gather.10.cloned.1.call-start = ((), (), s32[]{:S(2)}) async-start(), calls=%async_computation.7 | async-start | bytes 25952256 | tf_op jit(solution)/shard_map/all_gather | solution.py:129
  7.9 307.9 %all-gather.12.cloned.1.call-start = ((), (), s32[]{:S(2)}) async-start(), calls=%async_computation.8 | async-start | bytes 10485760 | tf_op jit(solution)/shard_map/all_gather | solution.py:149
  8.6 181.9 %copy-start.30 = (s32[1,2,2,128]{3,1,2,0:T(2,128)}, s32[1,2,2,128]{3,1,2,0:T(2,128)S(1)}, u32[]{:S(2)}) copy-start(s32[1,2,2,128]{3,1,2,0:T(2,128)S(1)} %copy.86) | copy-start | bytes 6148
  67.5 123.1 %copy-start.7 = (bf16[128,2048]{1,0:T(8,128)(2,1)}, bf16[128,2048]{1,0:T(8,128)(2,1)S(1)}, u32[]{:S(2)}) copy-start(bf16[128,2048]{1,0:T(8,128)(2,1)S(1)} %reshape.281) | copy-start | bytes 1572868
  68.1 141.0 %copy-start.20 = (f32[256,64]{1,0:T(8,128)}, f32[256,64]{1,0:T(8,128)S(1)}, u32[]{:S(2)}) copy-start(f32[256,64]{1,0:T(8,128)S(1)} %get-tuple-element.46) | copy-start | bytes 196612
  68.1 141.0 %copy-start.22 = (f32[256,64]{1,0:T(8,128)}, f32[256,64]{1,0:T(8,128)S(1)}, u32[]{:S(2)}) copy-start(f32[256,64]{1,0:T(8,128)S(1)} %get-tuple-element.47) | copy-start | bytes 196612
  68.9 121.7 %copy-start.15 = (bf16[512,2048]{1,0:T(8,128)(2,1)}, bf16[512,2048]{1,0:T(8,128)(2,1)S(1)}, u32[]{:S(2)}) copy-start(bf16[512,2048]{1,0:T(8,128)(2,1)S(1)} %convolution_convert_fusion.1) | copy-start | bytes 6291460
  224.6 91.2 %copy-start.3 = (bf16[2,256,16,64]{3,1,2,0:T(8,128)(2,1)}, bf16[2,256,16,64]{3,1,2,0:T(8,128)(2,1)S(1)}, u32[]{:S(2)}) copy-start(bf16[2,256,16,64]{3,1,2,0:T(8,128)(2,1)S(1)} %get-tuple-element.38) | copy-start | bytes 3145732
  227.1 178.0 %all-gather.22.cloned.1.call-start = ((), (), s32[]{:S(2)}) async-start(), calls=%async_computation.20 | async-start | bytes 10485760 | tf_op jit(solution)/shard_map/all_gather | solution.py:150
  231.0 7.1 copy-start.46
  231.0 7.1 copy-start.47
  231.0 7.3 copy-start.45
  231.0 8.0 copy-start.42
  231.0 8.5 copy-start.48
  231.0 8.7 copy-start.49
  231.0 9.0 copy-start.50
  231.0 9.2 copy-start.51
  235.5 250.2 %all-gather.14.cloned.1.call-start = ((), (), s32[]{:S(2)}) async-start(), calls=%async_computation.9 | async-start | bytes 8650752 | tf_op jit(solution)/shard_map/all_gather | solution.py:130
  236.1 391.2 %all-gather.16.cloned.1.call-start = ((), (), s32[]{:S(2)}) async-start(), calls=%async_computation.10 | async-start | bytes 23248896 | tf_op jit(solution)/shard_map/all_gather | solution.py:183
  236.7 533.6 %all-gather.18.cloned.1.call-start = ((), (), s32[]{:S(2)}) async-start(), calls=%async_computation.11 | async-start | bytes 23248896 | tf_op jit(solution)/shard_map/all_gather | solution.py:184
  237.2 676.2 %all-gather.20.cloned.1.call-start = ((), (), s32[]{:S(2)}) async-start(), calls=%async_computation.12 | async-start | bytes 23248896 | tf_op jit(solution)/shard_map/all_gather | solution.py:185
  238.0 944.3 %reduce-scatter.8.cloned.1.call-start = ((), (), s32[]{:S(2)}) async-start(), calls=%async_computation.13 | async-start | bytes 10485760 | tf_op jit(solution)/shard_map/reduce_scatter | solution.py:280
  422.2 63.4 %copy-start.16 = (bf16[512,2048]{1,0:T(8,128)(2,1)S(1)}, bf16[512,2048]{1,0:T(8,128)(2,1)}, u32[]{:S(2)}) copy-start(bf16[512,2048]{1,0:T(8,128)(2,1)} %copy-done.15) | copy-start | bytes 6291460
  493.4 2.0 copy-start
  494.0 152.1 %copy-start.26 = (f32[512]{0:T(512)}, f32[512]{0:T(512)S(1)}, u32[]{:S(2)}) copy-start(f32[512]{0:T(512)S(1)} %multiply_reduce_fusion.6) | copy-start | bytes 6148
  496.2 274.1 %copy-start.18 = (bf16[512,2048]{1,0:T(8,128)(2,1)}, bf16[512,2048]{1,0:T(8,128)(2,1)S(1)}, u32[]{:S(2)}) copy-start(bf16[512,2048]{1,0:T(8,128)(2,1)S(1)} %fusion.19) | copy-start | bytes 6291460
  913.4 23.9 copy-start.25
  934.4 3.4 copy-start.2
  934.4 3.4 copy-start.24
  937.3 1.3 copy-start.8
  937.8 1.8 copy-start.34
  937.9 1.8 copy-start.36
  938.6 3.1 copy-start.4
  939.5 2.2 copy-start.12
  939.5 2.2 copy-start.28
  939.6 2.2 copy-start.32
  942.9 29.4 copy-start.10
  942.9 48.9 copy-start.43
  991.8 21.0 copy-start.27
  991.8 21.0 copy-start.1
  1014.0 9.9 copy-start.11
  1023.9 5.0 copy-start.14
  1096.3 175.8 %reduce-scatter.10.cloned.1.call-start = ((), (), s32[]{:S(2)}) async-start(), calls=%async_computation.14 | async-start | bytes 10485760 | tf_op jit(solution)/shard_map/reduce_scatter | solution.py:283
  1113.2 352.8 %all-reduce.13.cloned.1.call-start = ((), (), s32[]{:S(2)}) async-start(), calls=%async_computation.21 | async-start | bytes 2097152
  1128.7 55.8 %copy-start.21 = (f32[256,64]{1,0:T(8,128)S(1)}, f32[256,64]{1,0:T(8,128)}, u32[]{:S(2)}) copy-start(f32[256,64]{1,0:T(8,128)} %copy-done.20) | copy-start | bytes 196612
  1128.7 55.8 %copy-start.23 = (f32[256,64]{1,0:T(8,128)S(1)}, f32[256,64]{1,0:T(8,128)}, u32[]{:S(2)}) copy-start(f32[256,64]{1,0:T(8,128)} %copy-done.22) | copy-start | bytes 196612
  1182.3 2.8 copy-start.6
  1292.2 21.2 copy-start.31
  1311.3 2.0 copy-start.9
  1313.4 1.8 copy-start.5
  1313.4 1.8 copy-start.13
  1313.4 1.8 copy-start.29
  1313.4 1.8 copy-start.33
  1313.4 1.8 copy-start.35
  1313.4 1.8 copy-start.37
  1316.8 490.0 %reduce-scatter.14.cloned.1.call-start = ((), (), s32[]{:S(2)}) async-start(), calls=%async_computation.16 | async-start | bytes 17301504 | tf_op jit(solution)/shard_map/reduce_scatter | solution.py:306
  1330.1 1.6 copy-start.17
  1330.1 916.2 %reduce-scatter.12.cloned.1.call-start = ((), (), s32[]{:S(2)}) async-start(), calls=%async_computation.15 | async-start | bytes 51904512 | tf_op jit(solution)/shard_map/reduce_scatter | solution.py:305
  1354.3 1842.2 %reduce-scatter.20.cloned.1.call-start = ((), (), s32[]{:S(2)}) async-start(), calls=%async_computation.19 | async-start | bytes 46497792 | tf_op jit(solution)/shard_map/reduce_scatter | solution.py:243
  1378.3 1.6 copy-start.19
  1378.3 2770.1 %reduce-scatter.18.cloned.1.call-start = ((), (), s32[]{:S(2)}) async-start(), calls=%async_computation.18 | async-start | bytes 46497792 | tf_op jit(solution)/shard_map/reduce_scatter | solution.py:242
  1400.5 3699.8 %reduce-scatter.16.cloned.1.call-start = ((), (), s32[]{:S(2)}) async-start(), calls=%async_computation.17 | async-start | bytes 46497792 | tf_op jit(solution)/shard_map/reduce_scatter | solution.py:241
  1421.3 0.7 copy-start.40
  1421.3 0.7 copy-start.41
  (3 other events, 2.1 us)
Sparse Core Ops, SparseCore 0:
  10.9 158.9 all-gather.9
  227.2 88.5 all-gather.11
  317.6 87.4 all-gather.21
  407.9 77.7 all-gather.13
  488.3 138.9 all-gather.15
  630.0 140.2 all-gather.17
  773.1 140.2 all-gather.19
  1096.4 85.8 reduce-scatter.7
  1185.6 86.3 reduce-scatter.9
  1316.9 127.8 all-reduce.12
  1447.8 358.9 reduce-scatter.13
  1814.8 431.5 reduce-scatter.11
  2249.3 947.0 reduce-scatter.19
  3199.3 949.0 reduce-scatter.17
  4151.2 949.0 reduce-scatter.15
where the time goes:
time: 5110 us
  waiting for transfers between devices  4390 us (86%)
  matrix products  414 us (8%)
  blocking collectives  141 us (3%)
  other arithmetic  83.6 us (2%)
  local copies, waits for them, and re-layouts  67.7 us (1%)
    reduce_scatter x1, waiting for transfers between devices, on_device(): lax.psum_scatter(up_grad_part, ('dp', 'seq'), scatter_dimension=0, tiled=...  952 us
    reduce_scatter x1, waiting for transfers between devices, on_device(): lax.psum_scatter(gate_grad_part, ('dp', 'seq'), scatter_dimension=0, tile...  952 us
    reduce_scatter x1, waiting for transfers between devices, on_device(): lax.psum_scatter(down_grad_part, ('dp', 'seq'), scatter_dimension=0, tile...  950 us
    reduce_scatter x1, waiting for transfers between devices, on_device(): lax.psum_scatter(qkv_grad_part, ('dp', 'seq'), scatter_dimension=0, tiled...  440 us
    reduce_scatter x1, waiting for transfers between devices, on_device(): lax.psum_scatter(out_grad_part, ('dp', 'seq'), scatter_dimension=0, tiled...  339 us
    all_gather x1, waiting for transfers between devices, on_device(): lax.all_gather(gate_weight, ('dp', 'seq'), axis=0, tiled=True)  131 us
    all_gather x1, waiting for transfers between devices, on_device(): lax.all_gather(up_weight, ('dp', 'seq'), axis=0, tiled=True)  124 us
    all_gather x1, waiting for transfers between devices, on_device(): lax.all_gather(down_weight, ('dp', 'seq'), axis=0, tiled=True)  113 us
  transfers between devices with their start and end apart: 15, of which 14 were waited for; matrix products, arithmetic and copies ran while one was open for 5% of the time, Pallas kernels for 0%

commit v1 on v0

v1 whole, which is shorter than its diff:
```python
import math

import jax
import jax.numpy as jnp
from jax import lax
from jax.sharding import PartitionSpec as P

HEADS = 16
HEAD = 128
LANES = 128

deep_alpha = math.sqrt(48.0)
loss_scale = 1024.0
norm_epsilon = 1e-05
lookup_scale = 0.1
score_scale = 1.0 / math.sqrt(HEAD)

bf16 = jnp.bfloat16
f32 = jnp.float32
BOTH = ("dp", "seq")
ROWS = (((0,), (0,)), ((), ()))
LAST = (((1,), (1,)), ((), ()))


def dot(left, right, dims=(((1,), (0,)), ((), ()))):
    return lax.dot_general(left, right, dims, preferred_element_type=f32)


def layer_norm(inputs_row, gain_row, bias_row):
    centred = inputs_row - jnp.mean(inputs_row, axis=-1, keepdims=True)
    spread_sq = jnp.mean(centred * centred, axis=-1, keepdims=True)
    return centred * lax.rsqrt(spread_sq + norm_epsilon) * gain_row + bias_row


def rotary_angles(positions, head_size):
    halves = head_size // 2
    freqs = jnp.power(10000.0, -2.0 * jnp.arange(halves, dtype=f32) / head_size)
    return positions.astype(f32)[:, None] * freqs[None, :]


def rotate(field, cosine, sine):
    halves = field.shape[-1] // 2
    first, second = field[..., :halves], field[..., halves:]
    return jnp.concatenate([first * cosine - second * sine, second * cosine + first * sine], axis=-1)


def gated_gelu(gate_in, up_in):
    return jax.nn.gelu(gate_in, approximate=True) * up_in


def exchange(blocks, axes):
    return lax.all_to_all(blocks, axes, split_axis=0, concat_axis=0, tiled=True)


def spread(block, axes):
    count = lax.axis_size(axes)
    return exchange(jnp.broadcast_to(block[None], (count,) + block.shape), axes)


def swap(block, bits):
    return lax.ppermute(block, "seq", [(s, s ^ bits) for s in range(lax.axis_size("seq"))])


def gather_tokens(block):
    if lax.axis_size("seq") != 4:
        return [block] + [swap(block, k) for k in range(1, lax.axis_size("seq"))]
    half = block.shape[0] // 2
    near = swap(block, 1)
    over = swap(block, 2)
    far = jnp.concatenate([swap(near[:half], 2), swap(over[half:], 1)], axis=0)
    return [block, near, over, far]


def scatter_tokens(parts):
    if lax.axis_size("seq") != 4:
        return parts[0] + sum(swap(p.astype(bf16), k).astype(f32) for k, p in enumerate(parts) if k)
    own, near, over, far = parts
    half = own.shape[0] // 2
    far_low = far.astype(bf16)
    by_near = swap(far_low[:half], 1)
    by_over = swap(far_low[half:], 2)
    over = jnp.concatenate([over[:half] + by_near.astype(f32), over[half:]], axis=0)
    near = jnp.concatenate([near[:half], near[half:] + by_over.astype(f32)], axis=0)
    from_over = swap(over.astype(bf16), 2)
    from_near = swap(near.astype(bf16), 1)
    return own + from_over.astype(f32) + from_near.astype(f32)


def on_device(
    token_ids,
    target_ids,
    prefix_lengths,
    cluster_ids,
    cluster_counts,
    embedding,
    qkv_weight,
    out_weight,
    norm1_gain,
    norm1_bias,
    gate_weight,
    up_weight,
    down_weight,
    norm2_gain,
    norm2_bias,
):
    seqs, local_len = token_ids.shape
    count = seqs * local_len
    groups = lax.axis_size("seq")
    dps = lax.axis_size("dp")
    devices = groups * dps
    seq_len = local_len * groups
    my_seq = lax.axis_index("seq")
    my_dp = lax.axis_index("dp")
    positions = my_seq * local_len + jnp.arange(local_len, dtype=jnp.int32)
    rows = qkv_weight.shape[0]
    width = embedding.shape[1]
    vocab_here = embedding.shape[0]
    vocab = vocab_here * devices
    hidden_units = gate_weight.shape[1]
    share = -(-hidden_units // (groups * LANES)) * LANES
    heads_here = HEADS // groups
    head_cols = heads_here * HEAD

    pack = jnp.concatenate(
        [
            embedding.reshape(-1),
            norm1_gain,
            norm1_bias,
            norm2_gain,
            norm2_bias,
            token_ids.reshape(-1).astype(bf16),
        ]
    )
    packs = spread(pack, BOTH)
    table_size = vocab_here * width
    embed_table = packs[:, :table_size].reshape(vocab, width)
    norms = packs[:, table_size : table_size + 4 * rows].reshape(devices, 4, rows)
    norms = norms.transpose(1, 0, 2).reshape(4, width).astype(f32)
    gain_one, bias_one, gain_two, bias_two = norms[0], norms[1], norms[2], norms[3]
    tokens_all = lax.dynamic_slice_in_dim(packs[:, table_size + 4 * rows :], my_dp * groups, groups, 0)
    tokens_all = tokens_all.reshape(groups, seqs, local_len).transpose(1, 0, 2)
    tokens_all = tokens_all.reshape(seqs * seq_len).astype(jnp.int32)
    vocab_ids = jnp.arange(vocab, dtype=jnp.int32)
    token_hot = (token_ids.reshape(count)[:, None] == vocab_ids[None, :]).astype(bf16)
    all_hot = (tokens_all[:, None] == vocab_ids[None, :]).astype(bf16)

    qkv_cols = qkv_weight.reshape(rows, 3, groups, head_cols).transpose(2, 0, 1, 3)
    qkv_cols = exchange(qkv_cols, "seq").reshape(groups * rows, 3 * head_cols)
    out_full = lax.all_gather(out_weight, BOTH, axis=0, tiled=True)

    def columns(weight):
        padded = jnp.pad(weight, ((0, 0), (0, groups * share - hidden_units)))
        return padded.reshape(rows, groups, share).transpose(1, 0, 2)

    ff_cols = jnp.concatenate([columns(gate_weight), columns(up_weight), columns(down_weight)], axis=2)
    ff_cols = exchange(ff_cols, "seq").reshape(groups * rows, 3 * share)
    gate_up_w = lax.all_gather(ff_cols[:, : 2 * share], "dp", axis=0, tiled=True)
    down_w = lax.all_gather(ff_cols[:, 2 * share :], "dp", axis=0, tiled=True)
    qkv_w = lax.all_gather(qkv_cols, "dp", axis=0, tiled=True)

    embed_dp = lax.dynamic_slice_in_dim(embed_table, my_dp * groups * rows, groups * rows, 1)
    qkv_part = dot(embed_dp, qkv_cols).reshape(dps, vocab // dps, 3 * head_cols)
    qkv_rows = jnp.sum(exchange(qkv_part, "dp"), axis=0)
    qkv_high = qkv_rows.astype(bf16)
    qkv_rest = (qkv_rows - qkv_high.astype(f32)).astype(bf16)
    qkv_table = spread(jnp.stack([qkv_high, qkv_rest]), "dp")
    qkv_table = qkv_table.transpose(1, 0, 2, 3).reshape(2 * vocab, 3 * head_cols)
    qkv_value = dot(jnp.concatenate([all_hot, all_hot], axis=1), qkv_table)
    qkv_value = qkv_value.reshape(seqs, seq_len, 3, heads_here, HEAD)
    angles = rotary_angles(jnp.arange(seq_len, dtype=jnp.int32), HEAD)
    cosine, sine = jnp.cos(angles)[:, None, :], jnp.sin(angles)[:, None, :]
    queries = rotate(qkv_value[:, :, 0], cosine, sine).astype(bf16)
    keys = rotate(qkv_value[:, :, 1], cosine, sine).astype(bf16)
    values = qkv_value[:, :, 2].astype(bf16)

    key_pos = jnp.arange(seq_len, dtype=jnp.int32)
    visible = (key_pos[None, None, :] < prefix_lengths[:, None, None]) | (
        key_pos[None, None, :] <= key_pos[None, :, None]
    )
    scores = jnp.einsum("sqhe,skhe->shqk", queries, keys, preferred_element_type=f32) * score_scale
    scores = jnp.where(visible[:, None], scores, -1e30)
    top_score = jnp.max(scores, axis=-1, keepdims=True)
    expo = jnp.exp(scores - top_score)
    probs = expo / jnp.sum(expo, axis=-1, keepdims=True)
    probs_low = probs.astype(bf16)
    context = jnp.einsum("shqk,skhe->sqhe", probs_low, values, preferred_element_type=f32)
    context = context.astype(bf16).reshape(seqs, groups, local_len, head_cols).transpose(1, 0, 2, 3)
    context = exchange(context, "seq").reshape(groups, count, head_cols)
    context = context.transpose(1, 0, 2).reshape(count, width)

    inputs = dot(token_hot, embed_table)
    hidden, norm_one_pull = jax.vjp(
        layer_norm, deep_alpha * inputs + dot(context, out_full), gain_one, bias_one
    )

    hidden_all = jnp.concatenate(gather_tokens(hidden.astype(bf16)), axis=0)
    gate_up = dot(hidden_all, gate_up_w)
    product_full, gelu_pull = jax.vjp(gated_gelu, gate_up[:, :share], gate_up[:, share:])
    product = product_full.astype(bf16)
    branch = scatter_tokens(jnp.split(dot(product, down_w, LAST), groups))
    normed, norm_two_pull = jax.vjp(layer_norm, deep_alpha * hidden + branch, gain_two, bias_two)
    activations = normed.astype(bf16)

    logits = dot(activations, embed_table, LAST)
    cluster_hot = cluster_ids[:, None] == jnp.arange(cluster_counts.shape[0], dtype=jnp.int32)[None, :]
    members = jnp.sum(jnp.where(cluster_hot, cluster_counts[None, :], 0), axis=1).astype(f32)
    counted = (positions[None, :] >= prefix_lengths[:, None]).astype(f32)
    coefs = (
        loss_scale
        * (1.0 / members)[:, None]
        / (seq_len - prefix_lengths)[:, None].astype(f32)
        * counted
    )
    logit_exp = jnp.exp(logits - jnp.max(logits, axis=-1, keepdims=True))
    logit_probs = logit_exp / jnp.sum(logit_exp, axis=-1, keepdims=True)
    target_hot = (target_ids.reshape(count)[:, None] == vocab_ids[None, :]).astype(f32)
    d_logits = (coefs.reshape(count, 1) * (logit_probs - target_hot)).astype(bf16)
    head_grad = dot(d_logits, activations, ROWS)
    d_second, d_gain_two, d_bias_two = norm_two_pull(dot(d_logits, embed_table))

    d_branch = jnp.concatenate(gather_tokens(d_second.astype(bf16)), axis=0)
    d_gate, d_up = gelu_pull(dot(d_branch, down_w))
    d_gate_up = jnp.concatenate([d_gate.astype(bf16), d_up.astype(bf16)], axis=1)
    d_hidden = scatter_tokens(jnp.split(dot(d_gate_up, gate_up_w, LAST), groups))
    d_hidden = d_hidden + deep_alpha * d_second
    down_part = dot(d_branch, product, ROWS).astype(bf16)
    gate_up_part = dot(hidden_all, d_gate_up, ROWS).astype(bf16)

    def own_rows(part, parts):
        mine = lax.psum_scatter(part, "dp", scatter_dimension=0, tiled=True)
        mine = exchange(mine.reshape(groups, rows, parts, share), "seq")
        mine = mine.transpose(2, 1, 0, 3).reshape(parts, rows, groups * share)
        return mine[:, :, :hidden_units].astype(f32)

    (down_grad,) = own_rows(down_part, 1)
    gate_grad, up_grad = own_rows(gate_up_part, 2)

    d_first, d_gain_one, d_bias_one = norm_one_pull(d_hidden)
    d_attention = d_first.astype(bf16)
    out_part = dot(context, d_attention, ROWS).astype(bf16)
    out_grad = lax.psum_scatter(
        lax.psum_scatter(out_part, "dp", scatter_dimension=0, tiled=True),
        "seq",
        scatter_dimension=0,
        tiled=True,
    ).astype(f32)
    d_context = dot(d_attention, out_full, LAST).astype(bf16)
    d_context = d_context.reshape(count, groups, head_cols).transpose(1, 0, 2)
    d_context = exchange(d_context, "seq").reshape(groups, seqs, local_len, head_cols)
    d_context = d_context.transpose(1, 0, 2, 3).reshape(seqs, seq_len, heads_here, HEAD)
    d_probs = jnp.einsum("sqhe,skhe->shqk", d_context, values, preferred_element_type=f32)
    inner = jnp.sum(probs * d_probs, axis=-1, keepdims=True)
    d_scores = (probs * (d_probs - inner)).astype(bf16)
    d_queries = jnp.einsum("shqk,skhe->sqhe", d_scores, keys, preferred_element_type=f32)
    d_keys = jnp.einsum("shqk,sqhe->skhe", d_scores, queries, preferred_element_type=f32)
    d_values = jnp.einsum("shqk,sqhe->skhe", probs_low, d_context, preferred_element_type=f32)
    d_qkv = jnp.stack(
        [
            rotate(d_queries * score_scale, cosine, -sine),
            rotate(d_keys * score_scale, cosine, -sine),
            d_values,
        ],
        axis=2,
    )
    d_qkv = d_qkv.astype(bf16).reshape(seqs * seq_len, 3 * head_cols)

    input_part = dot(d_qkv, qkv_w, LAST).reshape(seqs, groups, local_len, width)
    input_part = input_part.transpose(1, 0, 2, 3).reshape(groups, count, width)
    input_part = exchange(input_part.astype(bf16), "seq")
    input_grad = deep_alpha * d_first + jnp.sum(input_part.astype(f32), axis=0)

    qkv_sums = dot(all_hot, d_qkv, ROWS)
    sums_high = qkv_sums.astype(bf16)
    sums_rest = (qkv_sums - sums_high.astype(f32)).astype(bf16)
    lookup = dot(
        jnp.concatenate([sums_high, sums_rest], axis=1), jnp.concatenate([qkv_w, qkv_w], axis=1), LAST
    )
    lookup_first = lax.dot_general(
        token_hot.astype(f32),
        d_first,
        ROWS,
        precision=lax.Precision.HIGHEST,
        preferred_element_type=f32,
    )
    embed_part = lookup_scale * (lookup + deep_alpha * lookup_first) + head_grad
    norm_part = jnp.stack([d_gain_one, d_bias_one, d_gain_two, d_bias_two])
    norm_part = norm_part.reshape(4, devices, rows).transpose(1, 0, 2).reshape(devices, 4 * rows)
    small = jnp.concatenate([embed_part.reshape(devices, table_size), norm_part], axis=1)
    small = jnp.sum(exchange(small, BOTH), axis=0)
    embedding_grad = small[:table_size].reshape(vocab_here, width)
    norm_grads = small[table_size:].reshape(4, rows)

    sums_mine = jnp.sum(exchange(qkv_sums.reshape(dps, vocab // dps, 3 * head_cols), "dp"), axis=0)
    sums_all = spread(sums_mine.astype(bf16), BOTH)
    sums_all = sums_all.reshape(dps, groups, vocab // dps, 3, head_cols)
    sums_all = sums_all.transpose(0, 2, 3, 1, 4).reshape(vocab, 3 * width)
    embed_rows = lax.dynamic_slice_in_dim(embed_table, (my_dp * groups + my_seq) * rows, rows, 1)
    qkv_grad = dot(embed_rows, sums_all, ROWS)

    return (
        activations.reshape(seqs, local_len, width),
        input_grad.reshape(seqs, local_len, width),
        embedding_grad,
        qkv_grad,
        out_grad,
        norm_grads[0],
        norm_grads[1],
        gate_grad,
        up_grad,
        down_grad,
        norm_grads[2],
        norm_grads[3],
    )


def solution(mesh):
    split = P(BOTH, None)
    line = P(BOTH)
    return jax.shard_map(
        on_device,
        mesh=mesh,
        in_specs=(
            P("dp", "seq"),
            P("dp", "seq"),
            P("dp"),
            P("dp"),
            P(),
            split,
            split,
            split,
            line,
            line,
            split,
            split,
            split,
            line,
            line,
        ),
        out_specs=(
            P("dp", "seq", None),
            P("dp", "seq", None),
            split,
            split,
            split,
            line,
            line,
            split,
            split,
            split,
            line,
            line,
        ),
        check_vma=False,
    )
```

time: 5110 us -> 1230 us (0.24)
  waiting for transfers between devices: 4390 us -> 515 us
  blocking collectives: 141 us -> 30.4 us
  starting transfers between devices: 0.6 us -> 89.6 us
  matrix products: 414 us -> 327 us
  local copies, waits for them, and re-layouts: 67.7 us -> 137 us
    reduce_scatter x7 -> x4, waiting for transfers between devices: 3770 us -> 22.1 us  [the longest x1 22.1 us: on_device(): lax.psum_scatter(lax.psum_scatter(out_part, 'dp', scatter_dimension=0, ti...]
    all_gather x7 -> x4, waiting for transfers between devices: 616 us -> 0.01 us  [the longest x1 0.01 us: on_device(): out_full = lax.all_gather(out_weight, BOTH, axis=0, tiled=True)]
    ppermute x0 -> x16, waiting for transfers between devices: none -> 247 us  [swap(): lax.ppermute(block, 'seq', [(s, s ^ bits) for s in range(lax.axis_size('s...]
    all_to_all x0 -> x12, waiting for transfers between devices: none -> 244 us  [exchange(): return lax.all_to_all(blocks, axes, split_axis=0, concat_axis=0, tiled=True)]
    dot_general x26 -> x25, matrix products: 414 us -> 308 us  [the longest x19 228 us: dot(): return lax.dot_general(left, right, dims, preferred_element_type=f32)]
    unnamed x2 -> x0, blocking collectives: 82.2 us -> none
    all_to_all x0 -> x12, starting transfers between devices: none -> 69.2 us  [exchange(): return lax.all_to_all(blocks, axes, split_axis=0, concat_axis=0, tiled=True)]
    all_gather x1 -> x0, blocking collectives: 58.7 us -> none  [on_device(): lax.all_gather(embedding, ('dp', 'seq'), axis=0, tiled=True)]
  transfers between devices with their start and end apart: 15 -> 36, of which waited for: 14 -> 23; matrix products, arithmetic and copies ran while one was open for 5% -> 42% of each run, Pallas kernels for 0% -> 0%
where the time goes in v1:
time: 1230 us; the launch traced here: 1220 us
  waiting for transfers between devices  515 us (42%)
  matrix products  327 us (27%)
  local copies, waits for them, and re-layouts  137 us (11%)
  other arithmetic  108 us (9%)
  starting transfers between devices  89.6 us (7%)
  blocking collectives  30.4 us (2%)
  between operations  15.9 us (1%)
    ppermute x16, waiting for transfers between devices, swap(): lax.ppermute(block, 'seq', [(s, s ^ bits) for s in range(lax.axis_size('s...  247 us
    all_to_all x12, waiting for transfers between devices, exchange(): return lax.all_to_all(blocks, axes, split_axis=0, concat_axis=0, tiled=True)  244 us
    dot_general x19, matrix products, dot(): return lax.dot_general(left, right, dims, preferred_element_type=f32)  228 us
    all_to_all x12, starting transfers between devices, exchange(): return lax.all_to_all(blocks, axes, split_axis=0, concat_axis=0, tiled=True)  69.2 us
    unnamed x136, local copies, waits for them, and re-layouts  34 us
    convert_element_type x3, local copies, waits for them, and re-layouts, on_device(): d_qkv = d_qkv.astype(bf16).reshape(seqs * seq_len, 3 * head_cols)  32.9 us
    all_to_all x1, blocking collectives, exchange(): return lax.all_to_all(blocks, axes, split_axis=0, concat_axis=0, tiled=True)  30.4 us
    convert_element_type x1, other arithmetic, on_device(): d_scores = (probs * (d_probs - inner)).astype(bf16)  28.9 us
  transfers between devices with their start and end apart: 36, of which 23 were waited for; matrix products, arithmetic and copies ran while one was open for 42% of the time, Pallas kernels for 0%

profile of v1, /device:TPU:9, one launch (start us, length us, event | category | flops | bytes accessed | tf_op | source)
XLA Modules:
  0.0 1222.5 jit_solution(16222685291583163406)
XLA Ops:
  13.3 30.4 %all_to_all.73 = bf16[4,64,4224]{2,1,0:T(8,128)(2,1)S(1)} all-to-all(bf16[4,64,4224]{2,1,0:T(8,128)(2,1)S(1)} %copy.157), channel_id=1, replica_groups=mesh['dp'=8,'seq'=4] {'seq'}, dimensions={0} | all-to-all | bytes 4325376 | tf_op jit(solution)/shard_map/all_to_all | solution.py:52
  52.8 4.1 reduce.17
  61.2 7.0 all-to-all-start
  70.0 28.6 %all-to-all-done = bf16[32,2,4480]{2,1,0:T(2,128)(2,1)} async-done(((bf16[32,2,4480]{2,1,0:T(2,128)(2,1)}), bf16[32,2,4480]{2,1,0:T(2,128)(2,1)}, u32[]{:S(2)}, u32[]{:S(2)}) %all-to-all-start) | async-done | bytes 573472 | tf_op jit(solution)/shard_map/all_to_all | solution.py:52
  98.5 3.7 reshape.509
  104.8 5.1 all-to-all-start.2
  110.3 35.5 %all-to-all-done.2 = f32[8,16,1536]{2,1,0:T(8,128)S(1)} async-done(((f32[8,16,1536]{2,1,0:T(8,128)}), f32[8,16,1536]{2,1,0:T(8,128)S(1)}, u32[]{:S(2)}, u32[]{:S(2)}) %all-to-all-start.2) | async-done | bytes 786464 | tf_op jit(solution)/shard_map/all_to_all | solution.py:52
  146.9 6.5 all-to-all-start.3
  159.1 35.3 %all-to-all-done.3 = bf16[8,2,16,1536]{3,2,1,0:T(8,128)(2,1)S(1)} async-done(((bf16[8,2,16,1536]{3,2,1,0:T(8,128)(2,1)}), bf16[8,2,16,1536]{3,2,1,0:T(8,128)(2,1)S(1)}, u32[]{:S(2)}, u32[]{:S(2)}) %all-to-all-start.3) | async-done | bytes 786464 | tf_op jit(solution)/shard_map/all_to_all | solution.py:52
  201.8 3.7 subtract_convert_fusion.1
  205.5 18.9 %fusion.101 = (f32[2,4,1024]{2,1,0:T(4,128)S(1)}, f32[2,4,1024,1024]{2,3,1,0:T(8,128)}) fusion(pred[2,1024,1024]{1,2,0:T(8,128)(4,1)} %broadcast_or_fusion, bf16[2,1024,4,64]{1,3,2,0:T(8,128)(2,1)} %get-tuple-element.65, bf16[2,1024,4,64]{1,3,2,0:T(8,128)(2,1)} %get-tuple-element.66, bf16[2,1024,4,64]{1,3,2,0:T(8,128)(2,1)} %get-tuple-element.58, ...), kind=kOutput, calls=%fused_computation.200 | convolution fusion | flops 2189427712 | bytes 39878656 | tf_op jit(solution)/shard_map/sub | solution.py:183
  225.1 14.6 %convert_bitcast_fusion.1 = bf16[2,1024,4,128]{1,3,2,0:T(8,128)(2,1)} fusion(f32[2,1024,3,4,128]{1,4,3,2,0:T(8,128)} %copy-done.2, f32[2,4,1024,1024]{2,3,1,0:T(8,128)} %get-tuple-element.77, f32[2,4,1024]{2,1,0:T(4,128)S(1)} %get-tuple-element.76), kind=kOutput, calls=%fused_computation.101 | convolution fusion | flops 2165309440 | bytes 37781504 | tf_op jit(solution)/shard_map/shqk,skhe->sqhe/dot_general | solution.py:186
  246.0 3.6 all-to-all-start.4
  250.8 23.1 %all-to-all-done.4 = bf16[4,2,256,512]{3,2,1,0:T(8,128)(2,1)S(1)} async-done(((bf16[4,2,256,512]{3,2,1,0:T(8,128)(2,1)}), bf16[4,2,256,512]{3,2,1,0:T(8,128)(2,1)S(1)}, u32[]{:S(2)}, u32[]{:S(2)}) %all-to-all-start.4) | async-done | bytes 2097184 | tf_op jit(solution)/shard_map/all_to_all | solution.py:52
  276.3 7.6 fusion.107
  291.1 9.5 all-gather.11.cloned.1.call-start
  301.0 33.1 %collective-permute-done = bf16[512,2048]{1,0:T(8,128)(2,1)S(1)} collective-permute-done((bf16[512,2048]{1,0:T(8,128)(2,1)}, bf16[512,2048]{1,0:T(8,128)(2,1)S(1)}, u32[]{:S(2)}, u32[]{:S(2)}) %collective-permute-start) | collective-permute-done | bytes 2097184 | tf_op jit(solution)/shard_map/ppermute | solution.py:61
  334.9 11.1 collective-permute-done.1
  349.9 18.4 %collective-permute-done.2 = bf16[256,2048]{1,0:T(8,128)(2,1)S(1)} collective-permute-done((bf16[256,2048]{1,0:T(8,128)(2,1)S(1)}, bf16[256,2048]{1,0:T(8,128)(2,1)S(1)}, u32[]{:S(2)}, u32[]{:S(2)}) %collective-permute-start.2) | collective-permute-done | bytes 1048608 | tf_op jit(solution)/shard_map/ppermute | solution.py:61
  370.5 29.9 %fusion.108 = f32[2048,2816]{1,0:T(8,128)S(1)} fusion(bf16[2048,2048]{1,0:T(8,128)(2,1)} %constant_dynamic-update-slice_fusion, bf16[2048,2816]{1,0:T(8,128)(2,1)} %all-gather.7.cloned.1.call-done), kind=kOutput, calls=%fused_computation.207 | convolution fusion | flops 23622320128 | bytes 42991616 | tf_op jit(solution)/shard_map/dot_general | solution.py:26
  400.4 7.6 copy-done.7
  408.0 5.3 multiply_convert_fusion.2
  413.3 19.4 %fusion.103 = (bf16[2048,2048]{1,0:T(8,128)(2,1)S(1)}, f32[2048,2048]{1,0:T(8,128)}) fusion(bf16[2048,1408]{1,0:T(8,128)(2,1)} %multiply_convert_fusion.2, bf16[2048,1408]{1,0:T(8,128)(2,1)} %all-gather.9.cloned.1.call-done), kind=kOutput, calls=%fused_computation.202 | convolution fusion | flops 11815354368 | bytes 36700160 | tf_op jit(solution)/shard_map/dot_general | solution.py:26
  434.9 20.1 %collective-permute-done.4 = bf16[256,2048]{1,0:T(8,128)(2,1)S(1)} collective-permute-done((bf16[256,2048]{1,0:T(8,128)(2,1)S(1)}, bf16[256,2048]{1,0:T(8,128)(2,1)S(1)}, u32[]{:S(2)}, u32[]{:S(2)}) %collective-permute-start.4) | collective-permute-done | bytes 1048608 | tf_op jit(solution)/shard_map/ppermute | solution.py:61
  464.5 39.5 %collective-permute-done.7 = bf16[512,2048]{1,0:T(8,128)(2,1)} collective-permute-done((bf16[512,2048]{1,0:T(8,128)(2,1)}, bf16[512,2048]{1,0:T(8,128)(2,1)}, u32[]{:S(2)}, u32[]{:S(2)}) %collective-permute-start.7) | collective-permute-done | bytes 2097184 | tf_op jit(solution)/shard_map/ppermute | solution.py:61
  505.2 5.9 fusion.95
  520.2 40.0 %collective-permute-done.8 = bf16[512,2048]{1,0:T(8,128)(2,1)S(1)} collective-permute-done((bf16[512,2048]{1,0:T(8,128)(2,1)S(1)}, bf16[512,2048]{1,0:T(8,128)(2,1)S(1)}, u32[]{:S(2)}, u32[]{:S(2)}) %collective-permute-start.8) | collective-permute-done | bytes 2097184 | tf_op jit(solution)/shard_map/ppermute | solution.py:61
  562.7 22.8 %collective-permute-done.10 = bf16[256,2048]{1,0:T(8,128)(2,1)S(1)} collective-permute-done((bf16[256,2048]{1,0:T(8,128)(2,1)S(1)}, bf16[256,2048]{1,0:T(8,128)(2,1)S(1)}, u32[]{:S(2)}, u32[]{:S(2)}) %collective-permute-start.10) | collective-permute-done | bytes 1048608 | tf_op jit(solution)/shard_map/ppermute | solution.py:61
  589.0 15.6 %convolution_convert_fusion.2 = bf16[2048,1408]{1,0:T(8,128)(2,1)} fusion(bf16[2048,2048]{1,0:T(8,128)(2,1)S(1)} %constant_dynamic-update-slice_fusion.5, bf16[2048,1408]{1,0:T(8,128)(2,1)S(1)} %bitcast.169), kind=kOutput, calls=%fused_computation.36 | convolution fusion | flops 11814043648 | bytes 19922944 | tf_op jit(solution)/shard_map/dot_general | solution.py:26
  604.7 31.8 %fusion.15 = (bf16[2048,1408]{1,0:T(8,128)(2,1)}, bf16[2048,1408]{1,0:T(8,128)(2,1)}) fusion(f32[2048,2816]{1,0:T(8,128)} %copy-done.7, bf16[2048,2048]{1,0:T(8,128)(2,1)} %copy-done.28, bf16[2048,1408]{1,0:T(8,128)(2,1)} %all-gather.9.cloned.1.call-done), kind=kOutput, calls=%fused_computation.24 | convolution fusion | flops 11880366080 | bytes 48758784 | tf_op jit(solution)/shard_map/dot_general | solution.py:26
  636.5 32.7 %fusion.105 = (bf16[2048,2048]{1,0:T(8,128)(2,1)}, f32[2048,2048]{1,0:T(8,128)}) fusion(bf16[2048,2816]{1,0:T(8,128)(2,1)} %all-gather.7.cloned.1.call-done, bf16[2048,1408]{1,0:T(8,128)(2,1)} %get-tuple-element.38, bf16[2048,1408]{1,0:T(8,128)(2,1)} %get-tuple-element.37), kind=kOutput, calls=%fused_computation.204 | convolution fusion | flops 23649583104 | bytes 48234496 | tf_op jit(solution)/shard_map/dot_general | solution.py:26
  672.4 19.2 %collective-permute-done.12 = bf16[256,2048]{1,0:T(8,128)(2,1)S(1)} collective-permute-done((bf16[256,2048]{1,0:T(8,128)(2,1)S(1)}, bf16[256,2048]{1,0:T(8,128)(2,1)S(1)}, u32[]{:S(2)}, u32[]{:S(2)}) %collective-permute-start.12) | collective-permute-done | bytes 1048608 | tf_op jit(solution)/shard_map/ppermute | solution.py:61
  696.6 39.3 %collective-permute-done.15 = bf16[512,2048]{1,0:T(8,128)(2,1)S(1)} collective-permute-done((bf16[512,2048]{1,0:T(8,128)(2,1)S(1)}, bf16[512,2048]{1,0:T(8,128)(2,1)S(1)}, u32[]{:S(2)}, u32[]{:S(2)}) %collective-permute-start.15) | collective-permute-done | bytes 2097184 | tf_op jit(solution)/shard_map/ppermute | solution.py:61
  736.8 4.7 multiply_reduce_fusion.2
  744.7 7.1 convolution_convert_fusion.1
  753.2 9.2 convolution_convert_fusion.3
  764.0 3.6 all-to-all-start.6
  767.6 32.0 %convolution_convert_fusion = bf16[2048,2816]{1,0:T(8,128)(2,1)} fusion(bf16[2048,2048]{1,0:T(8,128)(2,1)} %constant_dynamic-update-slice_fusion, bf16[2048,1408]{1,0:T(8,128)(2,1)} %get-tuple-element.38, bf16[2048,1408]{1,0:T(8,128)(2,1)} %get-tuple-element.37), kind=kOutput, calls=%fused_computation.28 | convolution fusion | flops 23651155968 | bytes 31457280 | tf_op jit(solution)/shard_map/dot_general | solution.py:26
  805.8 23.7 %multiply_reduce_fusion = (f32[2,4,1024]{2,1,0:T(4,128)S(1)}, f32[2,4,1024,1024]{2,3,1,0:T(8,128)}) fusion(f32[2,4,1024,1024]{2,3,1,0:T(8,128)} %get-tuple-element.77, f32[2,4,1024]{2,1,0:T(4,128)S(1)} %copy-done.30, bf16[2,1024,4,128]{1,3,2,0:T(8,128)(2,1)S(1)} %reshape.506, f32[2,1024,3,4,128]{1,4,3,2,0:T(8,128)} %copy-done.2), kind=kOutput, calls=%fused_computation.2 | convolution fusion | flops 2172641280 | bytes 71368704 | tf_op jit(solution)/shard_map/sqhe,skhe->shqk/dot_general | solution.py:251
  829.6 28.9 %multiply_convert_fusion = bf16[2,4,1024,1024]{2,3,1,0:T(8,128)(2,1)} fusion(f32[2,4,1024,1024]{2,3,1,0:T(8,128)} %get-tuple-element.88, f32[2,4,1024]{2,1,0:T(4,128)S(1)} %get-tuple-element.87, f32[2,4,1024,1024]{2,3,1,0:T(8,128)} %get-tuple-element.77, f32[2,4,1024]{2,1,0:T(4,128)S(1)} %copy-done.30), kind=kLoop, calls=%fused_computation.1 | loop fusion | flops 33554432 | bytes 83951616 | tf_op jit(solution)/shard_map/convert_element_type | solution.py:253
  858.6 10.9 multiply_bitcast_fusion.1
  869.5 13.6 %multiply_bitcast_fusion = f32[2,1024,4,128]{1,3,2,0:T(8,128)} fusion(bf16[2,4,1024,1024]{2,3,1,0:T(8,128)(2,1)} %multiply_convert_fusion, bf16[2,1024,4,64]{1,3,2,0:T(8,128)(2,1)S(1)} %copy-done.16, bf16[2,1024,4,64]{1,3,2,0:T(8,128)(2,1)S(1)} %copy-done.15), kind=kOutput, calls=%fused_computation.55 | convolution fusion | flops 2152726528 | bytes 23068672 | tf_op jit(solution)/shard_map/shqk,sqhe->skhe/dot_general | solution.py:255
  883.1 5.0 multiply_subtract_fusion.1
  890.0 15.8 %fusion.43 = bf16[2,1024,1,4,128]{1,4,3,0,2:T(8,128)(2,1)} fusion(bf16[2,1024,4,128]{1,3,2,0:T(8,128)(2,1)} %copy-done.24, f32[2,4,1024,1024]{2,3,1,0:T(8,128)} %get-tuple-element.77, f32[2,4,1024]{2,1,0:T(4,128)S(1)} %copy-done.30), kind=kOutput, calls=%fused_computation.79 | convolution fusion | flops 2164260864 | bytes 37781504 | tf_op jit(solution)/shard_map/shqk,sqhe->skhe/dot_general | solution.py:256
  905.8 5.5 maximum_convert_fusion
  911.3 10.7 copy.168
  922.0 11.2 convert_element_type.303
  933.2 5.1 subtract_convert_fusion.2
  938.3 15.5 %all-to-all-start.9 = ((f32[8,16,1536]{2,1,0:T(8,128)}), f32[8,16,1536]{2,1,0:T(8,128)}, u32[]{:S(2)}, u32[]{:S(2)}) async-start(f32[8,16,1536]{2,1,0:T(8,128)} %bitcast.42), calls=%async_computation.9 | async-start | bytes 1572864 | tf_op jit(solution)/shard_map/all_to_all | solution.py:52
  953.8 8.8 fusion.5
  967.5 13.9 %all-to-all-done.9 = f32[8,16,1536]{2,1,0:T(8,128)} async-done(((f32[8,16,1536]{2,1,0:T(8,128)}), f32[8,16,1536]{2,1,0:T(8,128)}, u32[]{:S(2)}, u32[]{:S(2)}) %all-to-all-start.9) | async-done | bytes 786464 | tf_op jit(solution)/shard_map/all_to_all | solution.py:52
  981.5 7.0 all-to-all-start.8
  989.7 24.9 %all-to-all-done.8 = f32[32,1,8448]{2,1,0:T(1,128)S(1)} async-done(((f32[32,1,8448]{2,1,0:T(1,128)}), f32[32,1,8448]{2,1,0:T(1,128)S(1)}, u32[]{:S(2)}, u32[]{:S(2)}) %all-to-all-start.8) | async-done | bytes 1081376 | tf_op jit(solution)/shard_map/all_to_all | solution.py:52
  1015.8 4.5 all-to-all-start.10
  1020.4 11.0 convert_element_type.296
  1031.4 19.3 %convert_bitcast_fusion = bf16[4,2,256,2048]{3,2,0,1:T(8,128)(2,1)} fusion(bf16[2,4,256,1536]{3,2,1,0:T(8,128)(2,1)} %convert_element_type.296, bf16[2048,1536]{1,0:T(8,128)(2,1)} %all-gather.11.cloned.1.call-done), kind=kOutput, calls=%fused_computation.30 | convolution fusion | flops 12889096192 | bytes 20971520 | tf_op jit(solution)/shard_map/dot_general | solution.py:26
  1050.6 8.4 copy.169
  1060.1 5.8 all-to-all-start.7
  1067.8 4.6 reshape.468
  1081.3 76.7 %all-to-all-done.7 = bf16[4,512,2048]{2,1,0:T(8,128)(2,1)} async-done(((bf16[4,512,2048]{2,1,0:T(8,128)(2,1)}), bf16[4,512,2048]{2,1,0:T(8,128)(2,1)}, u32[]{:S(2)}, u32[]{:S(2)}) %all-to-all-start.7) | async-done | bytes 8388640 | tf_op jit(solution)/shard_map/all_to_all | solution.py:52
  1158.0 7.6 convert_reduce_fusion
  1169.9 6.0 multiply_add_fusion
  1178.8 4.2 reshape.470
  1187.7 22.1 %reduce-scatter.7.cloned.1.call-done = bf16[64,2048]{1,0:T(8,128)(2,1)} async-done(((bf16[256,2048]{1,0:T(8,128)(2,1)}), bf16[64,2048]{1,0:T(8,128)(2,1)}) %reduce-scatter.7.cloned.1.call-update) | async-done | bytes 262160 | tf_op jit(solution)/shard_map/reduce_scatter | solution.py:241
  (306 shorter events, 150.5 us)
Async XLA Ops:
  7.2 269.2 %all-gather.5.cloned.1.call-start = ((), (), s32[]{:S(2)}) async-start(), calls=%async_computation.17 | async-start | bytes 8650752 | tf_op jit(solution)/shard_map/all_gather | solution.py:149
  7.9 362.6 %all-gather.7.cloned.1.call-start = ((), (), s32[]{:S(2)}) async-start(), calls=%async_computation.18 | async-start | bytes 12976128 | tf_op jit(solution)/shard_map/all_gather | solution.py:157
  13.3 33.1 %copy-start.27 = (bf16[64,6144]{1,0:T(8,128)(2,1)S(1)}, bf16[64,6144]{1,0:T(8,128)(2,1)}, u32[]{:S(2)}) copy-start(bf16[64,6144]{1,0:T(8,128)(2,1)} %param.21) | copy-start | bytes 2359300
  45.1 6.4 copy-start.52
  45.1 6.4 copy-start.53
  45.1 6.4 copy-start.54
  45.1 6.4 copy-start.55
  48.0 13.2 %all-to-all-start.1 = ((bf16[4,64,3,512]{3,1,2,0:T(8,128)(2,1)}), bf16[4,64,3,512]{3,1,2,0:T(8,128)(2,1)S(1)}, u32[]{:S(2)}, u32[]{:S(2)}) async-start(bf16[4,64,3,512]{3,1,2,0:T(8,128)(2,1)} %copy.147), calls=%async_computation.1 | async-start | bytes 1572864 | tf_op jit(solution)/shard_map/all_to_all | solution.py:52
  51.5 232.4 %copy-start.33 = (s32[1,2,2,128]{3,1,2,0:T(2,128)}, s32[1,2,2,128]{3,1,2,0:T(2,128)S(1)}, u32[]{:S(2)}) copy-start(s32[1,2,2,128]{3,1,2,0:T(2,128)S(1)} %copy.191) | copy-start | bytes 6148
  61.2 37.4 %all-to-all-start = ((bf16[32,2,4480]{2,1,0:T(2,128)(2,1)}), bf16[32,2,4480]{2,1,0:T(2,128)(2,1)}, u32[]{:S(2)}, u32[]{:S(2)}) async-start(bf16[32,2,4480]{2,1,0:T(2,128)(2,1)} %reshape.508), calls=%async_computation | async-start | bytes 1146880 | tf_op jit(solution)/shard_map/all_to_all | solution.py:52
  68.8 36.0 %copy-start.10 = (bf16[4,64,3,512]{3,2,1,0:T(4,128)(2,1)}, bf16[4,64,3,512]{3,2,1,0:T(4,128)(2,1)S(1)}, u32[]{:S(2)}) copy-start(bf16[4,64,3,512]{3,2,1,0:T(4,128)(2,1)S(1)} %copy.148) | copy-start | bytes 2359300
  102.3 8.0 copy-start.50
  103.6 409.9 %copy-start.14 = (bf16[128,2048]{1,0:T(8,128)(2,1)}, bf16[128,2048]{1,0:T(8,128)(2,1)S(1)}, u32[]{:S(2)}) copy-start(bf16[128,2048]{1,0:T(8,128)(2,1)S(1)} %reshape.448) | copy-start | bytes 1572868
  104.8 41.0 %all-to-all-start.2 = ((f32[8,16,1536]{2,1,0:T(8,128)}), f32[8,16,1536]{2,1,0:T(8,128)S(1)}, u32[]{:S(2)}, u32[]{:S(2)}) async-start(f32[8,16,1536]{2,1,0:T(8,128)} %fusion.106), calls=%async_computation.2 | async-start | bytes 1572864 | tf_op jit(solution)/shard_map/all_to_all | solution.py:52
  146.9 47.5 %all-to-all-start.3 = ((bf16[8,2,16,1536]{3,2,1,0:T(8,128)(2,1)}), bf16[8,2,16,1536]{3,2,1,0:T(8,128)(2,1)S(1)}, u32[]{:S(2)}, u32[]{:S(2)}) async-start(bf16[8,2,16,1536]{3,2,1,0:T(8,128)(2,1)} %broadcast_in_dim.35), calls=%async_computation.3 | async-start | bytes 1572864 | tf_op jit(solution)/shard_map/all_to_all | solution.py:52
  246.0 27.9 %all-to-all-start.4 = ((bf16[4,2,256,512]{3,2,1,0:T(8,128)(2,1)}), bf16[4,2,256,512]{3,2,1,0:T(8,128)(2,1)S(1)}, u32[]{:S(2)}, u32[]{:S(2)}) async-start(bf16[4,2,256,512]{3,2,1,0:T(8,128)(2,1)} %bitcast.167), calls=%async_computation.4 | async-start | bytes 4194304 | tf_op jit(solution)/shard_map/all_to_all | solution.py:52
  249.6 163.7 %all-gather.9.cloned.1.call-start = ((), (), s32[]{:S(2)}) async-start(), calls=%async_computation.19 | async-start | bytes 6488064 | tf_op jit(solution)/shard_map/all_gather | solution.py:158
  288.1 46.0 %collective-permute-start = (bf16[512,2048]{1,0:T(8,128)(2,1)}, bf16[512,2048]{1,0:T(8,128)(2,1)S(1)}, u32[]{:S(2)}, u32[]{:S(2)}) collective-permute-start(bf16[512,2048]{1,0:T(8,128)(2,1)} %get-tuple-element.34), channel_id=1, source_target_pairs={{0,1},{1,0},{2,3},{3,2},{4,5},{5,4},{6,7},{7,6},{8,9},{9,8},{10,11... | collective-permute-start | bytes 6291464 | tf_op jit(solution)/shard_map/ppermute | solution.py:61
  291.1 662.7 %all-gather.11.cloned.1.call-start = ((), (), s32[]{:S(2)}) async-start(), calls=%async_computation.20 | async-start | bytes 7077888 | tf_op jit(solution)/shard_map/all_gather | solution.py:159
  300.5 45.5 %collective-permute-start.1 = (bf16[512,2048]{1,0:T(8,128)(2,1)}, bf16[512,2048]{1,0:T(8,128)(2,1)S(1)}, u32[]{:S(2)}, u32[]{:S(2)}) collective-permute-start(bf16[512,2048]{1,0:T(8,128)(2,1)} %get-tuple-element.34), channel_id=1, source_target_pairs={{0,2},{1,3},{2,0},{3,1},{4,6},{5,7},{6,4},{7,5},{8,10},{9,11},{10,... | collective-permute-start | bytes 6291464 | tf_op jit(solution)/shard_map/ppermute | solution.py:61
  334.2 34.2 %collective-permute-start.2 = (bf16[256,2048]{1,0:T(8,128)(2,1)S(1)}, bf16[256,2048]{1,0:T(8,128)(2,1)S(1)}, u32[]{:S(2)}, u32[]{:S(2)}) collective-permute-start(bf16[256,2048]{1,0:T(8,128)(2,1)S(1)} %slice.222), channel_id=1, source_target_pairs={{0,2},{1,3},{2,0},{3,1},{4,6},{5,7},{6,4},{7,5},{8,10},{9,11},{10,... | collective-permute-start | bytes 3145736 | tf_op jit(solution)/shard_map/ppermute | solution.py:61
  346.1 23.3 %collective-permute-start.3 = (bf16[256,2048]{1,0:T(8,128)(2,1)S(1)}, bf16[256,2048]{1,0:T(8,128)(2,1)S(1)}, u32[]{:S(2)}, u32[]{:S(2)}) collective-permute-start(bf16[256,2048]{1,0:T(8,128)(2,1)S(1)} %slice.223), channel_id=1, source_target_pairs={{0,1},{1,0},{2,3},{3,2},{4,5},{5,4},{6,7},{7,6},{8,9},{9,8},{10,11... | collective-permute-start | bytes 3145736 | tf_op jit(solution)/shard_map/ppermute | solution.py:61
  400.3 7.6 copy-start.7
  433.2 21.7 %collective-permute-start.4 = (bf16[256,2048]{1,0:T(8,128)(2,1)S(1)}, bf16[256,2048]{1,0:T(8,128)(2,1)S(1)}, u32[]{:S(2)}, u32[]{:S(2)}) collective-permute-start(bf16[256,2048]{1,0:T(8,128)(2,1)S(1)} %get-tuple-element.49), channel_id=1, source_target_pairs={{0,1},{1,0},{2,3},{3,2},{4,5},{5,4},{6,7},{7,6},{8,9},{9,8},{10,11... | collective-permute-start | bytes 3145736 | tf_op jit(solution)/shard_map/ppermute | solution.py:61
  434.1 21.7 %collective-permute-start.6 = (bf16[256,2048]{1,0:T(8,128)(2,1)S(1)}, bf16[256,2048]{1,0:T(8,128)(2,1)S(1)}, u32[]{:S(2)}, u32[]{:S(2)}) collective-permute-start(bf16[256,2048]{1,0:T(8,128)(2,1)S(1)} %get-tuple-element.50), channel_id=1, source_target_pairs={{0,2},{1,3},{2,0},{3,1},{4,6},{5,7},{6,4},{7,5},{8,10},{9,11},{10,... | collective-permute-start | bytes 3145736 | tf_op jit(solution)/shard_map/ppermute | solution.py:61
  460.4 43.5 %collective-permute-start.7 = (bf16[512,2048]{1,0:T(8,128)(2,1)}, bf16[512,2048]{1,0:T(8,128)(2,1)}, u32[]{:S(2)}, u32[]{:S(2)}) collective-permute-start(bf16[512,2048]{1,0:T(8,128)(2,1)} %pad_maximum_fusion.7), channel_id=1, source_target_pairs={{0,1},{1,0},{2,3},{3,2},{4,5},{5,4},{6,7},{7,6},{8,9},{9,8},{10,11... | collective-permute-start | bytes 6291464 | tf_op jit(solution)/shard_map/ppermute | solution.py:61
  462.2 43.0 %collective-permute-start.5 = (bf16[512,2048]{1,0:T(8,128)(2,1)}, bf16[512,2048]{1,0:T(8,128)(2,1)}, u32[]{:S(2)}, u32[]{:S(2)}) collective-permute-start(bf16[512,2048]{1,0:T(8,128)(2,1)} %pad_maximum_fusion.6), channel_id=1, source_target_pairs={{0,2},{1,3},{2,0},{3,1},{4,6},{5,7},{6,4},{7,5},{8,10},{9,11},{10,... | collective-permute-start | bytes 6291464 | tf_op jit(solution)/shard_map/ppermute | solution.py:61
  464.2 701.5 %reduce-scatter.11.cloned.1.call-start = ((), (), s32[]{:S(2)}) async-start(), calls=%async_computation.24 | async-start | bytes 6488064 | tf_op jit(solution)/shard_map/reduce_scatter | solution.py:230
  464.3 49.2 %copy-start.44 = (s32[1,2,2,128]{3,1,2,0:T(2,128)}, s32[1,2,2,128]{3,1,2,0:T(2,128)S(1)}, u32[]{:S(2)}) copy-start(s32[1,2,2,128]{3,1,2,0:T(2,128)S(1)} %copy.195) | copy-start | bytes 6148
  464.3 49.2 %copy-start.46 = (f32[1,2,2,128]{3,1,2,0:T(2,128)}, f32[1,2,2,128]{3,1,2,0:T(2,128)S(1)}, u32[]{:S(2)}) copy-start(f32[1,2,2,128]{3,1,2,0:T(2,128)S(1)} %copy.194) | copy-start | bytes 6148
  518.4 41.7 %collective-permute-start.8 = (bf16[512,2048]{1,0:T(8,128)(2,1)S(1)}, bf16[512,2048]{1,0:T(8,128)(2,1)S(1)}, u32[]{:S(2)}, u32[]{:S(2)}) collective-permute-start(bf16[512,2048]{1,0:T(8,128)(2,1)S(1)} %get-tuple-element.28), channel_id=1, source_target_pairs={{0,1},{1,0},{2,3},{3,2},{4,5},{5,4},{6,7},{7,6},{8,9},{9,8},{10,11... | collective-permute-start | bytes 6291464 | tf_op jit(solution)/shard_map/ppermute | solution.py:61
  519.9 41.7 %collective-permute-start.9 = (bf16[512,2048]{1,0:T(8,128)(2,1)S(1)}, bf16[512,2048]{1,0:T(8,128)(2,1)S(1)}, u32[]{:S(2)}, u32[]{:S(2)}) collective-permute-start(bf16[512,2048]{1,0:T(8,128)(2,1)S(1)} %get-tuple-element.28), channel_id=1, source_target_pairs={{0,2},{1,3},{2,0},{3,1},{4,6},{5,7},{6,4},{7,5},{8,10},{9,11},{10,... | collective-permute-start | bytes 6291464 | tf_op jit(solution)/shard_map/ppermute | solution.py:61
  560.2 25.3 %collective-permute-start.10 = (bf16[256,2048]{1,0:T(8,128)(2,1)S(1)}, bf16[256,2048]{1,0:T(8,128)(2,1)S(1)}, u32[]{:S(2)}, u32[]{:S(2)}) collective-permute-start(bf16[256,2048]{1,0:T(8,128)(2,1)S(1)} %slice.236), channel_id=1, source_target_pairs={{0,2},{1,3},{2,0},{3,1},{4,6},{5,7},{6,4},{7,5},{8,10},{9,11},{10,... | collective-permute-start | bytes 3145736 | tf_op jit(solution)/shard_map/ppermute | solution.py:61
  561.7 23.9 %collective-permute-start.11 = (bf16[256,2048]{1,0:T(8,128)(2,1)S(1)}, bf16[256,2048]{1,0:T(8,128)(2,1)S(1)}, u32[]{:S(2)}, u32[]{:S(2)}) collective-permute-start(bf16[256,2048]{1,0:T(8,128)(2,1)S(1)} %slice.237), channel_id=1, source_target_pairs={{0,1},{1,0},{2,3},{3,2},{4,5},{5,4},{6,7},{7,6},{8,9},{9,8},{10,11... | collective-permute-start | bytes 3145736 | tf_op jit(solution)/shard_map/ppermute | solution.py:61
  562.2 26.8 %slice-start = ((s8[5767168]{0:T(1024)(128)(4,1)}), s8[4194304]{0:T(1024)(128)(4,1)S(1)}, s32[]{:S(2)}) async-start(s8[5767168]{0:T(1024)(128)(4,1)} %bitcast.168), calls=%async_computation.25 | async-start | bytes 8388608
  562.5 26.5 %slice-start.1 = ((s8[5767168]{0:T(1024)(128)(4,1)}), s8[1572864]{0:T(1024)(128)(4,1)S(1)}, s32[]{:S(2)}) async-start(s8[5767168]{0:T(1024)(128)(4,1)} %bitcast.168), calls=%async_computation.26 | async-start | bytes 3145728
  604.7 564.5 %reduce-scatter.5.cloned.1.call-start = ((), (), s32[]{:S(2)}) async-start(), calls=%async_computation.21 | async-start | bytes 9437184 | tf_op jit(solution)/shard_map/reduce_scatter | solution.py:242
  672.0 19.6 %collective-permute-start.12 = (bf16[256,2048]{1,0:T(8,128)(2,1)S(1)}, bf16[256,2048]{1,0:T(8,128)(2,1)S(1)}, u32[]{:S(2)}, u32[]{:S(2)}) collective-permute-start(bf16[256,2048]{1,0:T(8,128)(2,1)S(1)} %get-tuple-element.45), channel_id=1, source_target_pairs={{0,1},{1,0},{2,3},{3,2},{4,5},{5,4},{6,7},{7,6},{8,9},{9,8},{10,11... | collective-permute-start | bytes 3145736 | tf_op jit(solution)/shard_map/ppermute | solution.py:61
  672.1 19.5 %collective-permute-start.14 = (bf16[256,2048]{1,0:T(8,128)(2,1)S(1)}, bf16[256,2048]{1,0:T(8,128)(2,1)S(1)}, u32[]{:S(2)}, u32[]{:S(2)}) collective-permute-start(bf16[256,2048]{1,0:T(8,128)(2,1)S(1)} %get-tuple-element.46), channel_id=1, source_target_pairs={{0,2},{1,3},{2,0},{3,1},{4,6},{5,7},{6,4},{7,5},{8,10},{9,11},{10,... | collective-permute-start | bytes 3145736 | tf_op jit(solution)/shard_map/ppermute | solution.py:61
  694.5 42.3 %copy-start.1 = (f32[512,2048]{1,0:T(8,128)S(1)}, f32[512,2048]{1,0:T(8,128)}, u32[]{:S(2)}) copy-start(f32[512,2048]{1,0:T(8,128)} %copy-done) | copy-start | bytes 12582916
  694.5 42.3 %copy-start.4 = (f32[512,2048]{1,0:T(8,128)S(1)}, f32[512,2048]{1,0:T(8,128)}, u32[]{:S(2)}) copy-start(f32[512,2048]{1,0:T(8,128)} %copy-done.3) | copy-start | bytes 12582916
  694.8 41.1 %collective-permute-start.15 = (bf16[512,2048]{1,0:T(8,128)(2,1)S(1)}, bf16[512,2048]{1,0:T(8,128)(2,1)S(1)}, u32[]{:S(2)}, u32[]{:S(2)}) collective-permute-start(bf16[512,2048]{1,0:T(8,128)(2,1)S(1)} %pad_maximum_fusion.9), channel_id=1, source_target_pairs={{0,1},{1,0},{2,3},{3,2},{4,5},{5,4},{6,7},{7,6},{8,9},{9,8},{10,11... | collective-permute-start | bytes 6291464 | tf_op jit(solution)/shard_map/ppermute | solution.py:61
  696.2 45.2 %copy-start.36 = (f32[512]{0:T(512)S(1)}, f32[512]{0:T(512)}, u32[]{:S(2)}) copy-start(f32[512]{0:T(512)} %copy-done.35) | copy-start | bytes 6148
  696.2 40.5 %collective-permute-start.13 = (bf16[512,2048]{1,0:T(8,128)(2,1)S(1)}, bf16[512,2048]{1,0:T(8,128)(2,1)S(1)}, u32[]{:S(2)}, u32[]{:S(2)}) collective-permute-start(bf16[512,2048]{1,0:T(8,128)(2,1)S(1)} %pad_maximum_fusion.8), channel_id=1, source_target_pairs={{0,2},{1,3},{2,0},{3,1},{4,6},{5,7},{6,4},{7,5},{8,10},{9,11},{10,... | collective-permute-start | bytes 6291464 | tf_op jit(solution)/shard_map/ppermute | solution.py:61
  742.7 10.5 copy-start.39
  764.0 36.0 %all-to-all-start.6 = ((bf16[4,512,512]{2,1,0:T(8,128)(2,1)}), bf16[4,512,512]{2,1,0:T(8,128)(2,1)S(1)}, u32[]{:S(2)}, u32[]{:S(2)}) async-start(bf16[4,512,512]{2,1,0:T(8,128)(2,1)} %bitcast.165), calls=%async_computation.6 | async-start | bytes 4194304 | tf_op jit(solution)/shard_map/all_to_all | solution.py:52
  767.6 411.2 %reduce-scatter.9.cloned.1.call-start = ((), (), s32[]{:S(2)}) async-start(), calls=%async_computation.23 | async-start | bytes 12976128 | tf_op jit(solution)/shard_map/reduce_scatter | solution.py:230
  805.8 23.8 %copy-start.24 = (bf16[2,1024,4,128]{1,3,2,0:T(8,128)(2,1)}, bf16[2,1024,4,128]{1,3,2,0:T(8,128)(2,1)S(1)}, u32[]{:S(2)}) copy-start(bf16[2,1024,4,128]{1,3,2,0:T(8,128)(2,1)S(1)} %reshape.506) | copy-start | bytes 6291460
  829.6 29.0 %copy-start.17 = (bf16[2,1024,4,64]{1,3,2,0:T(8,128)(2,1)S(1)}, bf16[2,1024,4,64]{1,3,2,0:T(8,128)(2,1)}, u32[]{:S(2)}) copy-start(bf16[2,1024,4,64]{1,3,2,0:T(8,128)(2,1)} %get-tuple-element.65) | copy-start | bytes 3145732
  858.6 10.9 copy-start.15
  858.6 10.9 copy-start.16
  869.5 13.6 %copy-start.21 = (f32[1024,64]{0,1:T(8,128)S(1)}, f32[1024,64]{0,1:T(8,128)}, u32[]{:S(2)}) copy-start(f32[1024,64]{0,1:T(8,128)} %get-tuple-element.73) | copy-start | bytes 786436
  869.5 13.6 %copy-start.25 = (f32[1024,64]{0,1:T(8,128)S(1)}, f32[1024,64]{0,1:T(8,128)}, u32[]{:S(2)}) copy-start(f32[1024,64]{0,1:T(8,128)} %get-tuple-element.71) | copy-start | bytes 786436
  922.0 11.2 copy-start.31
  938.3 43.1 %all-to-all-start.9 = ((f32[8,16,1536]{2,1,0:T(8,128)}), f32[8,16,1536]{2,1,0:T(8,128)}, u32[]{:S(2)}, u32[]{:S(2)}) async-start(f32[8,16,1536]{2,1,0:T(8,128)} %bitcast.42), calls=%async_computation.9 | async-start | bytes 1572864 | tf_op jit(solution)/shard_map/all_to_all | solution.py:52
  953.8 8.9 copy-start.6
  953.8 8.9 copy-start.34
  953.8 8.9 copy-start.40
  981.5 33.0 %all-to-all-start.8 = ((f32[32,1,8448]{2,1,0:T(1,128)}), f32[32,1,8448]{2,1,0:T(1,128)S(1)}, u32[]{:S(2)}, u32[]{:S(2)}) async-start(f32[32,1,8448]{2,1,0:T(1,128)} %all_to_all.54), calls=%async_computation.8 | async-start | bytes 2162688 | tf_op jit(solution)/shard_map/all_to_all | solution.py:52
  1015.8 43.2 %all-to-all-start.10 = ((bf16[32,16,1536]{2,1,0:T(8,128)(2,1)}), bf16[32,16,1536]{2,1,0:T(8,128)(2,1)S(1)}, u32[]{:S(2)}, u32[]{:S(2)}) async-start(bf16[32,16,1536]{2,1,0:T(8,128)(2,1)} %broadcast_in_dim.48), calls=%async_computation.10 | async-start | bytes 3145728 | tf_op jit(solution)/shard_map/all_to_all | solution.py:52
  1060.1 97.9 %all-to-all-start.7 = ((bf16[4,512,2048]{2,1,0:T(8,128)(2,1)}), bf16[4,512,2048]{2,1,0:T(8,128)(2,1)}, u32[]{:S(2)}, u32[]{:S(2)}) async-start(bf16[4,512,2048]{2,1,0:T(8,128)(2,1)} %bitcast.158), calls=%async_computation.7 | async-start | bytes 16777216 | tf_op jit(solution)/shard_map/all_to_all | solution.py:52
  1165.6 13.0 %all-to-all-start.12 = ((bf16[4,64,1,1408]{3,1,2,0:T(8,128)(2,1)}), bf16[4,64,1,1408]{3,1,2,0:T(8,128)(2,1)S(1)}, u32[]{:S(2)}, u32[]{:S(2)}) async-start(bf16[4,64,1,1408]{3,1,2,0:T(8,128)(2,1)} %bitcast.187), calls=%async_computation.16 | async-start | bytes 1441792 | tf_op jit(solution)/shard_map/all_to_all | solution.py:52
  1169.1 40.6 %reduce-scatter.7.cloned.1.call-start = ((), (), s32[]{:S(2)}) async-start(), calls=%async_computation.22 | async-start | bytes 1310720 | tf_op jit(solution)/shard_map/reduce_scatter | solution.py:241
  1182.9 28.6 %all-to-all-start.11 = ((bf16[4,64,2,1408]{3,2,1,0:T(2,128)(2,1)}), bf16[4,64,2,1408]{3,2,1,0:T(2,128)(2,1)S(1)}, u32[]{:S(2)}, u32[]{:S(2)}) async-start(bf16[4,64,2,1408]{3,2,1,0:T(2,128)(2,1)} %reshape.470), calls=%async_computation.14 | async-start | bytes 2883584 | tf_op jit(solution)/shard_map/all_to_all | solution.py:52
  (32 other events, 95.9 us)
Sparse Core Ops, SparseCore 0:
  10.9 89.4 all-gather.4
  102.6 134.4 all-gather.6
  291.2 61.8 all-gather.8
  464.3 69.1 all-gather.10
  604.8 70.0 reduce-scatter.10
  751.9 97.3 reduce-scatter.4
  851.6 134.8 reduce-scatter.8
  1172.9 36.8 reduce-scatter.6

commit v2 on v1

v2 whole, which is shorter than its diff:
```python
import math

import jax
import jax.numpy as jnp
from jax import lax
from jax.experimental import pallas as pl
from jax.experimental.pallas import tpu as pltpu
from jax.sharding import PartitionSpec as P

HEADS = 16
HEAD = 128
LANES = 128

deep_alpha = math.sqrt(48.0)
loss_scale = 1024.0
norm_epsilon = 1e-05
lookup_scale = 0.1
score_scale = 1.0 / math.sqrt(HEAD)
LOG2_E = math.log2(math.e)

bf16 = jnp.bfloat16
f32 = jnp.float32
BOTH = ("dp", "seq")
ROWS = (((0,), (0,)), ((), ()))
LAST = (((1,), (1,)), ((), ()))


def dot(left, right, dims=(((1,), (0,)), ((), ()))):
    return lax.dot_general(left, right, dims, preferred_element_type=f32)


def layer_norm(inputs_row, gain_row, bias_row):
    centred = inputs_row - jnp.mean(inputs_row, axis=-1, keepdims=True)
    spread_sq = jnp.mean(centred * centred, axis=-1, keepdims=True)
    return centred * lax.rsqrt(spread_sq + norm_epsilon) * gain_row + bias_row


def rotary_angles(positions, head_size):
    halves = head_size // 2
    freqs = jnp.power(10000.0, -2.0 * jnp.arange(halves, dtype=f32) / head_size)
    return positions.astype(f32)[:, None] * freqs[None, :]


def rotate(field, cosine, sine):
    halves = field.shape[-1] // 2
    first, second = field[..., :halves], field[..., halves:]
    return jnp.concatenate([first * cosine - second * sine, second * cosine + first * sine], axis=-1)


def gated_gelu(gate, up):
    root = math.sqrt(2.0 / math.pi)
    square = gate * gate
    bend = jnp.tanh(gate * (root + (root * 0.044715) * square))
    half = 0.5 + 0.5 * bend
    gelu = gate * half
    slope = half + gate * (0.5 - 0.5 * bend * bend) * (root + (3.0 * root * 0.044715) * square)
    return gelu * up, slope * up, gelu


def halves(value):
    high = lax.reduce_precision(value, 8, 7)
    return jnp.stack([high.astype(bf16), (value - high).astype(bf16)])


def together(*values):
    return lax.optimization_barrier(values)


def exchange(blocks, axes):
    return lax.all_to_all(blocks, axes, split_axis=0, concat_axis=0, tiled=True)


def spread(block, axes):
    count = lax.axis_size(axes)
    return exchange(jnp.broadcast_to(block[None], (count,) + block.shape), axes)


def swap(block, bits):
    return lax.ppermute(block, "seq", [(s, s ^ bits) for s in range(lax.axis_size("seq"))])


def swap_dp(block, bits):
    return lax.ppermute(block, "dp", [(d, d ^ bits) for d in range(lax.axis_size("dp"))])


def place(axis):
    return lax.axis_index(axis).astype(jnp.int32).reshape(1)


def take_columns(weight, groups, pieces, size):
    rows, columns = weight.shape

    def kernel(place_ref, weight_ref, out_ref):
        for g in range(groups):
            for i in range(pieces):
                first = (i * groups + g) * size
                block = weight_ref[:, first : min(first + size, columns)]
                if block.shape[1] < size:
                    rest = jnp.zeros((rows, size - block.shape[1]), block.dtype)
                    block = jnp.concatenate([block, rest], axis=1)
                out_ref[lax.bitwise_xor(place_ref[0], g), :, i * size : (i + 1) * size] = block

    return pl.pallas_call(
        kernel,
        in_specs=[pl.BlockSpec(memory_space=pltpu.SMEM), pl.BlockSpec(memory_space=pltpu.VMEM)],
        out_specs=pl.BlockSpec(memory_space=pltpu.VMEM),
        out_shape=jax.ShapeDtypeStruct((groups, rows, pieces * size), weight.dtype),
        compiler_params=pltpu.CompilerParams(vmem_limit_bytes=16 << 20),
    )(place("seq"), weight)


def swap_all(blocks):
    return [blocks[0]] + [swap(blocks[k], k) for k in range(1, blocks.shape[0])]


def join_rows(blocks):
    rows, columns = blocks[0].shape
    groups = len(blocks)

    def kernel(place_ref, *refs):
        for k in range(groups):
            first = pl.multiple_of(lax.bitwise_xor(place_ref[0], k) * rows, rows)
            refs[-1][pl.ds(first, rows), :] = refs[k][...]

    return pl.pallas_call(
        kernel,
        in_specs=[pl.BlockSpec(memory_space=pltpu.SMEM)] + [pl.BlockSpec(memory_space=pltpu.VMEM)] * groups,
        out_specs=pl.BlockSpec(memory_space=pltpu.VMEM),
        out_shape=jax.ShapeDtypeStruct((groups * rows, columns), blocks[0].dtype),
        compiler_params=pltpu.CompilerParams(vmem_limit_bytes=16 << 20),
    )(place("seq"), *blocks)


def take_rows(field, groups):
    rows, columns = field.shape[0] // groups, field.shape[1]

    def kernel(place_ref, field_ref, out_ref):
        for g in range(groups):
            out_ref[lax.bitwise_xor(place_ref[0], g)] = field_ref[g * rows : (g + 1) * rows]

    return pl.pallas_call(
        kernel,
        in_specs=[pl.BlockSpec(memory_space=pltpu.SMEM), pl.BlockSpec(memory_space=pltpu.VMEM)],
        out_specs=pl.BlockSpec(memory_space=pltpu.VMEM),
        out_shape=jax.ShapeDtypeStruct((groups, rows, columns), field.dtype),
        compiler_params=pltpu.CompilerParams(vmem_limit_bytes=16 << 20),
    )(place("seq"), field)


def join_columns(blocks, columns):
    rows, size = blocks[0].shape
    groups = len(blocks)

    def kernel(place_ref, *refs):
        for g in range(groups):
            source = lax.bitwise_xor(place_ref[0], g)
            block = refs[0][...]
            for k in range(1, groups):
                block = jnp.where(source == k, refs[k][...], block)
            end = min((g + 1) * size, columns)
            refs[-1][:, g * size : end] = block[:, : end - g * size].astype(f32)

    return pl.pallas_call(
        kernel,
        in_specs=[pl.BlockSpec(memory_space=pltpu.SMEM)] + [pl.BlockSpec(memory_space=pltpu.VMEM)] * groups,
        out_specs=pl.BlockSpec(memory_space=pltpu.VMEM),
        out_shape=jax.ShapeDtypeStruct((rows, columns), f32),
        compiler_params=pltpu.CompilerParams(vmem_limit_bytes=16 << 20),
    )(place("seq"), *blocks)


def table_grad(sums, embed_rows):
    dps, groups, piece, columns = sums.shape
    size = columns // 3
    rows = embed_rows.shape[1]

    def kernel(sums_ref, embed_ref, out_ref):
        embed = embed_ref[...]
        for i in range(3):
            for g in range(groups):
                block = sums_ref[:, g, :, i * size : (i + 1) * size].reshape(dps * piece, size)
                first = (i * groups + g) * size
                out_ref[:, first : first + size] = dot(embed, block, ROWS)

    return pl.pallas_call(
        kernel,
        in_specs=[pl.BlockSpec(memory_space=pltpu.VMEM)] * 2,
        out_specs=pl.BlockSpec(memory_space=pltpu.VMEM),
        out_shape=jax.ShapeDtypeStruct((rows, 3 * groups * size), f32),
        compiler_params=pltpu.CompilerParams(vmem_limit_bytes=24 << 20),
    )(sums, embed_rows)


def join_out(mine, other):
    groups, chips, rows, width = mine.shape

    def kernel(seq_ref, dp_ref, mine_ref, other_ref, out_ref):
        chip = dp_ref[0] // 2
        for source, ref in enumerate((mine_ref, other_ref)):

            @pl.when(pl.program_id(0) == source)
            def _(ref=ref):
                for j in range(chips):
                    out_ref[lax.bitwise_xor(chip, j), 0, 0] = ref[0, j]

    last = groups - 1
    return pl.pallas_call(
        kernel,
        grid_spec=pltpu.PrefetchScalarGridSpec(
            num_scalar_prefetch=2,
            grid=(2, groups),
            in_specs=[
                pl.BlockSpec((1, chips, rows, width), lambda a, k, at, dp: (jnp.where(a == 0, k, last), 0, 0, 0)),
                pl.BlockSpec((1, chips, rows, width), lambda a, k, at, dp: (jnp.where(a == 0, 0, k), 0, 0, 0)),
            ],
            out_specs=pl.BlockSpec(
                (chips, 1, 1, rows, width),
                lambda a, k, at, dp: (
                    0,
                    lax.bitwise_xor(lax.rem(dp[0], 2), a),
                    lax.bitwise_xor(at[0], k),
                    0,
                    0,
                ),
            ),
        ),
        out_shape=jax.ShapeDtypeStruct((chips, 2, groups, rows, width), mine.dtype),
        compiler_params=pltpu.CompilerParams(vmem_limit_bytes=24 << 20),
    )(place("seq"), place("dp"), mine, other).reshape(chips * 2 * groups * rows, width)


def sum_dp(parts):
    kept = parts[0] + swap_dp(parts[1], 1)
    return kept[0] + sum(swap_dp(kept[j], 2 * j) for j in range(1, kept.shape[0]))


def spread_dp(block):
    blocks = jnp.stack([block] + [swap_dp(block, 2 * j) for j in range(1, lax.axis_size("dp") // 2)])
    return jnp.stack([blocks, swap_dp(blocks, 1)]), blocks


def gather_tokens(block, work):
    if lax.axis_size("seq") != 4:
        blocks = [block] + [swap(block, k) for k in range(1, lax.axis_size("seq"))]
        return blocks, [work(k, b) for k, b in enumerate(blocks)]
    half = block.shape[0] // 2
    near = swap(block, 1)
    over = swap(block, 2)
    own_work = work(0, block)
    near, over, own_work = together(near, over, own_work)
    far_one = swap(near[:half], 2)
    far_two = swap(over[half:], 1)
    near_work, over_work = work(1, near), work(2, over)
    far_one, far_two, near_work, over_work = together(far_one, far_two, near_work, over_work)
    far = jnp.concatenate([far_one, far_two], axis=0)
    return [block, near, over, far], [own_work, near_work, over_work, work(3, far)]


def gather_blocks(block, held):
    if lax.axis_size("seq") != 4:
        return jnp.stack([block] + [swap(block, k) for k in range(1, lax.axis_size("seq"))])
    half = block.shape[0] // 2
    near, over = swap(block, 1), swap(block, 2)
    near_held, over_held, _ = together(near, over, held)
    far = jnp.concatenate([swap(near_held[:half], 2), swap(over_held[half:], 1)], axis=0)
    return jnp.stack([block, near, over, far])


def scatter_tokens(part, first=None, last=None, first_given=(), last_given=()):
    if lax.axis_size("seq") != 4:
        total = part(0).astype(f32)
        for k in range(1, lax.axis_size("seq")):
            total = total + swap(part(k).astype(bf16), k).astype(f32)
        return total, first and first(*first_given), last and last(*last_given)
    far = part(3).astype(bf16)
    half = far.shape[0] // 2
    far, *first_given = together(far, *first_given)
    by_near = swap(far[:half], 1)
    by_over = swap(far[half:], 2)
    first_done = first(*first_given) if first else ()
    by_near, by_over, near, over, own, first_done = together(
        by_near, by_over, part(1), part(2), part(0), first_done
    )
    near_sent = jnp.concatenate([near[:half], near[half:].astype(f32) + by_over.astype(f32)], axis=0)
    over_sent = jnp.concatenate([over[:half].astype(f32) + by_near.astype(f32), over[half:]], axis=0)
    near_sent, over_sent, *last_given = together(near_sent.astype(bf16), over_sent.astype(bf16), *last_given)
    from_near = swap(near_sent, 1)
    from_over = swap(over_sent, 2)
    last_done = last(*last_given) if last else ()
    from_over, from_near, last_done = together(from_over, from_near, last_done)
    return own.astype(f32) + from_over.astype(f32) + from_near.astype(f32), first_done, last_done


def head_fields(hot_ref, table_ref, cos_ref, sin_ref):
    length = cos_ref.shape[0]
    hot = hot_ref[...].reshape(length, hot_ref.shape[-1])
    field = dot(jnp.concatenate([hot, hot], axis=1), table_ref[...].reshape(table_ref.shape[0], 3 * HEAD))
    cosine, sine = cos_ref[...], sin_ref[...]
    queries, keys, values = field[:, :HEAD], field[:, HEAD : 2 * HEAD], field[:, 2 * HEAD :]
    queries = queries * cosine + pltpu.roll(queries, HEAD // 2, 1) * sine
    keys = keys * cosine + pltpu.roll(keys, HEAD // 2, 1) * sine
    return queries.astype(bf16), keys.astype(bf16), values.astype(bf16)


def softmax_columns(keys, block, first, prefix):
    raw = dot(keys, block, LAST)
    key_pos = lax.broadcasted_iota(jnp.int32, raw.shape, 0)
    query_pos = lax.broadcasted_iota(jnp.int32, (1, raw.shape[1]), 1) + first
    raw = jnp.where(key_pos < jnp.maximum(prefix, query_pos + 1), raw, -1e30)
    top = jnp.max(raw, axis=0, keepdims=True)
    expo = jnp.exp2((raw - top) * (score_scale * LOG2_E))
    return expo, jnp.sum(expo, axis=0, keepdims=True)


def attend_kernel(prefix_ref, hot_ref, table_ref, cos_ref, sin_ref, out_ref, query_ref):
    prefix = prefix_ref[pl.program_id(0)]
    queries, keys, values = head_fields(hot_ref, table_ref, cos_ref, sin_ref)
    query_ref[...] = queries
    blocks, _, size, _ = out_ref.shape
    for b in range(blocks):
        raw = dot(query_ref[b * size : (b + 1) * size], keys, LAST)
        key_pos = lax.broadcasted_iota(jnp.int32, (1, raw.shape[1]), 1)
        query_pos = lax.broadcasted_iota(jnp.int32, (size, 1), 0) + b * size
        raw = jnp.where(key_pos < jnp.maximum(prefix, query_pos + 1), raw, -1e30)
        top = jnp.max(raw, axis=1, keepdims=True)
        expo = jnp.exp2((raw - top) * (score_scale * LOG2_E))
        total = jnp.sum(expo, axis=1, keepdims=True)
        out_ref[b, 0] = (dot(expo.astype(bf16), values) * (1.0 / total)).astype(bf16)


def attend_back_kernel(place_ref, prefix_ref, hot_ref, table_ref, cos_ref, sin_ref, grad_ref, out_ref, query_ref, key_sum, value_sum):
    prefix = prefix_ref[pl.program_id(0)]
    head = pl.program_id(1)
    queries, keys, values = head_fields(hot_ref, table_ref, cos_ref, sin_ref)
    query_ref[...] = queries
    keys_t = keys.T
    blocks, _, size, _ = grad_ref.shape
    width = out_ref.shape[-1] // 3

    def store(b, part, block):
        column = pl.multiple_of(part * width + head * HEAD, HEAD)
        out_ref[lax.bitwise_xor(place_ref[0], b), 0, :, pl.ds(column, HEAD)] = block.astype(bf16)

    def unrotated(block, b):
        rows = slice(b * size, (b + 1) * size)
        block = block * score_scale
        return block * cos_ref[rows] - pltpu.roll(block, HEAD // 2, 1) * sin_ref[rows]

    for b in range(blocks):
        block = query_ref[b * size : (b + 1) * size]
        grad = grad_ref[b, 0]
        expo, total = softmax_columns(keys, block, b * size, prefix)
        probs = expo * (1.0 / total)
        d_probs = dot(values, grad, LAST)
        inner = jnp.sum(probs * d_probs, axis=0, keepdims=True)
        d_scores = (probs * (d_probs - inner)).astype(bf16)
        key_part = dot(d_scores, block)
        value_part = dot(probs.astype(bf16), grad)
        if b == 0:
            key_sum[...] = key_part
            value_sum[...] = value_part
        else:
            key_sum[...] += key_part
            value_sum[...] += value_part
        store(b, 0, unrotated(dot(keys_t, d_scores).T, b))
    for b in range(blocks):
        rows = slice(b * size, (b + 1) * size)
        store(b, 1, unrotated(key_sum[rows], b))
        store(b, 2, value_sum[rows])


def attention_specs(groups, size, vocab, twice):
    length = groups * size
    return [
        pl.BlockSpec(memory_space=pltpu.SMEM),
        pl.BlockSpec((groups, 1, size, vocab), lambda s, h: (0, s, 0, 0)),
        pl.BlockSpec((twice, 3, HEAD), lambda s, h: (0, 0, h)),
        pl.BlockSpec((length, HEAD), lambda s, h: (0, 0)),
        pl.BlockSpec((length, HEAD), lambda s, h: (0, 0)),
    ]


def attend(prefix, hot, table, cosine, sine):
    groups, seqs, size, vocab = hot.shape
    heads = table.shape[2] // HEAD
    length = groups * size
    return pl.pallas_call(
        attend_kernel,
        grid=(seqs, heads),
        in_specs=attention_specs(groups, size, vocab, table.shape[0]),
        out_specs=pl.BlockSpec((groups, 1, size, HEAD), lambda s, h: (0, s, 0, h)),
        out_shape=jax.ShapeDtypeStruct((groups, seqs, size, heads * HEAD), bf16),
        scratch_shapes=[pltpu.VMEM((length, HEAD), bf16)],
        compiler_params=pltpu.CompilerParams(vmem_limit_bytes=48 << 20),
        cost_estimate=pl.CostEstimate(
            flops=4 * seqs * heads * length * length * HEAD,
            bytes_accessed=4 * length * heads * HEAD * seqs,
            transcendentals=seqs * heads * length * length,
        ),
    )(prefix, hot, table, cosine, sine)


def attend_back(prefix, hot, table, cosine, sine, grad):
    groups, seqs, size, vocab = hot.shape
    heads = table.shape[2] // HEAD
    length = groups * size
    return pl.pallas_call(
        attend_back_kernel,
        grid=(seqs, heads),
        in_specs=[pl.BlockSpec(memory_space=pltpu.SMEM)]
        + attention_specs(groups, size, vocab, table.shape[0])
        + [pl.BlockSpec((groups, 1, size, HEAD), lambda s, h: (0, s, 0, h))],
        out_specs=pl.BlockSpec((groups, 1, size, 3 * heads * HEAD), lambda s, h: (0, s, 0, 0)),
        out_shape=jax.ShapeDtypeStruct((groups, seqs, size, 3 * heads * HEAD), bf16),
        scratch_shapes=[
            pltpu.VMEM((length, HEAD), bf16),
            pltpu.VMEM((length, HEAD), f32),
            pltpu.VMEM((length, HEAD), f32),
        ],
        compiler_params=pltpu.CompilerParams(vmem_limit_bytes=48 << 20),
        cost_estimate=pl.CostEstimate(
            flops=10 * seqs * heads * length * length * HEAD,
            bytes_accessed=10 * length * heads * HEAD * seqs,
            transcendentals=seqs * heads * length * length,
        ),
    )(place("seq"), prefix, hot, table, cosine, sine, grad)


def on_device(
    token_ids,
    target_ids,
    prefix_lengths,
    cluster_ids,
    cluster_counts,
    embedding,
    qkv_weight,
    out_weight,
    norm1_gain,
    norm1_bias,
    gate_weight,
    up_weight,
    down_weight,
    norm2_gain,
    norm2_bias,
):
    seqs, local_len = token_ids.shape
    count = seqs * local_len
    groups = lax.axis_size("seq")
    dps = lax.axis_size("dp")
    devices = groups * dps
    seq_len = local_len * groups
    my_seq = lax.axis_index("seq")
    my_dp = lax.axis_index("dp")
    positions = my_seq * local_len + jnp.arange(local_len, dtype=jnp.int32)
    rows = qkv_weight.shape[0]
    width = embedding.shape[1]
    vocab_here = embedding.shape[0]
    vocab = vocab_here * devices
    hidden_units = gate_weight.shape[1]
    share = -(-hidden_units // (groups * LANES)) * LANES
    heads_here = HEADS // groups
    head_cols = heads_here * HEAD

    extra = jnp.concatenate(
        [norm1_gain, norm1_bias, norm2_gain, norm2_bias, token_ids.reshape(-1).astype(bf16)]
    )
    extra = jnp.pad(extra, (0, width - extra.shape[0])).reshape(1, width)
    pack = jnp.concatenate([embedding, extra], axis=0)
    chips = dps // 2
    packs = jnp.stack([pack] + [swap(pack, k) for k in range(1, groups)])
    qkv_blocks = swap_all(take_columns(qkv_weight, groups, 3, head_cols))
    packs = jnp.stack([packs] + [swap_dp(packs, 2 * j) for j in range(1, chips)])

    ff_weights = (gate_weight, up_weight, down_weight)
    ff_cols = jnp.concatenate([take_columns(weight, groups, 1, share) for weight in ff_weights], axis=2)
    ff_blocks = swap_all(ff_cols)
    out_mine, packs = together(out_weight, packs)
    packs = jnp.stack([packs, swap_dp(packs, 1)])
    qkv_cols = join_rows(qkv_blocks)
    out_blocks = jnp.stack([out_mine] + [swap_dp(out_mine, 2 * j) for j in range(1, chips)])

    owner = lax.bitwise_xor(my_dp, jnp.arange(2)[:, None] + 2 * jnp.arange(chips)[None, :])
    sender = owner[:, :, None] * groups + lax.bitwise_xor(my_seq, jnp.arange(groups))
    order = (jnp.arange(devices)[:, None] == sender.reshape(1, devices)).astype(bf16)
    packs = dot(order, packs.reshape(devices, (vocab_here + 1) * width)).reshape(devices, vocab_here + 1, width)
    embed_table = packs[:, :vocab_here].reshape(vocab, width).astype(bf16)
    extras = packs[:, vocab_here]
    norms = extras[:, : 4 * rows].reshape(devices, 4, rows)
    norms = norms.transpose(1, 0, 2).reshape(4, width)
    gain_one, bias_one, gain_two, bias_two = norms[0], norms[1], norms[2], norms[3]
    tokens_all = lax.dynamic_slice_in_dim(extras[:, 4 * rows : 4 * rows + count], my_dp * groups, groups, 0)
    tokens_all = tokens_all.astype(jnp.int32).reshape(groups, seqs, local_len)
    vocab_ids = jnp.arange(vocab, dtype=jnp.int32)
    token_hot = (token_ids.reshape(count)[:, None] == vocab_ids[None, :]).astype(bf16)

    piece = vocab // dps
    row_ids = (owner[:, :, None] * piece + jnp.arange(piece)).reshape(vocab).astype(jnp.int32)
    row_hot = (row_ids[:, None] == vocab_ids[None, :]).astype(bf16)
    all_hot = (tokens_all[..., None] == row_ids).astype(bf16)
    embed_dp = lax.dynamic_slice_in_dim(embed_table, my_dp * groups * rows, groups * rows, 1)
    qkv_part = dot(dot(row_hot, embed_dp).astype(bf16), qkv_cols)
    qkv_rows = sum_dp(qkv_part.reshape(2, chips, piece, 3 * head_cols))

    qkv_rows, out_blocks = together(qkv_rows, out_blocks)
    qkv_table, chip_rows = spread_dp(halves(qkv_rows))
    qkv_table = qkv_table.transpose(2, 0, 1, 3, 4)

    ff_cols, qkv_cols, _ = together(join_rows(ff_blocks), qkv_cols, chip_rows)
    gate_w, up_w, down_w, qkv_w = (
        lax.all_gather(cols, "dp", axis=0, tiled=True)
        for cols in (*(ff_cols[:, i * share : (i + 1) * share] for i in range(3)), qkv_cols)
    )
    qkv_table = qkv_table.reshape(2 * vocab, 3, head_cols)
    angles = rotary_angles(jnp.arange(seq_len, dtype=jnp.int32), HEAD)
    cosine, sine = jnp.cos(angles), jnp.sin(angles)
    cosine = jnp.concatenate([cosine, cosine], axis=1)
    sine = jnp.concatenate([-sine, sine], axis=1)

    context = attend(prefix_lengths, all_hot, qkv_table, cosine, sine)
    out_blocks = gather_blocks(out_blocks, context)
    out_full = join_out(out_blocks, swap_dp(out_blocks, 1))
    context = exchange(context, "seq").reshape(groups, count, head_cols)
    context = context.transpose(1, 0, 2).reshape(count, width)

    inputs = dot(token_hot, embed_table)
    hidden, norm_one_pull = jax.vjp(
        layer_norm, deep_alpha * inputs + dot(context, out_full), gain_one, bias_one
    )

    def forward(k, block):
        values = gated_gelu(dot(block, gate_w), dot(block, up_w))
        return tuple(value.astype(bf16) for value in values)

    hidden_blocks, values = gather_tokens(hidden.astype(bf16), forward)
    products, gate_slopes, up_slopes = zip(*values)
    branch = scatter_tokens(lambda k: dot(products[k], down_w, LAST))[0]
    normed, norm_two_pull = jax.vjp(layer_norm, deep_alpha * hidden + branch, gain_two, bias_two)
    activations = normed.astype(bf16)

    logits = dot(activations, embed_table, LAST)
    cluster_hot = cluster_ids[:, None] == jnp.arange(cluster_counts.shape[0], dtype=jnp.int32)[None, :]
    members = jnp.sum(jnp.where(cluster_hot, cluster_counts[None, :], 0), axis=1).astype(f32)
    counted = (positions[None, :] >= prefix_lengths[:, None]).astype(f32)
    coefs = (
        loss_scale
        * (1.0 / members)[:, None]
        / (seq_len - prefix_lengths)[:, None].astype(f32)
        * counted
    )
    logit_exp = jnp.exp(logits - jnp.max(logits, axis=-1, keepdims=True))
    logit_probs = logit_exp / jnp.sum(logit_exp, axis=-1, keepdims=True)
    target_hot = (target_ids.reshape(count)[:, None] == vocab_ids[None, :]).astype(f32)
    d_logits = (coefs.reshape(count, 1) * (logit_probs - target_hot)).astype(bf16)
    head_grad = dot(d_logits, activations, ROWS)
    d_second, d_gain_two, d_bias_two = norm_two_pull(dot(d_logits, embed_table))

    d_second, qkv_w = together(d_second, qkv_w)

    def backward(k, block):
        d_product = dot(block, down_w)
        d_gate = (d_product * gate_slopes[k].astype(f32)).astype(bf16)
        d_up = (d_product * up_slopes[k].astype(f32)).astype(bf16)
        return d_gate, d_up

    d_blocks, values = gather_tokens(d_second.astype(bf16), backward)
    d_gates, d_ups = zip(*values)

    def weight_part(*blocks):
        return dot(jnp.concatenate(blocks[:groups]), jnp.concatenate(blocks[groups:]), ROWS).astype(bf16)

    def last_parts(*blocks):
        return weight_part(*blocks[: 2 * groups]), weight_part(*blocks[2 * groups :])

    d_hidden, gate_part, (up_part, down_part) = scatter_tokens(
        lambda k: dot(d_gates[k], gate_w, LAST) + dot(d_ups[k], up_w, LAST),
        weight_part,
        last_parts,
        (*hidden_blocks, *d_gates),
        (*hidden_blocks, *d_ups, *d_blocks, *products),
    )
    d_hidden = deep_alpha * d_second + d_hidden
    gate_rows, up_rows, down_rows = (
        lax.psum_scatter(part, "dp", scatter_dimension=0, tiled=True)
        for part in (gate_part, up_part, down_part)
    )

    d_first, d_gain_one, d_bias_one = norm_one_pull(d_hidden)
    d_attention = d_first.astype(bf16)
    d_context = dot(d_attention, out_full, LAST).astype(bf16)
    d_context = d_context.reshape(count, groups, head_cols).transpose(1, 0, 2)
    d_context = exchange(d_context, "seq").reshape(groups, seqs, local_len, head_cols)

    out_part = dot(context, d_attention, ROWS).astype(bf16)
    first_low = halves(d_first)
    lookup_first = dot(token_hot, first_low[0], ROWS) + dot(token_hot, first_low[1], ROWS)
    embed_part = head_grad + (lookup_scale * deep_alpha) * lookup_first
    out_part, embed_part, d_context = together(out_part, embed_part, d_context)
    out_rows = lax.psum_scatter(out_part, "dp", scatter_dimension=0, tiled=True)

    def back(s, *before):
        grad = together(d_context[:, s : s + 1], *before)[0]
        block = attend_back(
            prefix_lengths[s : s + 1], all_hot[:, s : s + 1], qkv_table, cosine, sine, grad
        )
        return block.reshape(seq_len, 3 * head_cols)

    def own_rows(mine, *before):
        mine = together(mine, *before)[0]
        return swap_all(take_rows(mine, groups))

    gate_blocks = own_rows(gate_rows, d_context)
    d_qkv, input_blocks = [], []
    for s in range(seqs):
        block = back(s, *input_blocks[-1][0]) if s else back(s)
        part = dot(block, qkv_w, LAST).astype(bf16).reshape(groups, local_len, width)
        if s:
            block, input_blocks[-1] = together(block, input_blocks[-1])
        d_qkv.append(block)
        blocks = swap_all(part)
        input_blocks.append(([part[0]], blocks))
    up_blocks = own_rows(up_rows, d_qkv[0])
    input_grad = deep_alpha * d_first + jnp.concatenate(
        [sum(block.astype(f32) for block in blocks) for _, blocks in input_blocks]
    )

    tokens_near = jnp.stack(
        [lax.dynamic_index_in_dim(tokens_all, lax.bitwise_xor(my_seq, k), 0, False) for k in range(groups)]
    )
    near_hot = (tokens_near[..., None] == row_ids).astype(bf16)
    qkv_sums = sum(dot(near_hot[:, s].reshape(seq_len, vocab), d_qkv[s], ROWS) for s in range(seqs))
    sums_low = halves(qkv_sums)
    sums_low = jnp.stack([dot(row_hot, sums_low[0], ROWS), dot(row_hot, sums_low[1], ROWS)]).astype(bf16)
    lookup = dot(sums_low.reshape(2 * vocab, 3 * head_cols), qkv_w, LAST)
    embed_part = embed_part + lookup_scale * (lookup[:vocab] + lookup[vocab:])
    norm_part = jnp.stack([d_gain_one, d_bias_one, d_gain_two, d_bias_two])
    norm_part = norm_part.reshape(4, devices, rows).transpose(1, 0, 2).reshape(devices, 4 * rows)
    norm_part = jnp.pad(norm_part, ((0, 0), (0, width - 4 * rows))).reshape(devices, 1, width)
    small = jnp.concatenate([embed_part.reshape(devices, vocab_here, width), norm_part], axis=1)
    sums_mine = sum_dp(qkv_sums.reshape(2, chips, piece, 3 * head_cols))
    small, sums_mine, gate_blocks, up_blocks = together(small, sums_mine, gate_blocks, up_blocks)
    small = jnp.sum(exchange(small, BOTH), axis=0)
    embedding_grad = small[:vocab_here]
    norm_grads = small[vocab_here, : 4 * rows].reshape(4, rows)

    sums_all = spread(sums_mine.astype(bf16), BOTH).reshape(dps, groups, piece, 3 * head_cols)
    embed_rows = lax.dynamic_slice_in_dim(embed_table, (my_dp * groups + my_seq) * rows, rows, 1)
    qkv_grad = table_grad(sums_all, embed_rows)

    down_blocks = own_rows(down_rows, sums_mine)
    out_grad = sum(block.astype(f32) for block in own_rows(out_rows, sums_mine))
    gate_grad = join_columns(gate_blocks, hidden_units)
    up_grad = join_columns(up_blocks, hidden_units)
    down_grad = join_columns(down_blocks, hidden_units)

    return (
        activations.reshape(seqs, local_len, width),
        input_grad.reshape(seqs, local_len, width),
        embedding_grad,
        qkv_grad,
        out_grad,
        norm_grads[0],
        norm_grads[1],
        gate_grad,
        up_grad,
        down_grad,
        norm_grads[2],
        norm_grads[3],
    )


def solution(mesh):
    split = P(BOTH, None)
    line = P(BOTH)
    return jax.shard_map(
        on_device,
        mesh=mesh,
        in_specs=(
            P("dp", "seq"),
            P("dp", "seq"),
            P("dp"),
            P("dp"),
            P(),
            split,
            split,
            split,
            line,
            line,
            split,
            split,
            split,
            line,
            line,
        ),
        out_specs=(
            P("dp", "seq", None),
            P("dp", "seq", None),
            split,
            split,
            split,
            line,
            line,
            split,
            split,
            split,
            line,
            line,
        ),
        check_vma=False,
    )
```

time: 1230 us -> 950 us (0.77)
  waiting for transfers between devices: 515 us -> 329 us
  Pallas kernels: 0 us -> 88.7 us
  local copies, waits for them, and re-layouts: 137 us -> 71.8 us
  matrix products: 327 us -> 268 us
  other arithmetic: 108 us -> 70.4 us
  blocking collectives: 30.4 us -> 0 us
    all_to_all x12 -> x4, waiting for transfers between devices: 244 us -> 95.7 us  [exchange(): return lax.all_to_all(blocks, axes, split_axis=0, concat_axis=0, tiled=True)]
    ppermute x16 -> x47, waiting for transfers between devices: 247 us -> 154 us  [swap(): lax.ppermute(block, 'seq', [(s, s ^ bits) for s in range(lax.axis_size('s...]
    pallas_call x0 -> x18, Pallas kernels: none -> 88.7 us  [the longest x2 48.5 us: attend_back(): pl.pallas_call(attend_back_kernel, grid=(seqs, heads), in_specs=[pl.Block...]
    dot_general x6 -> x0, matrix products: 80.5 us -> none  [the longest x1 23.7 us: on_device(): jnp.einsum('sqhe,skhe->shqk', d_context, values, preferred_element_type=f32)]
    all_to_all x12 -> x4, starting transfers between devices: 69.2 us -> 20.8 us  [exchange(): return lax.all_to_all(blocks, axes, split_axis=0, concat_axis=0, tiled=True)]
    dot_general x19 -> x45, matrix products: 228 us -> 268 us  [dot(): return lax.dot_general(left, right, dims, preferred_element_type=f32)]
    convert_element_type x5 -> x1, local copies, waits for them, and re-layouts: 41.4 us -> 1.16 us  [on_device(): embed_table = packs[:, :vocab_here].reshape(vocab, width).astype(bf16)]
    convert_element_type x7 -> x4, other arithmetic: 42.5 us -> 5.21 us  [the longest x1 2.49 us: on_device(): d_blocks, values = gather_tokens(d_second.astype(bf16), backward)]
  transfers between devices with their start and end apart: 36 -> 79, of which waited for: 23 -> 29; matrix products, arithmetic and copies ran while one was open for 42% -> 38% of each run, Pallas kernels for 0% -> 9%
where the time goes in v2:
time: 950 us; the launch traced here: 943 us
  waiting for transfers between devices  329 us (35%)
  matrix products  268 us (28%)
  starting transfers between devices  99 us (10%)
  Pallas kernels  88.7 us (9%)
  local copies, waits for them, and re-layouts  71.8 us (8%)
  other arithmetic  70.4 us (7%)
  between operations  16.3 us (2%)
    dot_general x45, matrix products, dot(): return lax.dot_general(left, right, dims, preferred_element_type=f32)  268 us
    ppermute x47, waiting for transfers between devices, swap(): lax.ppermute(block, 'seq', [(s, s ^ bits) for s in range(lax.axis_size('s...  154 us
    all_to_all x4, waiting for transfers between devices, exchange(): return lax.all_to_all(blocks, axes, split_axis=0, concat_axis=0, tiled=True)  95.7 us
    pallas_call x2, Pallas kernels, attend_back(): pl.pallas_call(attend_back_kernel, grid=(seqs, heads), in_specs=[pl.Block...  48.5 us
    ppermute x47, starting transfers between devices, swap(): lax.ppermute(block, 'seq', [(s, s ^ bits) for s in range(lax.axis_size('s...  42.4 us
    reduce_scatter x1, waiting for transfers between devices, on_device(): out_rows = lax.psum_scatter(out_part, 'dp', scatter_dimension=0, tiled=True)  35.5 us
    ppermute x20, waiting for transfers between devices, swap_dp(): lax.ppermute(block, 'dp', [(d, d ^ bits) for d in range(lax.axis_size('dp...  35.3 us
    ppermute x20, starting transfers between devices, swap_dp(): lax.ppermute(block, 'dp', [(d, d ^ bits) for d in range(lax.axis_size('dp...  34.5 us
  transfers between devices with their start and end apart: 79, of which 29 were waited for; matrix products, arithmetic and copies ran while one was open for 38% of the time, Pallas kernels for 9%

profile of v2, /device:TPU:9, one launch (start us, length us, event | category | flops | bytes accessed | tf_op | source)
XLA Modules:
  0.0 942.7 jit_solution(17872752155018425220)
XLA Ops:
  23.3 5.4 collective-permute-done.5
  43.7 4.6 collective-permute-start.10
  52.7 15.8 %collective-permute-done.16 = bf16[64,2048]{1,0:T(8,128)(2,1)S(1)} collective-permute-done((bf16[64,2048]{1,0:T(8,128)(2,1)S(1)}, bf16[64,2048]{1,0:T(8,128)(2,1)S(1)}, u32[]{:S(2)}, u32[]{:S(2)}) %collective-permute-start.16) | collective-permute-done | bytes 262176 | tf_op jit(solution)/shard_map/ppermute | solution.py:83
  70.5 4.7 collective-permute-done.15
  85.8 7.4 collective-permute-done.30.refs_3_
  109.3 24.8 %shard_map.240 = bf16[4,2,256,512]{3,2,1,0:T(8,128)(2,1)} custom-call(s32[2]{0:T(128)S(1)} %copy-done.22, bf16[4,2,256,128]{3,2,1,0:T(8,128)(2,1)S(1)} %get-tuple-element.323.hot_ref, bf16[256,3,512]{2,1,0:T(4,128)(2,1)S(1)} %reshape.373.table_ref, f32[1024,128]{1,0:T(8,128)S(1)} %get-tuple-element.335.cos_ref, f32[1024,128]{1,0:T(8,128)S(1)} %get-tuple-element.336.sin_ref), custom_call_target="tpu_custom_call" | custom-call | flops 4294967296 | bytes 4194304 | tf_op jit(solution)/shard_map/pallas_call | solution.py:387
  137.0 11.5 %collective-permute-done.24 = bf16[2,64,2048]{2,1,0:T(8,128)(2,1)S(1)} collective-permute-done((bf16[2,64,2048]{2,1,0:T(8,128)(2,1)S(1)}, bf16[2,64,2048]{2,1,0:T(8,128)(2,1)S(1)}, u32[]{:S(2)}, u32[]{:S(2)}) %collective-permute-start.24) | collective-permute-done | bytes 524320 | tf_op jit(solution)/shard_map/ppermute | solution.py:79
  149.6 3.6 pad_maximum_fusion.mine_ref
  154.7 4.5 all-to-all-start
  162.7 21.6 %all-to-all-done = bf16[4,2,256,512]{3,2,1,0:T(8,128)(2,1)} async-done(((bf16[4,2,256,512]{3,2,1,0:T(8,128)(2,1)}), bf16[4,2,256,512]{3,2,1,0:T(8,128)(2,1)}, u32[]{:S(2)}, u32[]{:S(2)}) %all-to-all-start) | async-done | bytes 2097184 | tf_op jit(solution)/shard_map/all_to_all | solution.py:70
  184.3 4.2 copy.49
  188.5 7.5 shard_map.241
  196.1 5.5 fusion.161
  207.5 8.3 fusion.163
  215.7 4.9 all-gather.7.cloned.1.call-done
  220.6 10.8 %fusion.63 = (bf16[512,1408]{1,0:T(8,128)(2,1)}, bf16[512,1408]{1,0:T(8,128)(2,1)}, bf16[512,1408]{1,0:T(8,128)(2,1)}) fusion(f32[512,1408]{1,0:T(8,128)} %fusion.163, bf16[512,2048]{1,0:T(8,128)(2,1)} %fusion.55, bf16[2048,1408]{1,0:T(8,128)(2,1)} %all-gather.7.cloned.1.call-done), kind=kOutput, calls=%fused_computation.92 | convolution fusion | flops 2966487040 | bytes 15073280 | tf_op jit(solution)/shard_map/dot_general | solution.py:29
  231.4 21.0 %collective-permute-done.26 = bf16[512,2048]{1,0:T(8,128)(2,1)} collective-permute-done((bf16[512,2048]{1,0:T(8,128)(2,1)}, bf16[512,2048]{1,0:T(8,128)(2,1)}, u32[]{:S(2)}, u32[]{:S(2)}) %collective-permute-start.26) | collective-permute-done | bytes 2097184 | tf_op jit(solution)/shard_map/ppermute | solution.py:79
  259.6 5.1 fusion.164
  264.7 6.7 fusion.165
  271.4 7.9 fusion.69
  281.4 8.7 fusion.169
  290.1 10.2 %fusion.75 = (bf16[512,1408]{1,0:T(8,128)(2,1)}, bf16[512,1408]{1,0:T(8,128)(2,1)S(1)}, bf16[512,1408]{1,0:T(8,128)(2,1)}) fusion(f32[512,1408]{1,0:T(8,128)S(1)} %copy-done.92, bf16[512,2048]{1,0:T(8,128)(2,1)} %collective-permute-done.27, bf16[2048,1408]{1,0:T(8,128)(2,1)} %all-gather.7.cloned.1.call-done), kind=kOutput, calls=%fused_computation.104 | convolution fusion | flops 2966487040 | bytes 15073280 | tf_op jit(solution)/shard_map/dot_general | solution.py:29
  306.0 5.2 multiply_convert_fusion.8
  311.2 3.9 convolution_convert_fusion.4
  317.8 3.4 fusion.167
  324.7 15.2 %collective-permute-done.33 = bf16[256,2048]{1,0:T(8,128)(2,1)S(1)} collective-permute-done((bf16[256,2048]{1,0:T(8,128)(2,1)S(1)}, bf16[256,2048]{1,0:T(8,128)(2,1)S(1)}, u32[]{:S(2)}, u32[]{:S(2)}) %collective-permute-start.33) | collective-permute-done | bytes 1048608 | tf_op jit(solution)/shard_map/ppermute | solution.py:79
  346.8 44.1 %collective-permute-done.35 = bf16[512,2048]{1,0:T(8,128)(2,1)} collective-permute-done((bf16[512,2048]{1,0:T(8,128)(2,1)}, bf16[512,2048]{1,0:T(8,128)(2,1)}, u32[]{:S(2)}, u32[]{:S(2)}) %collective-permute-start.35) | collective-permute-done | bytes 2097184 | tf_op jit(solution)/shard_map/ppermute | solution.py:79
  391.9 5.6 fusion.150
  409.0 6.6 fusion.170
  416.2 36.7 %collective-permute-done.37 = bf16[512,2048]{1,0:T(8,128)(2,1)S(1)} collective-permute-done((bf16[512,2048]{1,0:T(8,128)(2,1)S(1)}, bf16[512,2048]{1,0:T(8,128)(2,1)S(1)}, u32[]{:S(2)}, u32[]{:S(2)}) %collective-permute-start.37) | collective-permute-done | bytes 2097184 | tf_op jit(solution)/shard_map/ppermute | solution.py:79
  454.7 8.4 multiply_convert_fusion.4
  463.2 4.9 multiply_convert_fusion.2
  468.1 3.4 fusion.174
  471.6 5.0 convolution_add_fusion
  479.2 7.8 multiply_convert_fusion
  487.1 3.4 fusion.171
  490.5 3.7 add_convert_fusion
  496.9 19.1 %fusion.30 = bf16[2048,1408]{1,0:T(8,128)(2,1)} fusion(bf16[512,2048]{1,0:T(8,128)(2,1)} %copy-done.50, bf16[512,2048]{1,0:T(8,128)(2,1)} %collective-permute-done.27, bf16[512,2048]{1,0:T(8,128)(2,1)} %collective-permute-done.26, bf16[512,2048]{1,0:T(8,128)(2,1)} %fusion.55, bf16[512,1408]{1,0:T(8,128)(2,1)} %copy-done.87, ...), kind=kOutput, calls=%fused_computation.26 | convolution fusion | flops 11870666752 | bytes 19922944 | tf_op jit(solution)/shard_map/dot_general | solution.py:29
  516.0 6.1 fusion.172
  522.1 8.3 convolution_add_fusion.2
  533.8 5.0 convolution_add_fusion.1
  552.6 18.7 %fusion.27 = bf16[2048,1408]{1,0:T(8,128)(2,1)} fusion(bf16[512,2048]{1,0:T(8,128)(2,1)} %copy-done.50, bf16[512,2048]{1,0:T(8,128)(2,1)} %collective-permute-done.27, bf16[512,2048]{1,0:T(8,128)(2,1)} %collective-permute-done.26, bf16[512,2048]{1,0:T(8,128)(2,1)} %fusion.55, bf16[512,1408]{1,0:T(8,128)(2,1)} %copy-done.83, ...), kind=kOutput, calls=%fused_computation.25 | convolution fusion | flops 11870666752 | bytes 19922944 | tf_op jit(solution)/shard_map/dot_general | solution.py:29
  571.4 19.7 %fusion.24 = bf16[2048,1408]{1,0:T(8,128)(2,1)} fusion(bf16[512,2048]{1,0:T(8,128)(2,1)} %copy-done.51, bf16[512,2048]{1,0:T(8,128)(2,1)} %copy-done.49, bf16[512,2048]{1,0:T(8,128)(2,1)} %copy-done.48, bf16[512,2048]{1,0:T(8,128)(2,1)} %copy-done.42, bf16[512,1408]{1,0:T(8,128)(2,1)} %copy-done.82, bf16[512,1408]{1,0:T(8,128)(2,1)} %copy-done.85, ...), kind=kOutput, calls=%fused_computation.24 | convolution fusion | flops 11870666752 | bytes 19922944 | tf_op jit(solution)/shard_map/dot_general | solution.py:29
  596.8 8.2 multiply_reduce_fusion.1
  606.2 9.9 %convolution_convert_fusion.3 = bf16[512,2048]{1,0:T(8,128)(2,1)S(1)} fusion(bf16[2048,2048]{1,0:T(8,128)(2,1)} %bitcast.258, f32[512,2048]{1,0:T(8,128)S(1)} %get-tuple-element.227, f32[512]{0:T(512)S(1)} %negate_multiply_fusion), kind=kOutput, calls=%fused_computation.85 | convolution fusion | flops 4298113024 | bytes 14682112 | tf_op jit(solution)/shard_map/dot_general | solution.py:29
  617.6 4.6 all-to-all-start.1
  627.7 7.0 convolution_convert_fusion
  634.7 11.2 %all-to-all-done.1 = bf16[4,512,512]{2,1,0:T(8,128)(2,1)} async-done(((bf16[4,512,512]{2,1,0:T(8,128)(2,1)}), bf16[4,512,512]{2,1,0:T(8,128)(2,1)}, u32[]{:S(2)}, u32[]{:S(2)}) %all-to-all-start.1) | async-done | bytes 2097184 | tf_op jit(solution)/shard_map/all_to_all | solution.py:70
  649.2 24.2 %shard_map.246 = bf16[4,1,256,1536]{3,2,1,0:T(8,128)(2,1)} custom-call(s32[1]{0:T(128)} %bitcast.13.place_ref.seq_ref, s32[1]{0:T(128)} %get-tuple-element.324.prefix_ref, bf16[4,1,256,128]{3,2,1,0:T(8,128)(2,1)S(1)} %get-tuple-element.293.hot_ref, bf16[256,3,512]{2,1,0:T(4,128)(2,1)S(1)} %reshape.373.table_ref, f32[1024,128]{1,0:T(8,128)S(1)} %copy-done.10, ...), custom_call_target="tpu_custom_call" | custom-call | flops 5368709120 | bytes 5242880 | tf_op jit(solution)/shard_map/pallas_call | solution.py:407
  673.4 8.3 convolution_convert_fusion.2
  698.7 24.3 %shard_map.247 = bf16[4,1,256,1536]{3,2,1,0:T(8,128)(2,1)} custom-call(s32[1]{0:T(128)} %bitcast.13.place_ref.seq_ref, s32[1]{0:T(128)} %get-tuple-element.325.prefix_ref, bf16[4,1,256,128]{3,2,1,0:T(8,128)(2,1)S(1)} %get-tuple-element.294.hot_ref, bf16[256,3,512]{2,1,0:T(4,128)(2,1)S(1)} %reshape.373.table_ref, f32[1024,128]{1,0:T(8,128)S(1)} %copy-done.10, ...), custom_call_target="tpu_custom_call" | custom-call | flops 5368709120 | bytes 5242880 | tf_op jit(solution)/shard_map/pallas_call | solution.py:407
  723.1 5.2 collective-permute-done.47
  730.9 4.0 collective-permute-start.51
  735.8 4.8 fusion.175
  757.2 4.6 collective-permute-done.53
  765.2 6.0 collective-permute-done.59.refs_2_
  772.5 4.7 all-to-all-start.2
  777.2 9.9 %convolution_convert_fusion.1 = bf16[1024,2048]{1,0:T(8,128)(2,1)S(1)} fusion(bf16[1024,1536]{1,0:T(8,128)(2,1)} %bitcast.266, bf16[2048,1536]{1,0:T(8,128)(2,1)} %all-gather.11.cloned.1.call-done), kind=kOutput, calls=%fused_computation.76 | convolution fusion | flops 6444548096 | bytes 13631488 | tf_op jit(solution)/shard_map/dot_general | solution.py:29
  793.5 62.9 %all-to-all-done.2 = f32[32,5,2048]{2,1,0:T(8,128)S(1)} async-done(((f32[32,5,2048]{2,1,0:T(8,128)}), f32[32,5,2048]{2,1,0:T(8,128)S(1)}, u32[]{:S(2)}, u32[]{:S(2)}) %all-to-all-start.2) | async-done | bytes 1310752 | tf_op jit(solution)/shard_map/all_to_all | solution.py:70
  858.2 7.0 all-to-all-start.3
  865.2 4.3 convert_add_fusion.1
  869.5 4.3 convert_add_fusion
  878.4 35.5 %reduce-scatter.9.cloned.1.call-done.field_ref = bf16[256,2048]{1,0:T(8,128)(2,1)} async-done(((bf16[2048,2048]{1,0:T(8,128)(2,1)}), bf16[256,2048]{1,0:T(8,128)(2,1)}) %reduce-scatter.9.cloned.1.call-update) | async-done | bytes 1048592 | tf_op jit(solution)/shard_map/reduce_scatter | solution.py:598
  918.8 5.4 maximum_add_fusion
  (541 shorter events, 231.4 us)
Async XLA Ops:
  7.2 200.3 %all-gather.5.cloned.1.call-start = ((), (), s32[]{:S(2)}) async-start(), calls=%async_computation.8 | async-start | bytes 6488064 | tf_op jit(solution)/shard_map/all_gather | solution.py:510
  15.4 18.6 %collective-permute-start.7 = (bf16[64,1536]{1,0:T(8,128)(2,1)S(1)}, bf16[64,1536]{1,0:T(8,128)(2,1)S(1)}, u32[]{:S(2)}, u32[]{:S(2)}) collective-permute-start(bf16[64,1536]{1,0:T(8,128)(2,1)S(1)} %get-tuple-element.279), channel_id=1, source_target_pairs={{0,1},{1,0},{2,3},{3,2},{4,5},{5,4},{6,7},{7,6},{8,9},{9,8},{10,11... | collective-permute-start | bytes 589832 | tf_op jit(solution)/shard_map/ppermute | solution.py:79
  16.7 17.4 %collective-permute-start.8 = (bf16[64,1536]{1,0:T(8,128)(2,1)S(1)}, bf16[64,1536]{1,0:T(8,128)(2,1)S(1)}, u32[]{:S(2)}, u32[]{:S(2)}) collective-permute-start(bf16[64,1536]{1,0:T(8,128)(2,1)S(1)} %get-tuple-element.278), channel_id=1, source_target_pairs={{0,2},{1,3},{2,0},{3,1},{4,6},{5,7},{6,4},{7,5},{8,10},{9,11},{10,... | collective-permute-start | bytes 589832 | tf_op jit(solution)/shard_map/ppermute | solution.py:79
  19.7 9.0 collective-permute-start.5
  48.5 36.6 %collective-permute-start.28 = (bf16[64,4224]{1,0:T(8,128)(2,1)S(1)}, bf16[64,4224]{1,0:T(8,128)(2,1)S(1)}, u32[]{:S(2)}, u32[]{:S(2)}) collective-permute-start(bf16[64,4224]{1,0:T(8,128)(2,1)S(1)} %get-tuple-element.262), channel_id=1, source_target_pairs={{0,1},{1,0},{2,3},{3,2},{4,5},{5,4},{6,7},{7,6},{8,9},{9,8},{10,11... | collective-permute-start | bytes 1622024 | tf_op jit(solution)/shard_map/ppermute | solution.py:79
  48.8 37.0 %collective-permute-start.29 = (bf16[64,4224]{1,0:T(8,128)(2,1)S(1)}, bf16[64,4224]{1,0:T(8,128)(2,1)S(1)}, u32[]{:S(2)}, u32[]{:S(2)}) collective-permute-start(bf16[64,4224]{1,0:T(8,128)(2,1)S(1)} %get-tuple-element.261), channel_id=1, source_target_pairs={{0,2},{1,3},{2,0},{3,1},{4,6},{5,7},{6,4},{7,5},{8,10},{9,11},{10,... | collective-permute-start | bytes 1622024 | tf_op jit(solution)/shard_map/ppermute | solution.py:79
  49.8 18.8 %collective-permute-start.16 = (bf16[64,2048]{1,0:T(8,128)(2,1)S(1)}, bf16[64,2048]{1,0:T(8,128)(2,1)S(1)}, u32[]{:S(2)}, u32[]{:S(2)}) collective-permute-start(bf16[64,2048]{1,0:T(8,128)(2,1)S(1)} %copy-done.52), channel_id=1, source_target_pairs={{0,24},{4,28},{8,16},{12,20},{16,8},{20,12},{24,0},{28,4},{1,25},{... | collective-permute-start | bytes 786440 | tf_op jit(solution)/shard_map/ppermute | solution.py:83
  51.5 23.7 %collective-permute-start.15 = (bf16[64,2048]{1,0:T(8,128)(2,1)S(1)}, bf16[64,2048]{1,0:T(8,128)(2,1)S(1)}, u32[]{:S(2)}, u32[]{:S(2)}) collective-permute-start(bf16[64,2048]{1,0:T(8,128)(2,1)S(1)} %copy-done.52), channel_id=1, source_target_pairs={{0,16},{4,20},{8,24},{12,28},{16,0},{20,4},{24,8},{28,12},{1,17},{... | collective-permute-start | bytes 786440 | tf_op jit(solution)/shard_map/ppermute | solution.py:83
  51.5 24.9 %collective-permute-start.14 = (bf16[64,2048]{1,0:T(8,128)(2,1)S(1)}, bf16[64,2048]{1,0:T(8,128)(2,1)S(1)}, u32[]{:S(2)}, u32[]{:S(2)}) collective-permute-start(bf16[64,2048]{1,0:T(8,128)(2,1)S(1)} %copy-done.52), channel_id=1, source_target_pairs={{0,8},{4,12},{8,0},{12,4},{16,24},{20,28},{24,16},{28,20},{1,9},{5... | collective-permute-start | bytes 786440 | tf_op jit(solution)/shard_map/ppermute | solution.py:83
  68.5 10.9 %collective-permute-start.13 = (f32[16,1536]{1,0:T(8,128)S(1)}, f32[16,1536]{1,0:T(8,128)S(1)}, u32[]{:S(2)}, u32[]{:S(2)}) collective-permute-start(f32[16,1536]{1,0:T(8,128)S(1)} %get-tuple-element.301), channel_id=1, source_target_pairs={{0,24},{4,28},{8,16},{12,20},{16,8},{20,12},{24,0},{28,4},{1,25},{... | collective-permute-start | bytes 294920 | tf_op jit(solution)/shard_map/ppermute | solution.py:83
  79.4 13.8 %collective-permute-start.30 = (bf16[64,4224]{1,0:T(8,128)(2,1)S(1)}, bf16[64,4224]{1,0:T(8,128)(2,1)S(1)}, u32[]{:S(2)}, u32[]{:S(2)}) collective-permute-start(bf16[64,4224]{1,0:T(8,128)(2,1)S(1)} %get-tuple-element.260), channel_id=1, source_target_pairs={{0,3},{1,2},{2,1},{3,0},{4,7},{5,6},{6,5},{7,4},{8,11},{9,10},{10,... | collective-permute-start | bytes 1622024 | tf_op jit(solution)/shard_map/ppermute | solution.py:79
  83.1 10.3 %collective-permute-start.19 = (bf16[2,16,1536]{2,1,0:T(8,128)(2,1)S(1)}, bf16[2,16,1536]{2,1,0:T(8,128)(2,1)S(1)}, u32[]{:S(2)}, u32[]{:S(2)}) collective-permute-start(bf16[2,16,1536]{2,1,0:T(8,128)(2,1)S(1)} %get-tuple-element.306), channel_id=1, source_target_pairs={{0,24},{4,28},{8,16},{12,20},{16,8},{20,12},{24,0},{28,4},{1,25},{... | collective-permute-start | bytes 294920 | tf_op jit(solution)/shard_map/ppermute | solution.py:83
  83.2 10.2 %collective-permute-start.18 = (bf16[2,16,1536]{2,1,0:T(8,128)(2,1)S(1)}, bf16[2,16,1536]{2,1,0:T(8,128)(2,1)S(1)}, u32[]{:S(2)}, u32[]{:S(2)}) collective-permute-start(bf16[2,16,1536]{2,1,0:T(8,128)(2,1)S(1)} %get-tuple-element.306), channel_id=1, source_target_pairs={{0,16},{4,20},{8,24},{12,28},{16,0},{20,4},{24,8},{28,12},{1,17},{... | collective-permute-start | bytes 294920 | tf_op jit(solution)/shard_map/ppermute | solution.py:83
  94.9 125.7 %all-gather.7.cloned.1.call-start = ((), (), s32[]{:S(2)}) async-start(), calls=%async_computation.9 | async-start | bytes 6488064 | tf_op jit(solution)/shard_map/all_gather | solution.py:510
  95.7 185.8 %all-gather.9.cloned.1.call-start = ((), (), s32[]{:S(2)}) async-start(), calls=%async_computation.10 | async-start | bytes 6488064 | tf_op jit(solution)/shard_map/all_gather | solution.py:510
  99.5 34.6 %collective-permute-start.21 = (bf16[4,64,2048]{2,1,0:T(8,128)(2,1)}, bf16[4,64,2048]{2,1,0:T(8,128)(2,1)}, u32[]{:S(2)}, u32[]{:S(2)}) collective-permute-start(bf16[4,64,2048]{2,1,0:T(8,128)(2,1)} %pad_maximum_fusion.8), channel_id=1, source_target_pairs={{0,1},{1,0},{2,3},{3,2},{4,5},{5,4},{6,7},{7,6},{8,9},{9,8},{10,11... | collective-permute-start | bytes 3145736 | tf_op jit(solution)/shard_map/ppermute | solution.py:79
  100.6 33.5 %collective-permute-start.22 = (bf16[4,64,2048]{2,1,0:T(8,128)(2,1)}, bf16[4,64,2048]{2,1,0:T(8,128)(2,1)}, u32[]{:S(2)}, u32[]{:S(2)}) collective-permute-start(bf16[4,64,2048]{2,1,0:T(8,128)(2,1)} %pad_maximum_fusion.8), channel_id=1, source_target_pairs={{0,2},{1,3},{2,0},{3,1},{4,6},{5,7},{6,4},{7,5},{8,10},{9,11},{10,... | collective-permute-start | bytes 3145736 | tf_op jit(solution)/shard_map/ppermute | solution.py:79
  135.2 13.3 %collective-permute-start.24 = (bf16[2,64,2048]{2,1,0:T(8,128)(2,1)S(1)}, bf16[2,64,2048]{2,1,0:T(8,128)(2,1)S(1)}, u32[]{:S(2)}, u32[]{:S(2)}) collective-permute-start(bf16[2,64,2048]{2,1,0:T(8,128)(2,1)S(1)} %slice.309), channel_id=1, source_target_pairs={{0,1},{1,0},{2,3},{3,2},{4,5},{5,4},{6,7},{7,6},{8,9},{9,8},{10,11... | collective-permute-start | bytes 1572872 | tf_op jit(solution)/shard_map/ppermute | solution.py:79
  136.6 12.9 %collective-permute-start.23 = (bf16[2,64,2048]{2,1,0:T(8,128)(2,1)S(1)}, bf16[2,64,2048]{2,1,0:T(8,128)(2,1)S(1)}, u32[]{:S(2)}, u32[]{:S(2)}) collective-permute-start(bf16[2,64,2048]{2,1,0:T(8,128)(2,1)S(1)} %slice.308), channel_id=1, source_target_pairs={{0,2},{1,3},{2,0},{3,1},{4,6},{5,7},{6,4},{7,5},{8,10},{9,11},{10,... | collective-permute-start | bytes 1572872 | tf_op jit(solution)/shard_map/ppermute | solution.py:79
  153.2 35.3 %collective-permute-start.25 = (bf16[4,4,64,2048]{3,2,1,0:T(8,128)(2,1)}, bf16[4,4,64,2048]{3,2,1,0:T(8,128)(2,1)}, u32[]{:S(2)}, u32[]{:S(2)}) collective-permute-start(bf16[4,4,64,2048]{3,2,1,0:T(8,128)(2,1)} %pad_maximum_fusion.mine_ref), channel_id=1, source_target_pairs={{0,4},{4,0},{8,12},{12,8},{16,20},{20,16},{24,28},{28,24},{1,5},{5... | collective-permute-start | bytes 12582920 | tf_op jit(solution)/shard_map/ppermute | solution.py:83
  154.7 29.6 %all-to-all-start = ((bf16[4,2,256,512]{3,2,1,0:T(8,128)(2,1)}), bf16[4,2,256,512]{3,2,1,0:T(8,128)(2,1)}, u32[]{:S(2)}, u32[]{:S(2)}) async-start(bf16[4,2,256,512]{3,2,1,0:T(8,128)(2,1)} %shard_map.240), calls=%async_computation | async-start | bytes 4194304 | tf_op jit(solution)/shard_map/all_to_all | solution.py:70
  159.2 246.4 %all-gather.11.cloned.1.call-start = ((), (), s32[]{:S(2)}) async-start(), calls=%async_computation.11 | async-start | bytes 7077888 | tf_op jit(solution)/shard_map/all_gather | solution.py:510
  205.7 46.7 %collective-permute-start.26 = (bf16[512,2048]{1,0:T(8,128)(2,1)}, bf16[512,2048]{1,0:T(8,128)(2,1)}, u32[]{:S(2)}, u32[]{:S(2)}) collective-permute-start(bf16[512,2048]{1,0:T(8,128)(2,1)} %fusion.55), channel_id=1, source_target_pairs={{0,1},{1,0},{2,3},{3,2},{4,5},{5,4},{6,7},{7,6},{8,9},{9,8},{10,11... | collective-permute-start | bytes 6291464 | tf_op jit(solution)/shard_map/ppermute | solution.py:79
  206.8 46.4 %collective-permute-start.27 = (bf16[512,2048]{1,0:T(8,128)(2,1)}, bf16[512,2048]{1,0:T(8,128)(2,1)}, u32[]{:S(2)}, u32[]{:S(2)}) collective-permute-start(bf16[512,2048]{1,0:T(8,128)(2,1)} %fusion.55), channel_id=1, source_target_pairs={{0,2},{1,3},{2,0},{3,1},{4,6},{5,7},{6,4},{7,5},{8,10},{9,11},{10,... | collective-permute-start | bytes 6291464 | tf_op jit(solution)/shard_map/ppermute | solution.py:79
  207.0 541.1 %reduce-scatter.5.cloned.1.call-start = ((), (), s32[]{:S(2)}) async-start(), calls=%async_computation.12 | async-start | bytes 6488064 | tf_op jit(solution)/shard_map/reduce_scatter | solution.py:583
  255.5 44.8 %collective-permute-start.31 = (bf16[256,2048]{1,0:T(8,128)(2,1)}, bf16[256,2048]{1,0:T(8,128)(2,1)S(1)}, u32[]{:S(2)}, u32[]{:S(2)}) collective-permute-start(bf16[256,2048]{1,0:T(8,128)(2,1)} %slice.319), channel_id=1, source_target_pairs={{0,2},{1,3},{2,0},{3,1},{4,6},{5,7},{6,4},{7,5},{8,10},{9,11},{10,... | collective-permute-start | bytes 3145736 | tf_op jit(solution)/shard_map/ppermute | solution.py:79
  258.5 41.9 %collective-permute-start.32 = (bf16[256,2048]{1,0:T(8,128)(2,1)}, bf16[256,2048]{1,0:T(8,128)(2,1)}, u32[]{:S(2)}, u32[]{:S(2)}) collective-permute-start(bf16[256,2048]{1,0:T(8,128)(2,1)} %slice.320), channel_id=1, source_target_pairs={{0,1},{1,0},{2,3},{3,2},{4,5},{5,4},{6,7},{7,6},{8,9},{9,8},{10,11... | collective-permute-start | bytes 3145736 | tf_op jit(solution)/shard_map/ppermute | solution.py:79
  315.3 24.7 %collective-permute-start.33 = (bf16[256,2048]{1,0:T(8,128)(2,1)S(1)}, bf16[256,2048]{1,0:T(8,128)(2,1)S(1)}, u32[]{:S(2)}, u32[]{:S(2)}) collective-permute-start(bf16[256,2048]{1,0:T(8,128)(2,1)S(1)} %get-tuple-element.269), channel_id=1, source_target_pairs={{0,1},{1,0},{2,3},{3,2},{4,5},{5,4},{6,7},{7,6},{8,9},{9,8},{10,11... | collective-permute-start | bytes 3145736 | tf_op jit(solution)/shard_map/ppermute | solution.py:79
  316.6 24.2 %collective-permute-start.34 = (bf16[256,2048]{1,0:T(8,128)(2,1)S(1)}, bf16[256,2048]{1,0:T(8,128)(2,1)S(1)}, u32[]{:S(2)}, u32[]{:S(2)}) collective-permute-start(bf16[256,2048]{1,0:T(8,128)(2,1)S(1)} %get-tuple-element.268), channel_id=1, source_target_pairs={{0,2},{1,3},{2,0},{3,1},{4,6},{5,7},{6,4},{7,5},{8,10},{9,11},{10,... | collective-permute-start | bytes 3145736 | tf_op jit(solution)/shard_map/ppermute | solution.py:79
  344.8 46.1 %collective-permute-start.35 = (bf16[512,2048]{1,0:T(8,128)(2,1)}, bf16[512,2048]{1,0:T(8,128)(2,1)}, u32[]{:S(2)}, u32[]{:S(2)}) collective-permute-start(bf16[512,2048]{1,0:T(8,128)(2,1)} %pad_maximum_fusion.3), channel_id=1, source_target_pairs={{0,2},{1,3},{2,0},{3,1},{4,6},{5,7},{6,4},{7,5},{8,10},{9,11},{10,... | collective-permute-start | bytes 6291464 | tf_op jit(solution)/shard_map/ppermute | solution.py:79
  346.0 45.9 %collective-permute-start.36 = (bf16[512,2048]{1,0:T(8,128)(2,1)}, bf16[512,2048]{1,0:T(8,128)(2,1)}, u32[]{:S(2)}, u32[]{:S(2)}) collective-permute-start(bf16[512,2048]{1,0:T(8,128)(2,1)} %pad_maximum_fusion.2), channel_id=1, source_target_pairs={{0,1},{1,0},{2,3},{3,2},{4,5},{5,4},{6,7},{7,6},{8,9},{9,8},{10,11... | collective-permute-start | bytes 6291464 | tf_op jit(solution)/shard_map/ppermute | solution.py:79
  408.1 44.7 %collective-permute-start.37 = (bf16[512,2048]{1,0:T(8,128)(2,1)S(1)}, bf16[512,2048]{1,0:T(8,128)(2,1)S(1)}, u32[]{:S(2)}, u32[]{:S(2)}) collective-permute-start(bf16[512,2048]{1,0:T(8,128)(2,1)S(1)} %convert_element_type.296), channel_id=1, source_target_pairs={{0,1},{1,0},{2,3},{3,2},{4,5},{5,4},{6,7},{7,6},{8,9},{9,8},{10,11... | collective-permute-start | bytes 6291464 | tf_op jit(solution)/shard_map/ppermute | solution.py:79
  408.6 44.4 %collective-permute-start.38 = (bf16[512,2048]{1,0:T(8,128)(2,1)S(1)}, bf16[512,2048]{1,0:T(8,128)(2,1)S(1)}, u32[]{:S(2)}, u32[]{:S(2)}) collective-permute-start(bf16[512,2048]{1,0:T(8,128)(2,1)S(1)} %convert_element_type.296), channel_id=1, source_target_pairs={{0,2},{1,3},{2,0},{3,1},{4,6},{5,7},{6,4},{7,5},{8,10},{9,11},{10,... | collective-permute-start | bytes 6291464 | tf_op jit(solution)/shard_map/ppermute | solution.py:79
  453.1 23.6 %collective-permute-start.39 = (bf16[256,2048]{1,0:T(8,128)(2,1)S(1)}, bf16[256,2048]{1,0:T(8,128)(2,1)S(1)}, u32[]{:S(2)}, u32[]{:S(2)}) collective-permute-start(bf16[256,2048]{1,0:T(8,128)(2,1)S(1)} %slice.330), channel_id=1, source_target_pairs={{0,2},{1,3},{2,0},{3,1},{4,6},{5,7},{6,4},{7,5},{8,10},{9,11},{10,... | collective-permute-start | bytes 3145736 | tf_op jit(solution)/shard_map/ppermute | solution.py:79
  453.7 22.9 %collective-permute-start.40 = (bf16[256,2048]{1,0:T(8,128)(2,1)S(1)}, bf16[256,2048]{1,0:T(8,128)(2,1)S(1)}, u32[]{:S(2)}, u32[]{:S(2)}) collective-permute-start(bf16[256,2048]{1,0:T(8,128)(2,1)S(1)} %slice.331), channel_id=1, source_target_pairs={{0,1},{1,0},{2,3},{3,2},{4,5},{5,4},{6,7},{7,6},{8,9},{9,8},{10,11... | collective-permute-start | bytes 3145736 | tf_op jit(solution)/shard_map/ppermute | solution.py:79
  495.8 43.0 %collective-permute-start.41 = (bf16[256,2048]{1,0:T(8,128)(2,1)}, bf16[256,2048]{1,0:T(8,128)(2,1)}, u32[]{:S(2)}, u32[]{:S(2)}) collective-permute-start(bf16[256,2048]{1,0:T(8,128)(2,1)} %get-tuple-element.267), channel_id=1, source_target_pairs={{0,1},{1,0},{2,3},{3,2},{4,5},{5,4},{6,7},{7,6},{8,9},{9,8},{10,11... | collective-permute-start | bytes 3145736 | tf_op jit(solution)/shard_map/ppermute | solution.py:79
  496.2 42.7 %collective-permute-start.42 = (bf16[256,2048]{1,0:T(8,128)(2,1)}, bf16[256,2048]{1,0:T(8,128)(2,1)}, u32[]{:S(2)}, u32[]{:S(2)}) collective-permute-start(bf16[256,2048]{1,0:T(8,128)(2,1)} %get-tuple-element.266), channel_id=1, source_target_pairs={{0,2},{1,3},{2,0},{3,1},{4,6},{5,7},{6,4},{7,5},{8,10},{9,11},{10,... | collective-permute-start | bytes 3145736 | tf_op jit(solution)/shard_map/ppermute | solution.py:79
  538.9 212.1 %reduce-scatter.7.cloned.1.call-start = ((), (), s32[]{:S(2)}) async-start(), calls=%async_computation.13 | async-start | bytes 6488064 | tf_op jit(solution)/shard_map/reduce_scatter | solution.py:583
  550.7 42.0 %collective-permute-start.43 = (bf16[512,2048]{1,0:T(8,128)(2,1)}, bf16[512,2048]{1,0:T(8,128)(2,1)}, u32[]{:S(2)}, u32[]{:S(2)}) collective-permute-start(bf16[512,2048]{1,0:T(8,128)(2,1)} %pad_maximum_fusion.5), channel_id=1, source_target_pairs={{0,2},{1,3},{2,0},{3,1},{4,6},{5,7},{6,4},{7,5},{8,10},{9,11},{10,... | collective-permute-start | bytes 6291464 | tf_op jit(solution)/shard_map/ppermute | solution.py:79
  551.5 42.1 %collective-permute-start.44 = (bf16[512,2048]{1,0:T(8,128)(2,1)}, bf16[512,2048]{1,0:T(8,128)(2,1)}, u32[]{:S(2)}, u32[]{:S(2)}) collective-permute-start(bf16[512,2048]{1,0:T(8,128)(2,1)} %pad_maximum_fusion.4), channel_id=1, source_target_pairs={{0,1},{1,0},{2,3},{3,2},{4,5},{5,4},{6,7},{7,6},{8,9},{9,8},{10,11... | collective-permute-start | bytes 6291464 | tf_op jit(solution)/shard_map/ppermute | solution.py:79
  593.7 280.1 %reduce-scatter.11.cloned.1.call-start = ((), (), s32[]{:S(2)}) async-start(), calls=%async_computation.15 | async-start | bytes 6488064 | tf_op jit(solution)/shard_map/reduce_scatter | solution.py:583
  617.6 28.4 %all-to-all-start.1 = ((bf16[4,512,512]{2,1,0:T(8,128)(2,1)}), bf16[4,512,512]{2,1,0:T(8,128)(2,1)}, u32[]{:S(2)}, u32[]{:S(2)}) async-start(bf16[4,512,512]{2,1,0:T(8,128)(2,1)} %bitcast.263), calls=%async_computation.1 | async-start | bytes 4194304 | tf_op jit(solution)/shard_map/all_to_all | solution.py:70
  622.2 291.7 %reduce-scatter.9.cloned.1.call-start = ((), (), s32[]{:S(2)}) async-start(), calls=%async_computation.14 | async-start | bytes 9437184 | tf_op jit(solution)/shard_map/reduce_scatter | solution.py:598
  683.8 39.2 %collective-permute-start.45 = (bf16[256,2048]{1,0:T(8,128)(2,1)}, bf16[256,2048]{1,0:T(8,128)(2,1)}, u32[]{:S(2)}, u32[]{:S(2)}) collective-permute-start(bf16[256,2048]{1,0:T(8,128)(2,1)} %get-tuple-element.243), channel_id=1, source_target_pairs={{0,1},{1,0},{2,3},{3,2},{4,5},{5,4},{6,7},{7,6},{8,9},{9,8},{10,11... | collective-permute-start | bytes 3145736 | tf_op jit(solution)/shard_map/ppermute | solution.py:79
  683.8 39.2 %collective-permute-start.46 = (bf16[256,2048]{1,0:T(8,128)(2,1)}, bf16[256,2048]{1,0:T(8,128)(2,1)}, u32[]{:S(2)}, u32[]{:S(2)}) collective-permute-start(bf16[256,2048]{1,0:T(8,128)(2,1)} %get-tuple-element.242), channel_id=1, source_target_pairs={{0,2},{1,3},{2,0},{3,1},{4,6},{5,7},{6,4},{7,5},{8,10},{9,11},{10,... | collective-permute-start | bytes 3145736 | tf_op jit(solution)/shard_map/ppermute | solution.py:79
  684.2 44.1 %collective-permute-start.47 = (bf16[256,2048]{1,0:T(8,128)(2,1)}, bf16[256,2048]{1,0:T(8,128)(2,1)}, u32[]{:S(2)}, u32[]{:S(2)}) collective-permute-start(bf16[256,2048]{1,0:T(8,128)(2,1)} %get-tuple-element.241), channel_id=1, source_target_pairs={{0,3},{1,2},{2,1},{3,0},{4,7},{5,6},{6,5},{7,4},{8,11},{9,10},{10,... | collective-permute-start | bytes 3145736 | tf_op jit(solution)/shard_map/ppermute | solution.py:79
  730.9 12.4 %collective-permute-start.51 = (f32[4,16,1536]{2,1,0:T(8,128)S(1)}, f32[4,16,1536]{2,1,0:T(8,128)S(1)}, u32[]{:S(2)}, u32[]{:S(2)}) collective-permute-start(f32[4,16,1536]{2,1,0:T(8,128)S(1)} %bitcast.278), channel_id=1, source_target_pairs={{0,4},{4,0},{8,12},{12,8},{16,20},{20,16},{24,28},{28,24},{1,5},{5... | collective-permute-start | bytes 1179656 | tf_op jit(solution)/shard_map/ppermute | solution.py:83
  745.0 10.8 %collective-permute-start.52 = (f32[16,1536]{1,0:T(8,128)S(1)}, f32[16,1536]{1,0:T(8,128)S(1)}, u32[]{:S(2)}, u32[]{:S(2)}) collective-permute-start(f32[16,1536]{1,0:T(8,128)S(1)} %get-tuple-element.297), channel_id=1, source_target_pairs={{0,8},{4,12},{8,0},{12,4},{16,24},{20,28},{24,16},{28,20},{1,9},{5... | collective-permute-start | bytes 294920 | tf_op jit(solution)/shard_map/ppermute | solution.py:83
  746.2 15.5 %collective-permute-start.53 = (f32[16,1536]{1,0:T(8,128)S(1)}, f32[16,1536]{1,0:T(8,128)S(1)}, u32[]{:S(2)}, u32[]{:S(2)}) collective-permute-start(f32[16,1536]{1,0:T(8,128)S(1)} %get-tuple-element.295), channel_id=1, source_target_pairs={{0,16},{4,20},{8,24},{12,28},{16,0},{20,4},{24,8},{28,12},{1,17},{... | collective-permute-start | bytes 294920 | tf_op jit(solution)/shard_map/ppermute | solution.py:83
  749.3 13.5 %collective-permute-start.55 = (bf16[64,1408]{1,0:T(8,128)(2,1)S(1)}, bf16[64,1408]{1,0:T(8,128)(2,1)S(1)}, u32[]{:S(2)}, u32[]{:S(2)}) collective-permute-start(bf16[64,1408]{1,0:T(8,128)(2,1)S(1)} %get-tuple-element.291), channel_id=1, source_target_pairs={{0,1},{1,0},{2,3},{3,2},{4,5},{5,4},{6,7},{7,6},{8,9},{9,8},{10,11... | collective-permute-start | bytes 540680 | tf_op jit(solution)/shard_map/ppermute | solution.py:79
  750.9 13.5 %collective-permute-start.56 = (bf16[64,1408]{1,0:T(8,128)(2,1)S(1)}, bf16[64,1408]{1,0:T(8,128)(2,1)S(1)}, u32[]{:S(2)}, u32[]{:S(2)}) collective-permute-start(bf16[64,1408]{1,0:T(8,128)(2,1)S(1)} %get-tuple-element.290), channel_id=1, source_target_pairs={{0,2},{1,3},{2,0},{3,1},{4,6},{5,7},{6,4},{7,5},{8,10},{9,11},{10,... | collective-permute-start | bytes 540680 | tf_op jit(solution)/shard_map/ppermute | solution.py:79
  752.2 12.2 %collective-permute-start.57 = (bf16[64,1408]{1,0:T(8,128)(2,1)S(1)}, bf16[64,1408]{1,0:T(8,128)(2,1)S(1)}, u32[]{:S(2)}, u32[]{:S(2)}) collective-permute-start(bf16[64,1408]{1,0:T(8,128)(2,1)S(1)} %get-tuple-element.289), channel_id=1, source_target_pairs={{0,3},{1,2},{2,1},{3,0},{4,7},{5,6},{6,5},{7,4},{8,11},{9,10},{10,... | collective-permute-start | bytes 540680 | tf_op jit(solution)/shard_map/ppermute | solution.py:79
  761.8 9.4 collective-permute-start.59
  772.5 83.9 %all-to-all-start.2 = ((f32[32,5,2048]{2,1,0:T(8,128)}), f32[32,5,2048]{2,1,0:T(8,128)S(1)}, u32[]{:S(2)}, u32[]{:S(2)}) async-start(f32[32,5,2048]{2,1,0:T(8,128)} %pad_maximum_fusion.6), calls=%async_computation.4 | async-start | bytes 4194304 | tf_op jit(solution)/shard_map/all_to_all | solution.py:70
  790.0 79.5 %collective-permute-start.50 = (bf16[256,2048]{1,0:T(8,128)(2,1)}, bf16[256,2048]{1,0:T(8,128)(2,1)}, u32[]{:S(2)}, u32[]{:S(2)}) collective-permute-start(bf16[256,2048]{1,0:T(8,128)(2,1)} %get-tuple-element.246), channel_id=1, source_target_pairs={{0,3},{1,2},{2,1},{3,0},{4,7},{5,6},{6,5},{7,4},{8,11},{9,10},{10,... | collective-permute-start | bytes 3145736 | tf_op jit(solution)/shard_map/ppermute | solution.py:79
  792.1 77.4 %collective-permute-start.49 = (bf16[256,2048]{1,0:T(8,128)(2,1)}, bf16[256,2048]{1,0:T(8,128)(2,1)}, u32[]{:S(2)}, u32[]{:S(2)}) collective-permute-start(bf16[256,2048]{1,0:T(8,128)(2,1)} %get-tuple-element.247), channel_id=1, source_target_pairs={{0,2},{1,3},{2,0},{3,1},{4,6},{5,7},{6,4},{7,5},{8,10},{9,11},{10,... | collective-permute-start | bytes 3145736 | tf_op jit(solution)/shard_map/ppermute | solution.py:79
  792.4 77.1 %collective-permute-start.48 = (bf16[256,2048]{1,0:T(8,128)(2,1)}, bf16[256,2048]{1,0:T(8,128)(2,1)}, u32[]{:S(2)}, u32[]{:S(2)}) collective-permute-start(bf16[256,2048]{1,0:T(8,128)(2,1)} %get-tuple-element.245), channel_id=1, source_target_pairs={{0,1},{1,0},{2,3},{3,2},{4,5},{5,4},{6,7},{7,6},{8,9},{9,8},{10,11... | collective-permute-start | bytes 3145736 | tf_op jit(solution)/shard_map/ppermute | solution.py:79
  858.2 73.8 %all-to-all-start.3 = ((bf16[32,16,1536]{2,1,0:T(8,128)(2,1)}), bf16[32,16,1536]{2,1,0:T(8,128)(2,1)S(1)}, u32[]{:S(2)}, u32[]{:S(2)}) async-start(bf16[32,16,1536]{2,1,0:T(8,128)(2,1)} %broadcast_in_dim.28), calls=%async_computation.5 | async-start | bytes 3145728 | tf_op jit(solution)/shard_map/all_to_all | solution.py:70
  875.8 42.7 %collective-permute-start.64 = (bf16[64,1408]{1,0:T(8,128)(2,1)}, bf16[64,1408]{1,0:T(8,128)(2,1)}, u32[]{:S(2)}, u32[]{:S(2)}) collective-permute-start(bf16[64,1408]{1,0:T(8,128)(2,1)} %get-tuple-element.283), channel_id=1, source_target_pairs={{0,1},{1,0},{2,3},{3,2},{4,5},{5,4},{6,7},{7,6},{8,9},{9,8},{10,11... | collective-permute-start | bytes 540680 | tf_op jit(solution)/shard_map/ppermute | solution.py:79
  877.0 49.8 %collective-permute-start.65 = (bf16[64,1408]{1,0:T(8,128)(2,1)}, bf16[64,1408]{1,0:T(8,128)(2,1)}, u32[]{:S(2)}, u32[]{:S(2)}) collective-permute-start(bf16[64,1408]{1,0:T(8,128)(2,1)} %get-tuple-element.282), channel_id=1, source_target_pairs={{0,2},{1,3},{2,0},{3,1},{4,6},{5,7},{6,4},{7,5},{8,10},{9,11},{10,... | collective-permute-start | bytes 540680 | tf_op jit(solution)/shard_map/ppermute | solution.py:79
  878.2 48.6 %collective-permute-start.66 = (bf16[64,1408]{1,0:T(8,128)(2,1)}, bf16[64,1408]{1,0:T(8,128)(2,1)}, u32[]{:S(2)}, u32[]{:S(2)}) collective-permute-start(bf16[64,1408]{1,0:T(8,128)(2,1)} %get-tuple-element.281), channel_id=1, source_target_pairs={{0,3},{1,2},{2,1},{3,0},{4,7},{5,6},{6,5},{7,4},{8,11},{9,10},{10,... | collective-permute-start | bytes 540680 | tf_op jit(solution)/shard_map/ppermute | solution.py:79
  916.1 17.5 %collective-permute-start.63 = (bf16[64,2048]{1,0:T(8,128)(2,1)}, bf16[64,2048]{1,0:T(8,128)(2,1)}, u32[]{:S(2)}, u32[]{:S(2)}) collective-permute-start(bf16[64,2048]{1,0:T(8,128)(2,1)} %get-tuple-element.271), channel_id=1, source_target_pairs={{0,3},{1,2},{2,1},{3,0},{4,7},{5,6},{6,5},{7,4},{8,11},{9,10},{10,... | collective-permute-start | bytes 786440 | tf_op jit(solution)/shard_map/ppermute | solution.py:79
  917.8 15.8 %collective-permute-start.62 = (bf16[64,2048]{1,0:T(8,128)(2,1)}, bf16[64,2048]{1,0:T(8,128)(2,1)}, u32[]{:S(2)}, u32[]{:S(2)}) collective-permute-start(bf16[64,2048]{1,0:T(8,128)(2,1)} %get-tuple-element.272), channel_id=1, source_target_pairs={{0,2},{1,3},{2,0},{3,1},{4,6},{5,7},{6,4},{7,5},{8,10},{9,11},{10,... | collective-permute-start | bytes 786440 | tf_op jit(solution)/shard_map/ppermute | solution.py:79
  918.5 15.1 %collective-permute-start.61 = (bf16[64,2048]{1,0:T(8,128)(2,1)}, bf16[64,2048]{1,0:T(8,128)(2,1)}, u32[]{:S(2)}, u32[]{:S(2)}) collective-permute-start(bf16[64,2048]{1,0:T(8,128)(2,1)} %get-tuple-element.270), channel_id=1, source_target_pairs={{0,1},{1,0},{2,3},{3,2},{4,5},{5,4},{6,7},{7,6},{8,9},{9,8},{10,11... | collective-permute-start | bytes 786440 | tf_op jit(solution)/shard_map/ppermute | solution.py:79
  (128 other events, 2307.7 us)
Sparse Core Ops, SparseCore 0:
  95.0 59.1 all-gather.4
  156.5 64.1 all-gather.6
  222.3 59.0 all-gather.8
  283.5 63.2 all-gather.10
  539.0 68.0 reduce-scatter.4
  609.2 63.2 reduce-scatter.6
  674.8 63.2 reduce-scatter.10
  740.3 173.5 reduce-scatter.8

commit v3 on v2

--- a/solution.py
+++ b/solution.py
@@ -147,18 +147,43 @@
     )(place("seq"), field)
 
 
-def join_columns(blocks, columns):
+def take_groups(field, groups, rows):
+    dps = field.shape[0] // (groups * rows)
+    columns = field.shape[1]
+
+    def kernel(place_ref, field_ref, out_ref):
+        for d in range(dps):
+            out_ref[0, d * rows : (d + 1) * rows] = field_ref[d, 0]
+
+    return pl.pallas_call(
+        kernel,
+        grid_spec=pltpu.PrefetchScalarGridSpec(
+            num_scalar_prefetch=1,
+            grid=(groups,),
+            in_specs=[
+                pl.BlockSpec((dps, 1, rows, columns), lambda k, at: (0, lax.bitwise_xor(at[0], k), 0, 0))
+            ],
+            out_specs=pl.BlockSpec((1, dps * rows, columns), lambda k, at: (k, 0, 0)),
+        ),
+        out_shape=jax.ShapeDtypeStruct((groups, dps * rows, columns), field.dtype),
+    )(place("seq"), field.reshape(dps, groups, rows, columns))
+
+
+def join_columns(blocks, columns, pieces):
     rows, size = blocks[0].shape
+    size //= pieces
     groups = len(blocks)
 
     def kernel(place_ref, *refs):
         for g in range(groups):
             source = lax.bitwise_xor(place_ref[0], g)
-            block = refs[0][...]
-            for k in range(1, groups):
-                block = jnp.where(source == k, refs[k][...], block)
-            end = min((g + 1) * size, columns)
-            refs[-1][:, g * size : end] = block[:, : end - g * size].astype(f32)
+            for i in range(pieces):
+                block = refs[0][:, i * size : (i + 1) * size]
+                for k in range(1, groups):
+                    block = jnp.where(source == k, refs[k][:, i * size : (i + 1) * size], block)
+                first = (i * groups + g) * size
+                end = min(first + size, columns)
+                refs[-1][:, first:end] = block[:, : end - first].astype(f32)
 
     return pl.pallas_call(
         kernel,
@@ -167,28 +192,6 @@
         out_shape=jax.ShapeDtypeStruct((rows, columns), f32),
         compiler_params=pltpu.CompilerParams(vmem_limit_bytes=16 << 20),
     )(place("seq"), *blocks)
-
-
-def table_grad(sums, embed_rows):
-    dps, groups, piece, columns = sums.shape
-    size = columns // 3
-    rows = embed_rows.shape[1]
-
-    def kernel(sums_ref, embed_ref, out_ref):
-        embed = embed_ref[...]
-        for i in range(3):
-            for g in range(groups):
-                block = sums_ref[:, g, :, i * size : (i + 1) * size].reshape(dps * piece, size)
-                first = (i * groups + g) * size
-                out_ref[:, first : first + size] = dot(embed, block, ROWS)
-
-    return pl.pallas_call(
-        kernel,
-        in_specs=[pl.BlockSpec(memory_space=pltpu.VMEM)] * 2,
-        out_specs=pl.BlockSpec(memory_space=pltpu.VMEM),
-        out_shape=jax.ShapeDtypeStruct((rows, 3 * groups * size), f32),
-        compiler_params=pltpu.CompilerParams(vmem_limit_bytes=24 << 20),
-    )(sums, embed_rows)
 
 
 def join_out(mine, other):
@@ -229,6 +232,27 @@
     )(place("seq"), place("dp"), mine, other).reshape(chips * 2 * groups * rows, width)
 
 
+def join_lanes(sequences):
+    groups = len(sequences[0])
+    rows, size = sequences[0][0].shape
+
+    def kernel(place_ref, *refs):
+        for s in range(len(sequences)):
+            for k in range(groups):
+                first = pl.multiple_of(lax.bitwise_xor(place_ref[0], k) * size, size)
+                refs[-1][s * rows : (s + 1) * rows, pl.ds(first, size)] = refs[s * groups + k][...]
+
+    blocks = [block for sequence in sequences for block in sequence]
+    return pl.pallas_call(
+        kernel,
+        in_specs=[pl.BlockSpec(memory_space=pltpu.SMEM)]
+        + [pl.BlockSpec(memory_space=pltpu.VMEM)] * len(blocks),
+        out_specs=pl.BlockSpec(memory_space=pltpu.VMEM),
+        out_shape=jax.ShapeDtypeStruct((len(sequences) * rows, groups * size), blocks[0].dtype),
+        compiler_params=pltpu.CompilerParams(vmem_limit_bytes=16 << 20),
+    )(place("seq"), *blocks)
+
+
 def sum_dp(parts):
     kept = parts[0] + swap_dp(parts[1], 1)
     return kept[0] + sum(swap_dp(kept[j], 2 * j) for j in range(1, kept.shape[0]))
@@ -239,48 +263,46 @@
     return jnp.stack([blocks, swap_dp(blocks, 1)]), blocks
 
 
-def gather_tokens(block, work):
+def gather_tokens(block, work, own_work):
     if lax.axis_size("seq") != 4:
         blocks = [block] + [swap(block, k) for k in range(1, lax.axis_size("seq"))]
-        return blocks, [work(k, b) for k, b in enumerate(blocks)]
+        return blocks, [None] + [work(k, blocks[k]) for k in range(1, len(blocks))], own_work(block)
     half = block.shape[0] // 2
     near = swap(block, 1)
     over = swap(block, 2)
-    own_work = work(0, block)
-    near, over, own_work = together(near, over, own_work)
+    own_done = own_work(block)
+    near, over, own_done = together(near, over, own_done)
     far_one = swap(near[:half], 2)
     far_two = swap(over[half:], 1)
     near_work, over_work = work(1, near), work(2, over)
     far_one, far_two, near_work, over_work = together(far_one, far_two, near_work, over_work)
     far = jnp.concatenate([far_one, far_two], axis=0)
-    return [block, near, over, far], [own_work, near_work, over_work, work(3, far)]
+    return [block, near, over, far], [None, near_work, over_work, work(3, far)], own_done
 
 
 def gather_blocks(block, held):
     if lax.axis_size("seq") != 4:
-        return jnp.stack([block] + [swap(block, k) for k in range(1, lax.axis_size("seq"))])
+        return jnp.stack([block] + [swap(block, k) for k in range(1, lax.axis_size("seq"))]), held
     half = block.shape[0] // 2
-    near, over = swap(block, 1), swap(block, 2)
-    near_held, over_held, _ = together(near, over, held)
-    far = jnp.concatenate([swap(near_held[:half], 2), swap(over_held[half:], 1)], axis=0)
-    return jnp.stack([block, near, over, far])
-
-
-def scatter_tokens(part, first=None, last=None, first_given=(), last_given=()):
+    near, over, held = together(swap(block, 1), swap(block, 2), held)
+    far = jnp.concatenate([swap(near[:half], 2), swap(over[half:], 1)], axis=0)
+    return jnp.stack([block, near, over, far]), held
+
+
+def scatter_tokens(part, given, first=None, last=None, first_given=(), last_given=()):
     if lax.axis_size("seq") != 4:
-        total = part(0).astype(f32)
+        total = part(given[0]).astype(f32)
         for k in range(1, lax.axis_size("seq")):
-            total = total + swap(part(k).astype(bf16), k).astype(f32)
+            total = total + swap(part(given[k]).astype(bf16), k).astype(f32)
         return total, first and first(*first_given), last and last(*last_given)
-    far = part(3).astype(bf16)
+    far = part(given[3]).astype(bf16)
     half = far.shape[0] // 2
-    far, *first_given = together(far, *first_given)
+    far, given, *first_given = together(far, given[:3], *first_given)
     by_near = swap(far[:half], 1)
     by_over = swap(far[half:], 2)
     first_done = first(*first_given) if first else ()
-    by_near, by_over, near, over, own, first_done = together(
-        by_near, by_over, part(1), part(2), part(0), first_done
-    )
+    near, over, own = part(given[1]), part(given[2]), part(given[0])
+    by_near, by_over, near, over, own, _ = together(by_near, by_over, near, over, own, first_done)
     near_sent = jnp.concatenate([near[:half], near[half:].astype(f32) + by_over.astype(f32)], axis=0)
     over_sent = jnp.concatenate([over[:half].astype(f32) + by_near.astype(f32), over[half:]], axis=0)
     near_sent, over_sent, *last_given = together(near_sent.astype(bf16), over_sent.astype(bf16), *last_given)
@@ -312,7 +334,7 @@
     return expo, jnp.sum(expo, axis=0, keepdims=True)
 
 
-def attend_kernel(prefix_ref, hot_ref, table_ref, cos_ref, sin_ref, out_ref, query_ref):
+def attend_kernel(place_ref, prefix_ref, hot_ref, table_ref, cos_ref, sin_ref, out_ref, query_ref):
     prefix = prefix_ref[pl.program_id(0)]
     queries, keys, values = head_fields(hot_ref, table_ref, cos_ref, sin_ref)
     query_ref[...] = queries
@@ -325,7 +347,7 @@
         top = jnp.max(raw, axis=1, keepdims=True)
         expo = jnp.exp2((raw - top) * (score_scale * LOG2_E))
         total = jnp.sum(expo, axis=1, keepdims=True)
-        out_ref[b, 0] = (dot(expo.astype(bf16), values) * (1.0 / total)).astype(bf16)
+        out_ref[lax.bitwise_xor(place_ref[0], b), 0] = (dot(expo.astype(bf16), values) * (1.0 / total)).astype(bf16)
 
 
 def attend_back_kernel(place_ref, prefix_ref, hot_ref, table_ref, cos_ref, sin_ref, grad_ref, out_ref, query_ref, key_sum, value_sum):
@@ -387,7 +409,8 @@
     return pl.pallas_call(
         attend_kernel,
         grid=(seqs, heads),
-        in_specs=attention_specs(groups, size, vocab, table.shape[0]),
+        in_specs=[pl.BlockSpec(memory_space=pltpu.SMEM)]
+        + attention_specs(groups, size, vocab, table.shape[0]),
         out_specs=pl.BlockSpec((groups, 1, size, HEAD), lambda s, h: (0, s, 0, h)),
         out_shape=jax.ShapeDtypeStruct((groups, seqs, size, heads * HEAD), bf16),
         scratch_shapes=[pltpu.VMEM((length, HEAD), bf16)],
@@ -397,7 +420,7 @@
             bytes_accessed=4 * length * heads * HEAD * seqs,
             transcendentals=seqs * heads * length * length,
         ),
-    )(prefix, hot, table, cosine, sine)
+    )(place("seq"), prefix, hot, table, cosine, sine)
 
 
 def attend_back(prefix, hot, table, cosine, sine, grad):
@@ -498,7 +521,8 @@
     row_hot = (row_ids[:, None] == vocab_ids[None, :]).astype(bf16)
     all_hot = (tokens_all[..., None] == row_ids).astype(bf16)
     embed_dp = lax.dynamic_slice_in_dim(embed_table, my_dp * groups * rows, groups * rows, 1)
-    qkv_part = dot(dot(row_hot, embed_dp).astype(bf16), qkv_cols)
+    embed_dp = dot(row_hot, embed_dp).astype(bf16)
+    qkv_part = dot(embed_dp, qkv_cols)
     qkv_rows = sum_dp(qkv_part.reshape(2, chips, piece, 3 * head_cols))
 
     qkv_rows, out_blocks = together(qkv_rows, out_blocks)
@@ -516,11 +540,15 @@
     cosine = jnp.concatenate([cosine, cosine], axis=1)
     sine = jnp.concatenate([-sine, sine], axis=1)
 
-    context = attend(prefix_lengths, all_hot, qkv_table, cosine, sine)
-    out_blocks = gather_blocks(out_blocks, context)
-    out_full = join_out(out_blocks, swap_dp(out_blocks, 1))
-    context = exchange(context, "seq").reshape(groups, count, head_cols)
-    context = context.transpose(1, 0, 2).reshape(count, width)
+    out_blocks, qkv_table = gather_blocks(out_blocks, qkv_table)
+    contexts = []
+    for s in range(seqs):
+        context = attend(prefix_lengths[s : s + 1], all_hot[:, s : s + 1], qkv_table, cosine, sine)
+        contexts.append(swap_all(context.reshape(groups, local_len, head_cols)))
+    out_blocks, context = together(out_blocks, context)
+    out_other = swap_dp(out_blocks, 1)
+    context = join_lanes(contexts)
+    out_full = join_out(out_blocks, out_other)
 
     inputs = dot(token_hot, embed_table)
     hidden, norm_one_pull = jax.vjp(
@@ -531,9 +559,11 @@
         values = gated_gelu(dot(block, gate_w), dot(block, up_w))
         return tuple(value.astype(bf16) for value in values)
 
-    hidden_blocks, values = gather_tokens(hidden.astype(bf16), forward)
-    products, gate_slopes, up_slopes = zip(*values)
-    branch = scatter_tokens(lambda k: dot(products[k], down_w, LAST))[0]
+    hidden_blocks, values, own_values = gather_tokens(
+        hidden.astype(bf16), forward, lambda block: forward(0, block)
+    )
+    products, gate_slopes, up_slopes = zip(own_values, *values[1:])
+    branch = scatter_tokens(lambda product: dot(product, down_w, LAST), products)[0]
     normed, norm_two_pull = jax.vjp(layer_norm, deep_alpha * hidden + branch, gain_two, bias_two)
     activations = normed.astype(bf16)
 
@@ -562,21 +592,35 @@
         d_up = (d_product * up_slopes[k].astype(f32)).astype(bf16)
         return d_gate, d_up
 
-    d_blocks, values = gather_tokens(d_second.astype(bf16), backward)
-    d_gates, d_ups = zip(*values)
-
-    def weight_part(*blocks):
-        return dot(jnp.concatenate(blocks[:groups]), jnp.concatenate(blocks[groups:]), ROWS).astype(bf16)
-
-    def last_parts(*blocks):
-        return weight_part(*blocks[: 2 * groups]), weight_part(*blocks[2 * groups :])
+    def backward_own(block):
+        d_gate, d_up = backward(0, block)
+        parts = [
+            dot(left, right, ROWS).astype(bf16)
+            for left, right in ((hidden_blocks[0], d_gate), (hidden_blocks[0], d_up), (block, products[0]))
+        ]
+        return d_gate, d_up, dot(d_gate, gate_w, LAST) + dot(d_up, up_w, LAST), parts
+
+    d_blocks, values, own_values = gather_tokens(d_second.astype(bf16), backward, backward_own)
+    d_gates, d_ups = zip(own_values[:2], *values[1:])
+    d_hidden_own, own_parts = own_values[2:]
+
+    def weight_part(own_part, *blocks):
+        rest = dot(jnp.concatenate(blocks[: groups - 1]), jnp.concatenate(blocks[groups - 1 :]), ROWS)
+        return (own_part.astype(f32) + rest).astype(bf16)
+
+    def last_parts(*values):
+        return weight_part(*values[: 2 * groups - 1]), weight_part(*values[2 * groups - 1 :])
+
+    def hidden_part(given):
+        return dot(given[0], gate_w, LAST) + dot(given[1], up_w, LAST) if len(given) > 1 else given[0]
 
     d_hidden, gate_part, (up_part, down_part) = scatter_tokens(
-        lambda k: dot(d_gates[k], gate_w, LAST) + dot(d_ups[k], up_w, LAST),
+        hidden_part,
+        ((d_hidden_own,), *zip(d_gates[1:], d_ups[1:])),
         weight_part,
         last_parts,
-        (*hidden_blocks, *d_gates),
-        (*hidden_blocks, *d_ups, *d_blocks, *products),
+        (own_parts[0], *hidden_blocks[1:], *d_gates[1:]),
+        (own_parts[1], *hidden_blocks[1:], *d_ups[1:], own_parts[2], *d_blocks[1:], *products[1:]),
     )
     d_hidden = deep_alpha * d_second + d_hidden
     gate_rows, up_rows, down_rows = (
@@ -590,12 +634,16 @@
     d_context = d_context.reshape(count, groups, head_cols).transpose(1, 0, 2)
     d_context = exchange(d_context, "seq").reshape(groups, seqs, local_len, head_cols)
 
-    out_part = dot(context, d_attention, ROWS).astype(bf16)
+    half = width // 2
+    out_left = dot(context, d_attention[:, :half], ROWS).astype(bf16)
+    out_right = dot(context, d_attention[:, half:], ROWS).astype(bf16)
     first_low = halves(d_first)
     lookup_first = dot(token_hot, first_low[0], ROWS) + dot(token_hot, first_low[1], ROWS)
     embed_part = head_grad + (lookup_scale * deep_alpha) * lookup_first
-    out_part, embed_part, d_context = together(out_part, embed_part, d_context)
-    out_rows = lax.psum_scatter(out_part, "dp", scatter_dimension=0, tiled=True)
+    out_left = take_groups(out_left, groups, rows)
+    out_left, out_right, embed_part, d_context = together(out_left, out_right, embed_part, d_context)
+    out_right = lax.psum_scatter(out_right, "dp", scatter_dimension=0, tiled=True)
+    out_left = swap_all(out_left)
 
     def back(s, *before):
         grad = together(d_context[:, s : s + 1], *before)[0]
@@ -608,20 +656,23 @@
         mine = together(mine, *before)[0]
         return swap_all(take_rows(mine, groups))
 
-    gate_blocks = own_rows(gate_rows, d_context)
+    gate_blocks = own_rows(gate_rows, d_first)
+    d_context, gate_blocks = together(d_context, gate_blocks)
     d_qkv, input_blocks = [], []
     for s in range(seqs):
-        block = back(s, *input_blocks[-1][0]) if s else back(s)
-        part = dot(block, qkv_w, LAST).astype(bf16).reshape(groups, local_len, width)
+        block = back(s, *input_blocks[-1][:1]) if s else back(s)
         if s:
             block, input_blocks[-1] = together(block, input_blocks[-1])
+        part = dot(block, qkv_w, LAST).astype(bf16).reshape(groups, local_len, width)
+        if s == 0:
+            up_blocks = own_rows(up_rows, block)
+            part, up_blocks, out_left = together(part, up_blocks, out_left)
+        block, part = together(block, part)
         d_qkv.append(block)
-        blocks = swap_all(part)
-        input_blocks.append(([part[0]], blocks))
-    up_blocks = own_rows(up_rows, d_qkv[0])
-    input_grad = deep_alpha * d_first + jnp.concatenate(
-        [sum(block.astype(f32) for block in blocks) for _, blocks in input_blocks]
-    )
+        input_blocks.append(swap_all(part))
+    out_left, _ = together(out_left, d_qkv[-1])
+    out_left = sum(block.astype(f32) for block in out_left).astype(bf16)
+    out_left = lax.psum_scatter(out_left, "dp", scatter_dimension=0, tiled=True)
 
     tokens_near = jnp.stack(
         [lax.dynamic_index_in_dim(tokens_all, lax.bitwise_xor(my_seq, k), 0, False) for k in range(groups)]
@@ -632,25 +683,32 @@
     sums_low = jnp.stack([dot(row_hot, sums_low[0], ROWS), dot(row_hot, sums_low[1], ROWS)]).astype(bf16)
     lookup = dot(sums_low.reshape(2 * vocab, 3 * head_cols), qkv_w, LAST)
     embed_part = embed_part + lookup_scale * (lookup[:vocab] + lookup[vocab:])
-    norm_part = jnp.stack([d_gain_one, d_bias_one, d_gain_two, d_bias_two])
-    norm_part = norm_part.reshape(4, devices, rows).transpose(1, 0, 2).reshape(devices, 4 * rows)
-    norm_part = jnp.pad(norm_part, ((0, 0), (0, width - 4 * rows))).reshape(devices, 1, width)
-    small = jnp.concatenate([embed_part.reshape(devices, vocab_here, width), norm_part], axis=1)
+    norm_part = halves(jnp.stack([d_gain_one, d_bias_one, d_gain_two, d_bias_two]))
+    norm_part = norm_part.reshape(8, devices, rows).transpose(1, 0, 2).reshape(devices, 8 * rows)
+    norm_part = jnp.pad(norm_part, ((0, 0), (0, width - 8 * rows))).reshape(devices, 1, width)
+    small = embed_part.astype(bf16).reshape(devices, vocab_here, width)
+    small = jnp.concatenate([small, norm_part], axis=1)
+    small = jnp.sum(exchange(small, BOTH).astype(f32), axis=0)
+    embedding_grad = small[:vocab_here]
+    norm_grads = small[vocab_here, : 8 * rows].reshape(2, 4, rows)
+    norm_grads = norm_grads[0] + norm_grads[1]
+
     sums_mine = sum_dp(qkv_sums.reshape(2, chips, piece, 3 * head_cols))
-    small, sums_mine, gate_blocks, up_blocks = together(small, sums_mine, gate_blocks, up_blocks)
-    small = jnp.sum(exchange(small, BOTH), axis=0)
-    embedding_grad = small[:vocab_here]
-    norm_grads = small[vocab_here, : 4 * rows].reshape(4, rows)
-
-    sums_all = spread(sums_mine.astype(bf16), BOTH).reshape(dps, groups, piece, 3 * head_cols)
-    embed_rows = lax.dynamic_slice_in_dim(embed_table, (my_dp * groups + my_seq) * rows, rows, 1)
-    qkv_grad = table_grad(sums_all, embed_rows)
+    sums_mine, input_blocks[-1] = together(sums_mine, input_blocks[-1])
+    input_grad = deep_alpha * d_first + jnp.concatenate(
+        [sum(block.astype(f32) for block in blocks) for blocks in input_blocks]
+    )
+    sums_all = spread_dp(sums_mine.astype(bf16))[0].reshape(vocab, 3 * head_cols)
+    qkv_rows = dot(embed_dp, sums_all, ROWS).astype(bf16)
+    qkv_grad = join_columns(own_rows(qkv_rows), 3 * width, 3)
 
     down_blocks = own_rows(down_rows, sums_mine)
-    out_grad = sum(block.astype(f32) for block in own_rows(out_rows, sums_mine))
-    gate_grad = join_columns(gate_blocks, hidden_units)
-    up_grad = join_columns(up_blocks, hidden_units)
-    down_grad = join_columns(down_blocks, hidden_units)
+    gate_grad = join_columns(gate_blocks, hidden_units, 1)
+    up_grad = join_columns(up_blocks, hidden_units, 1)
+    out_blocks = own_rows(out_right, qkv_grad, *down_blocks)
+    down_grad = join_columns(down_blocks, hidden_units, 1)
+    out_right = sum(block.astype(f32) for block in out_blocks)
+    out_grad = jnp.concatenate([out_left.astype(f32), out_right], axis=1)
 
     return (
         activations.reshape(seqs, local_len, width),

time: 950 us -> 836 us (0.88)
  waiting for transfers between devices: 329 us -> 238 us
  matrix products: 268 us -> 245 us
  local copies, waits for them, and re-layouts: 71.8 us -> 51.3 us
  starting transfers between devices: 99 us -> 115 us
    all_to_all x4 -> x2, waiting for transfers between devices: 95.7 us -> 1.69 us  [exchange(): return lax.all_to_all(blocks, axes, split_axis=0, concat_axis=0, tiled=True)]
    reduce_scatter x1 -> x2, waiting for transfers between devices: 35.5 us -> 0.02 us  [the longest x1 0.02 us: on_device(): out_left = lax.psum_scatter(out_left, 'dp', scatter_dimension=0, tiled=True)]
    ppermute x20 -> x24, waiting for transfers between devices: 35.3 us -> 64.2 us  [swap_dp(): lax.ppermute(block, 'dp', [(d, d ^ bits) for d in range(lax.axis_size('dp...]
    dot_general x45 -> x51, matrix products: 268 us -> 245 us  [dot(): return lax.dot_general(left, right, dims, preferred_element_type=f32)]
    ppermute x47 -> x59, starting transfers between devices: 42.4 us -> 52.8 us  [swap(): lax.ppermute(block, 'seq', [(s, s ^ bits) for s in range(lax.axis_size('s...]
    ppermute x20 -> x24, starting transfers between devices: 34.5 us -> 43.6 us  [swap_dp(): lax.ppermute(block, 'dp', [(d, d ^ bits) for d in range(lax.axis_size('dp...]
    pallas_call x2 -> x4, Pallas kernels: 26.3 us -> 30.4 us  [the longest x2 25.3 us: attend(): pl.pallas_call(attend_kernel, grid=(seqs, heads), in_specs=[pl.BlockSpec(...]
    all_to_all x4 -> x2, starting transfers between devices: 20.8 us -> 17.9 us  [exchange(): return lax.all_to_all(blocks, axes, split_axis=0, concat_axis=0, tiled=True)]
  transfers between devices with their start and end apart: 79 -> 94, of which waited for: 29 -> 42; matrix products, arithmetic and copies ran while one was open for 38% -> 36% of each run, Pallas kernels for 9% -> 11%
where the time goes in v3:
time: 836 us; the launch traced here: 824 us
  matrix products  245 us (29%)
  waiting for transfers between devices  238 us (28%)
  starting transfers between devices  115 us (14%)
  Pallas kernels  92.8 us (11%)
  other arithmetic  65 us (8%)
  local copies, waits for them, and re-layouts  51.3 us (6%)
  between operations  16.7 us (2%)
    dot_general x51, matrix products, dot(): return lax.dot_general(left, right, dims, preferred_element_type=f32)  245 us
    ppermute x59, waiting for transfers between devices, swap(): lax.ppermute(block, 'seq', [(s, s ^ bits) for s in range(lax.axis_size('s...  154 us
    ppermute x24, waiting for transfers between devices, swap_dp(): lax.ppermute(block, 'dp', [(d, d ^ bits) for d in range(lax.axis_size('dp...  64.2 us
    ppermute x59, starting transfers between devices, swap(): lax.ppermute(block, 'seq', [(s, s ^ bits) for s in range(lax.axis_size('s...  52.8 us
    pallas_call x2, Pallas kernels, attend_back(): pl.pallas_call(attend_back_kernel, grid=(seqs, heads), in_specs=[pl.Block...  48.4 us
    ppermute x24, starting transfers between devices, swap_dp(): lax.ppermute(block, 'dp', [(d, d ^ bits) for d in range(lax.axis_size('dp...  43.6 us
    pallas_call x2, Pallas kernels, attend(): pl.pallas_call(attend_kernel, grid=(seqs, heads), in_specs=[pl.BlockSpec(...  25.3 us
    unnamed x289, local copies, waits for them, and re-layouts  17.9 us
  transfers between devices with their start and end apart: 94, of which 42 were waited for; matrix products, arithmetic and copies ran while one was open for 36% of the time, Pallas kernels for 11%

profile of v3, /device:TPU:9, one launch (start us, length us, event | category | flops | bytes accessed | tf_op | source)
XLA Modules:
  0.0 823.6 jit_solution(6060904920587854070)
XLA Ops:
  26.3 7.1 collective-permute-done.5
  46.8 7.1 collective-permute-done.14
  57.9 13.4 %collective-permute-done.16 = bf16[64,2048]{1,0:T(8,128)(2,1)S(1)} collective-permute-done((bf16[64,2048]{1,0:T(8,128)(2,1)S(1)}, bf16[64,2048]{1,0:T(8,128)(2,1)S(1)}, u32[]{:S(2)}, u32[]{:S(2)}) %collective-permute-start.16) | collective-permute-done | bytes 262176 | tf_op jit(solution)/shard_map/ppermute | solution.py:83
  80.0 3.8 collective-permute-done.36.refs_3_
  93.8 5.7 collective-permute-start.22
  105.1 6.2 collective-permute-done.17
  117.7 12.7 %shard_map.241 = bf16[4,1,256,512]{3,2,1,0:T(8,128)(2,1)S(1)} custom-call(s32[1]{0:T(128)} %bitcast.12.place_ref.seq_ref, s32[1]{0:T(128)} %get-tuple-element.403.prefix_ref, bf16[4,1,256,128]{3,2,1,0:T(8,128)(2,1)S(1)} %get-tuple-element.366.hot_ref, bf16[256,3,512]{2,1,0:T(4,128)(2,1)S(1)} %reshape.522.table_ref, ...), custom_call_target="tpu_custom_call" | custom-call | flops 2147483648 | bytes 2097152 | tf_op jit(solution)/shard_map/pallas_call | solution.py:409
  134.1 8.7 %collective-permute-start.31 = (bf16[4,4,64,2048]{3,2,1,0:T(8,128)(2,1)}, bf16[4,4,64,2048]{3,2,1,0:T(8,128)(2,1)}, u32[]{:S(2)}, u32[]{:S(2)}) collective-permute-start(bf16[4,4,64,2048]{3,2,1,0:T(8,128)(2,1)} %pad_maximum_fusion.mine_ref), channel_id=1, source_target_pairs={{0,4},{4,0},{8,12},{12,8},{16,20},{20,16},{24,28},{28,24},{1,5},{5... | collective-permute-start | bytes 12582920 | tf_op jit(solution)/shard_map/ppermute | solution.py:83
  146.1 12.6 %shard_map.240 = bf16[4,1,256,512]{3,2,1,0:T(8,128)(2,1)S(1)} custom-call(s32[1]{0:T(128)} %bitcast.12.place_ref.seq_ref, s32[1]{0:T(128)} %get-tuple-element.404.prefix_ref, bf16[4,1,256,128]{3,2,1,0:T(8,128)(2,1)S(1)} %get-tuple-element.367.hot_ref, bf16[256,3,512]{2,1,0:T(4,128)(2,1)S(1)} %reshape.522.table_ref, ...), custom_call_target="tpu_custom_call" | custom-call | flops 2147483648 | bytes 2097152 | tf_op jit(solution)/shard_map/pallas_call | solution.py:409
  162.3 3.7 collective-permute-done.23.refs_1_
  167.5 4.3 collective-permute-done.25.refs_3_
  171.9 7.4 shard_map.243
  179.4 4.7 fusion.131
  188.3 7.6 fusion.134
  195.9 16.1 %all-gather.7.cloned.1.call-done = bf16[2048,1408]{1,0:T(8,128)(2,1)} async-done(((bf16[256,1408]{1,0:T(8,128)(2,1)}), bf16[2048,1408]{1,0:T(8,128)(2,1)}) %all-gather.7.cloned.1.call-update) | async-done | bytes 5767184 | tf_op jit(solution)/shard_map/all_gather | solution.py:534
  212.0 9.2 %fusion.37 = (bf16[512,1408]{1,0:T(8,128)(2,1)}, bf16[512,1408]{1,0:T(8,128)(2,1)}, bf16[512,1408]{1,0:T(8,128)(2,1)}) fusion(f32[512,1408]{1,0:T(8,128)} %fusion.134, bf16[512,2048]{1,0:T(8,128)(2,1)S(1)} %fusion.31, bf16[2048,1408]{1,0:T(8,128)(2,1)} %all-gather.7.cloned.1.call-done), kind=kOutput, calls=%fused_computation.78 | convolution fusion | flops 2966487040 | bytes 15073280 | tf_op jit(solution)/shard_map/dot_general | solution.py:29
  221.2 9.4 %collective-permute-done.32 = bf16[512,2048]{1,0:T(8,128)(2,1)} collective-permute-done((bf16[512,2048]{1,0:T(8,128)(2,1)S(1)}, bf16[512,2048]{1,0:T(8,128)(2,1)}, u32[]{:S(2)}, u32[]{:S(2)}) %collective-permute-start.32) | collective-permute-done | bytes 2097184 | tf_op jit(solution)/shard_map/ppermute | solution.py:79
  236.3 5.2 fusion.136
  241.5 5.1 fusion.135
  246.7 7.8 fusion.49
  254.5 8.1 fusion.43
  268.0 5.2 multiply_convert_fusion.8
  273.3 6.7 convolution_convert_fusion.8
  282.6 5.1 fusion.140
  294.6 6.8 collective-permute-done.39
  307.5 40.6 %collective-permute-done.41 = bf16[512,2048]{1,0:T(8,128)(2,1)} collective-permute-done((bf16[512,2048]{1,0:T(8,128)(2,1)S(1)}, bf16[512,2048]{1,0:T(8,128)(2,1)}, u32[]{:S(2)}, u32[]{:S(2)}) %collective-permute-start.41) | collective-permute-done | bytes 2097184 | tf_op jit(solution)/shard_map/ppermute | solution.py:79
  350.0 5.6 fusion.121
  366.3 5.6 convolution_convert_fusion
  377.3 5.3 convolution_convert_fusion.1
  382.6 5.3 convolution_convert_fusion.2
  391.4 5.0 convolution_add_fusion.2
  396.4 17.4 %collective-permute-done.43 = bf16[512,2048]{1,0:T(8,128)(2,1)S(1)} collective-permute-done((bf16[512,2048]{1,0:T(8,128)(2,1)S(1)}, bf16[512,2048]{1,0:T(8,128)(2,1)S(1)}, u32[]{:S(2)}, u32[]{:S(2)}) %collective-permute-start.43) | collective-permute-done | bytes 2097184 | tf_op jit(solution)/shard_map/ppermute | solution.py:79
  415.5 8.5 %multiply_convert_fusion.2 = (bf16[512,1408]{1,0:T(8,128)(2,1)S(1)}, bf16[512,1408]{1,0:T(8,128)(2,1)}) fusion(bf16[512,1408]{1,0:T(8,128)(2,1)S(1)} %copy-done.121, bf16[512,1408]{1,0:T(8,128)(2,1)S(1)} %copy-done.120, bf16[512,2048]{1,0:T(8,128)(2,1)S(1)} %collective-permute-done.44, bf16[2048,1408]{1,0:T(8,128)(2,1)} %all-gather.9.cloned.1.call-done), kind=kOutput, calls=%fused_computation.99 | convolution fusion | flops 2957115392 | bytes 13631488 | tf_op jit(solution)/shard_map/dot_general | solution.py:29
  424.1 5.0 multiply_convert_fusion.4
  429.1 6.4 collective-permute-done.45
  435.7 4.6 multiply_convert_fusion
  443.8 3.7 add_convert_fusion.3
  447.5 15.9 %add_convert_fusion.2 = bf16[2048,1408]{1,0:T(8,128)(2,1)} fusion(bf16[2048,1408]{1,0:T(8,128)(2,1)} %convolution_convert_fusion.2, bf16[512,2048]{1,0:T(8,128)(2,1)S(1)} %copy-done.63, bf16[512,2048]{1,0:T(8,128)(2,1)} %collective-permute-done.33, bf16[512,2048]{1,0:T(8,128)(2,1)} %collective-permute-done.32, bf16[512,1408]{1,0:T(8,128)(2,1)} %copy-done.119, ...), kind=kOutput, calls=%fused_computation.2 | convolution fusion | flops 8898871296 | bytes 22151168 | tf_op jit(solution)/shard_map/dot_general | solution.py:29
  465.1 5.6 fusion.145
  474.3 4.8 fusion.144
  479.1 5.2 convolution_add_fusion.1
  490.7 15.2 %add_convert_fusion = bf16[2048,1408]{1,0:T(8,128)(2,1)} fusion(bf16[2048,1408]{1,0:T(8,128)(2,1)} %convolution_convert_fusion, bf16[512,2048]{1,0:T(8,128)(2,1)S(1)} %copy-done.65, bf16[512,2048]{1,0:T(8,128)(2,1)S(1)} %copy-done.61, bf16[512,2048]{1,0:T(8,128)(2,1)S(1)} %copy-done.59, bf16[512,1408]{1,0:T(8,128)(2,1)S(1)} %copy-done.112, ...), kind=kOutput, calls=%fused_computation | convolution fusion | flops 8898871296 | bytes 22151168 | tf_op jit(solution)/shard_map/dot_general | solution.py:29
  505.9 15.5 %add_convert_fusion.1 = bf16[2048,1408]{1,0:T(8,128)(2,1)} fusion(bf16[2048,1408]{1,0:T(8,128)(2,1)} %convolution_convert_fusion.1, bf16[512,2048]{1,0:T(8,128)(2,1)} %copy-done.62, bf16[512,2048]{1,0:T(8,128)(2,1)} %collective-permute-done.33, bf16[512,2048]{1,0:T(8,128)(2,1)} %collective-permute-done.32, bf16[512,1408]{1,0:T(8,128)(2,1)} %copy-done.115, ...), kind=kOutput, calls=%fused_computation.1 | convolution fusion | flops 8898871296 | bytes 22151168 | tf_op jit(solution)/shard_map/dot_general | solution.py:29
  521.4 7.0 collective-permute-done.49
  532.5 7.6 multiply_reduce_fusion.1
  543.8 4.8 convolution_convert_fusion.7
  550.1 4.6 all-to-all-start
  554.8 5.6 convolution_convert_fusion.6
  560.4 4.9 shard_map.248
  570.8 4.4 convolution_convert_fusion.5
  580.9 4.3 slice_bitcast_fusion.8
  591.0 24.2 %shard_map.250 = bf16[4,1,256,1536]{3,2,1,0:T(8,128)(2,1)} custom-call(s32[1]{0:T(128)} %bitcast.12.place_ref.seq_ref, s32[1]{0:T(128)} %get-tuple-element.404.prefix_ref, bf16[4,1,256,128]{3,2,1,0:T(8,128)(2,1)S(1)} %copy-done.20, bf16[256,3,512]{2,1,0:T(4,128)(2,1)S(1)} %copy-done.4, f32[1024,128]{1,0:T(8,128)S(1)} %copy-done.13, ...), custom_call_target="tpu_custom_call" | custom-call | flops 5368709120 | bytes 5242880 | tf_op jit(solution)/shard_map/pallas_call | solution.py:430
  619.2 10.0 %convolution_convert_fusion.4 = bf16[1024,2048]{1,0:T(8,128)(2,1)S(1)} fusion(bf16[1024,1536]{1,0:T(8,128)(2,1)} %bitcast.333, bf16[2048,1536]{1,0:T(8,128)(2,1)} %all-gather.11.cloned.1.call-done), kind=kOutput, calls=%fused_computation.64 | convolution fusion | flops 6444548096 | bytes 13631488 | tf_op jit(solution)/shard_map/dot_general | solution.py:29
  631.6 5.1 collective-permute-done.54.refs_1_
  636.6 6.1 collective-permute-done.55.refs_2_
  650.7 24.2 %shard_map.252 = bf16[4,1,256,1536]{3,2,1,0:T(8,128)(2,1)} custom-call(s32[1]{0:T(128)} %bitcast.12.place_ref.seq_ref, s32[1]{0:T(128)} %get-tuple-element.403.prefix_ref, bf16[4,1,256,128]{3,2,1,0:T(8,128)(2,1)S(1)} %copy-done.18, bf16[256,3,512]{2,1,0:T(4,128)(2,1)S(1)} %copy-done.4, f32[1024,128]{1,0:T(8,128)S(1)} %copy-done.13, ...), custom_call_target="tpu_custom_call" | custom-call | flops 5368709120 | bytes 5242880 | tf_op jit(solution)/shard_map/pallas_call | solution.py:430
  675.0 14.6 %collective-permute-done.62 = bf16[256,2048]{1,0:T(8,128)(2,1)S(1)} collective-permute-done((bf16[256,2048]{1,0:T(8,128)(2,1)S(1)}, bf16[256,2048]{1,0:T(8,128)(2,1)S(1)}, u32[]{:S(2)}, u32[]{:S(2)}) %collective-permute-start.62) | collective-permute-done | bytes 1048608 | tf_op jit(solution)/shard_map/ppermute | solution.py:79
  689.6 10.4 %convolution_convert_fusion.3 = bf16[1024,2048]{1,0:T(8,128)(2,1)S(1)} fusion(bf16[1024,1536]{1,0:T(8,128)(2,1)} %bitcast.331, bf16[2048,1536]{1,0:T(8,128)(2,1)} %all-gather.11.cloned.1.call-done), kind=kOutput, calls=%fused_computation.63 | convolution fusion | flops 6444548096 | bytes 13631488 | tf_op jit(solution)/shard_map/dot_general | solution.py:29
  706.4 4.1 collective-permute-start.63
  715.9 13.3 %all-to-all-start.1 = ((bf16[32,5,2048]{2,1,0:T(8,128)(2,1)}), bf16[32,5,2048]{2,1,0:T(8,128)(2,1)S(1)}, u32[]{:S(2)}, u32[]{:S(2)}) async-start(bf16[32,5,2048]{2,1,0:T(8,128)(2,1)} %pad_maximum_fusion.8), calls=%async_computation.3 | async-start | bytes 2097152 | tf_op jit(solution)/shard_map/all_to_all | solution.py:70
  731.9 3.7 add_convert_fusion.5
  738.0 14.4 %collective-permute-done.64 = f32[16,1536]{1,0:T(8,128)S(1)} collective-permute-done((f32[16,1536]{1,0:T(8,128)S(1)}, f32[16,1536]{1,0:T(8,128)S(1)}, u32[]{:S(2)}, u32[]{:S(2)}) %collective-permute-start.64) | collective-permute-done | bytes 98336 | tf_op jit(solution)/shard_map/ppermute | solution.py:83
  758.1 7.5 collective-permute-done.65
  765.6 5.8 collective-permute-done.66
  (647 shorter events, 255.3 us)
Async XLA Ops:
  7.2 181.1 %all-gather.5.cloned.1.call-start = ((), (), s32[]{:S(2)}) async-start(), calls=%async_computation.7 | async-start | bytes 6488064 | tf_op jit(solution)/shard_map/all_gather | solution.py:534
  16.7 19.0 %collective-permute-start.7 = (bf16[64,1536]{1,0:T(8,128)(2,1)}, bf16[64,1536]{1,0:T(8,128)(2,1)S(1)}, u32[]{:S(2)}, u32[]{:S(2)}) collective-permute-start(bf16[64,1536]{1,0:T(8,128)(2,1)} %get-tuple-element.349), channel_id=1, source_target_pairs={{0,1},{1,0},{2,3},{3,2},{4,5},{5,4},{6,7},{7,6},{8,9},{9,8},{10,11... | collective-permute-start | bytes 589832 | tf_op jit(solution)/shard_map/ppermute | solution.py:79
  17.9 17.8 %collective-permute-start.8 = (bf16[64,1536]{1,0:T(8,128)(2,1)}, bf16[64,1536]{1,0:T(8,128)(2,1)S(1)}, u32[]{:S(2)}, u32[]{:S(2)}) collective-permute-start(bf16[64,1536]{1,0:T(8,128)(2,1)} %get-tuple-element.348), channel_id=1, source_target_pairs={{0,2},{1,3},{2,0},{3,1},{4,6},{5,7},{6,4},{7,5},{8,10},{9,11},{10,... | collective-permute-start | bytes 589832 | tf_op jit(solution)/shard_map/ppermute | solution.py:79
  22.2 11.1 %collective-permute-start.5 = (bf16[4,5,2048]{2,1,0:T(8,128)(2,1)S(1)}, bf16[4,5,2048]{2,1,0:T(8,128)(2,1)S(1)}, u32[]{:S(2)}, u32[]{:S(2)}) collective-permute-start(bf16[4,5,2048]{2,1,0:T(8,128)(2,1)S(1)} %get-tuple-element.381), channel_id=1, source_target_pairs={{0,24},{4,28},{8,16},{12,20},{16,8},{20,12},{24,0},{28,4},{1,25},{... | collective-permute-start | bytes 245768 | tf_op jit(solution)/shard_map/ppermute | solution.py:83
  23.8 12.0 %collective-permute-start.9 = (bf16[64,1536]{1,0:T(8,128)(2,1)}, bf16[64,1536]{1,0:T(8,128)(2,1)S(1)}, u32[]{:S(2)}, u32[]{:S(2)}) collective-permute-start(bf16[64,1536]{1,0:T(8,128)(2,1)} %get-tuple-element.347), channel_id=1, source_target_pairs={{0,3},{1,2},{2,1},{3,0},{4,7},{5,6},{6,5},{7,4},{8,11},{9,10},{10,... | collective-permute-start | bytes 589832 | tf_op jit(solution)/shard_map/ppermute | solution.py:79
  43.3 36.6 %collective-permute-start.34 = (bf16[64,4224]{1,0:T(8,128)(2,1)S(1)}, bf16[64,4224]{1,0:T(8,128)(2,1)S(1)}, u32[]{:S(2)}, u32[]{:S(2)}) collective-permute-start(bf16[64,4224]{1,0:T(8,128)(2,1)S(1)} %get-tuple-element.323), channel_id=1, source_target_pairs={{0,1},{1,0},{2,3},{3,2},{4,5},{5,4},{6,7},{7,6},{8,9},{9,8},{10,11... | collective-permute-start | bytes 1622024 | tf_op jit(solution)/shard_map/ppermute | solution.py:79
  43.6 36.4 %collective-permute-start.35 = (bf16[64,4224]{1,0:T(8,128)(2,1)S(1)}, bf16[64,4224]{1,0:T(8,128)(2,1)S(1)}, u32[]{:S(2)}, u32[]{:S(2)}) collective-permute-start(bf16[64,4224]{1,0:T(8,128)(2,1)S(1)} %get-tuple-element.322), channel_id=1, source_target_pairs={{0,2},{1,3},{2,0},{3,1},{4,6},{5,7},{6,4},{7,5},{8,10},{9,11},{10,... | collective-permute-start | bytes 1622024 | tf_op jit(solution)/shard_map/ppermute | solution.py:79
  44.1 13.8 %collective-permute-start.15 = (bf16[64,2048]{1,0:T(8,128)(2,1)S(1)}, bf16[64,2048]{1,0:T(8,128)(2,1)S(1)}, u32[]{:S(2)}, u32[]{:S(2)}) collective-permute-start(bf16[64,2048]{1,0:T(8,128)(2,1)S(1)} %copy-done.70), channel_id=1, source_target_pairs={{0,16},{4,20},{8,24},{12,28},{16,0},{20,4},{24,8},{28,12},{1,17},{... | collective-permute-start | bytes 786440 | tf_op jit(solution)/shard_map/ppermute | solution.py:83
  46.6 24.8 %collective-permute-start.16 = (bf16[64,2048]{1,0:T(8,128)(2,1)S(1)}, bf16[64,2048]{1,0:T(8,128)(2,1)S(1)}, u32[]{:S(2)}, u32[]{:S(2)}) collective-permute-start(bf16[64,2048]{1,0:T(8,128)(2,1)S(1)} %copy-done.70), channel_id=1, source_target_pairs={{0,24},{4,28},{8,16},{12,20},{16,8},{20,12},{24,0},{28,4},{1,25},{... | collective-permute-start | bytes 786440 | tf_op jit(solution)/shard_map/ppermute | solution.py:83
  54.0 19.7 %collective-permute-start.11 = (f32[16,1536]{1,0:T(8,128)S(1)}, f32[16,1536]{1,0:T(8,128)S(1)}, u32[]{:S(2)}, u32[]{:S(2)}) collective-permute-start(f32[16,1536]{1,0:T(8,128)S(1)} %get-tuple-element.375), channel_id=1, source_target_pairs={{0,8},{4,12},{8,0},{12,4},{16,24},{20,28},{24,16},{28,20},{1,9},{5... | collective-permute-start | bytes 294920 | tf_op jit(solution)/shard_map/ppermute | solution.py:83
  57.9 17.8 %collective-permute-start.12 = (f32[16,1536]{1,0:T(8,128)S(1)}, f32[16,1536]{1,0:T(8,128)S(1)}, u32[]{:S(2)}, u32[]{:S(2)}) collective-permute-start(f32[16,1536]{1,0:T(8,128)S(1)} %get-tuple-element.373), channel_id=1, source_target_pairs={{0,16},{4,20},{8,24},{12,28},{16,0},{20,4},{24,8},{28,12},{1,17},{... | collective-permute-start | bytes 294920 | tf_op jit(solution)/shard_map/ppermute | solution.py:83
  87.7 124.2 %all-gather.7.cloned.1.call-start = ((), (), s32[]{:S(2)}) async-start(), calls=%async_computation.8 | async-start | bytes 6488064 | tf_op jit(solution)/shard_map/all_gather | solution.py:534
  88.5 184.8 %all-gather.9.cloned.1.call-start = ((), (), s32[]{:S(2)}) async-start(), calls=%async_computation.9 | async-start | bytes 6488064 | tf_op jit(solution)/shard_map/all_gather | solution.py:534
  89.2 274.4 %all-gather.11.cloned.1.call-start = ((), (), s32[]{:S(2)}) async-start(), calls=%async_computation.10 | async-start | bytes 7077888 | tf_op jit(solution)/shard_map/all_gather | solution.py:534
  91.5 19.7 %collective-permute-start.17 = (bf16[4,64,2048]{2,1,0:T(8,128)(2,1)S(1)}, bf16[4,64,2048]{2,1,0:T(8,128)(2,1)}, u32[]{:S(2)}, u32[]{:S(2)}) collective-permute-start(bf16[4,64,2048]{2,1,0:T(8,128)(2,1)S(1)} %pad_maximum_fusion.7), channel_id=1, source_target_pairs={{0,1},{1,0},{2,3},{3,2},{4,5},{5,4},{6,7},{7,6},{8,9},{9,8},{10,11... | collective-permute-start | bytes 3145736 | tf_op jit(solution)/shard_map/ppermute | solution.py:79
  92.6 19.4 %collective-permute-start.18 = (bf16[4,64,2048]{2,1,0:T(8,128)(2,1)S(1)}, bf16[4,64,2048]{2,1,0:T(8,128)(2,1)}, u32[]{:S(2)}, u32[]{:S(2)}) collective-permute-start(bf16[4,64,2048]{2,1,0:T(8,128)(2,1)S(1)} %pad_maximum_fusion.7), channel_id=1, source_target_pairs={{0,2},{1,3},{2,0},{3,1},{4,6},{5,7},{6,4},{7,5},{8,10},{9,11},{10,... | collective-permute-start | bytes 3145736 | tf_op jit(solution)/shard_map/ppermute | solution.py:79
  113.0 17.5 %collective-permute-start.29 = (bf16[2,64,2048]{2,1,0:T(8,128)(2,1)S(1)}, bf16[2,64,2048]{2,1,0:T(8,128)(2,1)S(1)}, u32[]{:S(2)}, u32[]{:S(2)}) collective-permute-start(bf16[2,64,2048]{2,1,0:T(8,128)(2,1)S(1)} %slice.383), channel_id=1, source_target_pairs={{0,2},{1,3},{2,0},{3,1},{4,6},{5,7},{6,4},{7,5},{8,10},{9,11},{10,... | collective-permute-start | bytes 1572872 | tf_op jit(solution)/shard_map/ppermute | solution.py:79
  115.4 15.1 %collective-permute-start.30 = (bf16[2,64,2048]{2,1,0:T(8,128)(2,1)S(1)}, bf16[2,64,2048]{2,1,0:T(8,128)(2,1)S(1)}, u32[]{:S(2)}, u32[]{:S(2)}) collective-permute-start(bf16[2,64,2048]{2,1,0:T(8,128)(2,1)S(1)} %slice.384), channel_id=1, source_target_pairs={{0,1},{1,0},{2,3},{3,2},{4,5},{5,4},{6,7},{7,6},{8,9},{9,8},{10,11... | collective-permute-start | bytes 1572872 | tf_op jit(solution)/shard_map/ppermute | solution.py:79
  134.1 37.8 %collective-permute-start.31 = (bf16[4,4,64,2048]{3,2,1,0:T(8,128)(2,1)}, bf16[4,4,64,2048]{3,2,1,0:T(8,128)(2,1)}, u32[]{:S(2)}, u32[]{:S(2)}) collective-permute-start(bf16[4,4,64,2048]{3,2,1,0:T(8,128)(2,1)} %pad_maximum_fusion.mine_ref), channel_id=1, source_target_pairs={{0,4},{4,0},{8,12},{12,8},{16,20},{20,16},{24,28},{28,24},{1,5},{5... | collective-permute-start | bytes 12582920 | tf_op jit(solution)/shard_map/ppermute | solution.py:83
  143.4 16.8 %collective-permute-start.26 = (bf16[256,512]{1,0:T(8,128)(2,1)S(1)}, bf16[256,512]{1,0:T(8,128)(2,1)S(1)}, u32[]{:S(2)}, u32[]{:S(2)}) collective-permute-start(bf16[256,512]{1,0:T(8,128)(2,1)S(1)} %get-tuple-element.333), channel_id=1, source_target_pairs={{0,1},{1,0},{2,3},{3,2},{4,5},{5,4},{6,7},{7,6},{8,9},{9,8},{10,11... | collective-permute-start | bytes 786440 | tf_op jit(solution)/shard_map/ppermute | solution.py:79
  144.7 15.7 %collective-permute-start.27 = (bf16[256,512]{1,0:T(8,128)(2,1)S(1)}, bf16[256,512]{1,0:T(8,128)(2,1)S(1)}, u32[]{:S(2)}, u32[]{:S(2)}) collective-permute-start(bf16[256,512]{1,0:T(8,128)(2,1)S(1)} %get-tuple-element.332), channel_id=1, source_target_pairs={{0,2},{1,3},{2,0},{3,1},{4,6},{5,7},{6,4},{7,5},{8,10},{9,11},{10,... | collective-permute-start | bytes 786440 | tf_op jit(solution)/shard_map/ppermute | solution.py:79
  144.9 17.4 %collective-permute-start.28 = (bf16[256,512]{1,0:T(8,128)(2,1)S(1)}, bf16[256,512]{1,0:T(8,128)(2,1)S(1)}, u32[]{:S(2)}, u32[]{:S(2)}) collective-permute-start(bf16[256,512]{1,0:T(8,128)(2,1)S(1)} %get-tuple-element.331), channel_id=1, source_target_pairs={{0,3},{1,2},{2,1},{3,0},{4,7},{5,6},{6,5},{7,4},{8,11},{9,10},{10,... | collective-permute-start | bytes 786440 | tf_op jit(solution)/shard_map/ppermute | solution.py:79
  160.3 11.4 %collective-permute-start.25 = (bf16[256,512]{1,0:T(8,128)(2,1)S(1)}, bf16[256,512]{1,0:T(8,128)(2,1)S(1)}, u32[]{:S(2)}, u32[]{:S(2)}) collective-permute-start(bf16[256,512]{1,0:T(8,128)(2,1)S(1)} %get-tuple-element.335), channel_id=1, source_target_pairs={{0,3},{1,2},{2,1},{3,0},{4,7},{5,6},{6,5},{7,4},{8,11},{9,10},{10,... | collective-permute-start | bytes 786440 | tf_op jit(solution)/shard_map/ppermute | solution.py:79
  186.1 44.5 %collective-permute-start.32 = (bf16[512,2048]{1,0:T(8,128)(2,1)S(1)}, bf16[512,2048]{1,0:T(8,128)(2,1)}, u32[]{:S(2)}, u32[]{:S(2)}) collective-permute-start(bf16[512,2048]{1,0:T(8,128)(2,1)S(1)} %fusion.31), channel_id=1, source_target_pairs={{0,1},{1,0},{2,3},{3,2},{4,5},{5,4},{6,7},{7,6},{8,9},{9,8},{10,11... | collective-permute-start | bytes 6291464 | tf_op jit(solution)/shard_map/ppermute | solution.py:79
  186.9 44.9 %collective-permute-start.33 = (bf16[512,2048]{1,0:T(8,128)(2,1)S(1)}, bf16[512,2048]{1,0:T(8,128)(2,1)}, u32[]{:S(2)}, u32[]{:S(2)}) collective-permute-start(bf16[512,2048]{1,0:T(8,128)(2,1)S(1)} %fusion.31), channel_id=1, source_target_pairs={{0,2},{1,3},{2,0},{3,1},{4,6},{5,7},{6,4},{7,5},{8,10},{9,11},{10,... | collective-permute-start | bytes 6291464 | tf_op jit(solution)/shard_map/ppermute | solution.py:79
  188.2 388.7 %reduce-scatter.6.cloned.1.call-start = ((), (), s32[]{:S(2)}) async-start(), calls=%async_computation.11 | async-start | bytes 6488064 | tf_op jit(solution)/shard_map/reduce_scatter | solution.py:627
  233.1 29.5 %collective-permute-start.37 = (bf16[256,2048]{1,0:T(8,128)(2,1)S(1)}, bf16[256,2048]{1,0:T(8,128)(2,1)S(1)}, u32[]{:S(2)}, u32[]{:S(2)}) collective-permute-start(bf16[256,2048]{1,0:T(8,128)(2,1)S(1)} %slice.394), channel_id=1, source_target_pairs={{0,2},{1,3},{2,0},{3,1},{4,6},{5,7},{6,4},{7,5},{8,10},{9,11},{10,... | collective-permute-start | bytes 3145736 | tf_op jit(solution)/shard_map/ppermute | solution.py:79
  236.0 26.7 %collective-permute-start.38 = (bf16[256,2048]{1,0:T(8,128)(2,1)S(1)}, bf16[256,2048]{1,0:T(8,128)(2,1)S(1)}, u32[]{:S(2)}, u32[]{:S(2)}) collective-permute-start(bf16[256,2048]{1,0:T(8,128)(2,1)S(1)} %slice.395), channel_id=1, source_target_pairs={{0,1},{1,0},{2,3},{3,2},{4,5},{5,4},{6,7},{7,6},{8,9},{9,8},{10,11... | collective-permute-start | bytes 3145736 | tf_op jit(solution)/shard_map/ppermute | solution.py:79
  280.3 21.1 %collective-permute-start.39 = (bf16[256,2048]{1,0:T(8,128)(2,1)S(1)}, bf16[256,2048]{1,0:T(8,128)(2,1)S(1)}, u32[]{:S(2)}, u32[]{:S(2)}) collective-permute-start(bf16[256,2048]{1,0:T(8,128)(2,1)S(1)} %get-tuple-element.330), channel_id=1, source_target_pairs={{0,1},{1,0},{2,3},{3,2},{4,5},{5,4},{6,7},{7,6},{8,9},{9,8},{10,11... | collective-permute-start | bytes 3145736 | tf_op jit(solution)/shard_map/ppermute | solution.py:79
  281.5 20.9 %collective-permute-start.40 = (bf16[256,2048]{1,0:T(8,128)(2,1)S(1)}, bf16[256,2048]{1,0:T(8,128)(2,1)S(1)}, u32[]{:S(2)}, u32[]{:S(2)}) collective-permute-start(bf16[256,2048]{1,0:T(8,128)(2,1)S(1)} %get-tuple-element.329), channel_id=1, source_target_pairs={{0,2},{1,3},{2,0},{3,1},{4,6},{5,7},{6,4},{7,5},{8,10},{9,11},{10,... | collective-permute-start | bytes 3145736 | tf_op jit(solution)/shard_map/ppermute | solution.py:79
  305.1 43.0 %collective-permute-start.41 = (bf16[512,2048]{1,0:T(8,128)(2,1)S(1)}, bf16[512,2048]{1,0:T(8,128)(2,1)}, u32[]{:S(2)}, u32[]{:S(2)}) collective-permute-start(bf16[512,2048]{1,0:T(8,128)(2,1)S(1)} %pad_maximum_fusion.3), channel_id=1, source_target_pairs={{0,2},{1,3},{2,0},{3,1},{4,6},{5,7},{6,4},{7,5},{8,10},{9,11},{10,... | collective-permute-start | bytes 6291464 | tf_op jit(solution)/shard_map/ppermute | solution.py:79
  306.8 43.2 %collective-permute-start.42 = (bf16[512,2048]{1,0:T(8,128)(2,1)}, bf16[512,2048]{1,0:T(8,128)(2,1)}, u32[]{:S(2)}, u32[]{:S(2)}) collective-permute-start(bf16[512,2048]{1,0:T(8,128)(2,1)} %pad_maximum_fusion.2), channel_id=1, source_target_pairs={{0,1},{1,0},{2,3},{3,2},{4,5},{5,4},{6,7},{7,6},{8,9},{9,8},{10,11... | collective-permute-start | bytes 6291464 | tf_op jit(solution)/shard_map/ppermute | solution.py:79
  371.9 41.9 %collective-permute-start.43 = (bf16[512,2048]{1,0:T(8,128)(2,1)S(1)}, bf16[512,2048]{1,0:T(8,128)(2,1)S(1)}, u32[]{:S(2)}, u32[]{:S(2)}) collective-permute-start(bf16[512,2048]{1,0:T(8,128)(2,1)S(1)} %convert_element_type.364), channel_id=1, source_target_pairs={{0,1},{1,0},{2,3},{3,2},{4,5},{5,4},{6,7},{7,6},{8,9},{9,8},{10,11... | collective-permute-start | bytes 6291464 | tf_op jit(solution)/shard_map/ppermute | solution.py:79
  372.2 41.7 %collective-permute-start.44 = (bf16[512,2048]{1,0:T(8,128)(2,1)S(1)}, bf16[512,2048]{1,0:T(8,128)(2,1)S(1)}, u32[]{:S(2)}, u32[]{:S(2)}) collective-permute-start(bf16[512,2048]{1,0:T(8,128)(2,1)S(1)} %convert_element_type.364), channel_id=1, source_target_pairs={{0,2},{1,3},{2,0},{3,1},{4,6},{5,7},{6,4},{7,5},{8,10},{9,11},{10,... | collective-permute-start | bytes 6291464 | tf_op jit(solution)/shard_map/ppermute | solution.py:79
  413.9 21.5 %collective-permute-start.45 = (bf16[256,2048]{1,0:T(8,128)(2,1)S(1)}, bf16[256,2048]{1,0:T(8,128)(2,1)S(1)}, u32[]{:S(2)}, u32[]{:S(2)}) collective-permute-start(bf16[256,2048]{1,0:T(8,128)(2,1)S(1)} %slice.405), channel_id=1, source_target_pairs={{0,2},{1,3},{2,0},{3,1},{4,6},{5,7},{6,4},{7,5},{8,10},{9,11},{10,... | collective-permute-start | bytes 3145736 | tf_op jit(solution)/shard_map/ppermute | solution.py:79
  414.3 21.2 %collective-permute-start.46 = (bf16[256,2048]{1,0:T(8,128)(2,1)S(1)}, bf16[256,2048]{1,0:T(8,128)(2,1)S(1)}, u32[]{:S(2)}, u32[]{:S(2)}) collective-permute-start(bf16[256,2048]{1,0:T(8,128)(2,1)S(1)} %slice.406), channel_id=1, source_target_pairs={{0,1},{1,0},{2,3},{3,2},{4,5},{5,4},{6,7},{7,6},{8,9},{9,8},{10,11... | collective-permute-start | bytes 3145736 | tf_op jit(solution)/shard_map/ppermute | solution.py:79
  463.4 151.8 %reduce-scatter.8.cloned.1.call-start = ((), (), s32[]{:S(2)}) async-start(), calls=%async_computation.12 | async-start | bytes 6488064 | tf_op jit(solution)/shard_map/reduce_scatter | solution.py:627
  463.7 20.6 %collective-permute-start.47 = (bf16[256,2048]{1,0:T(8,128)(2,1)S(1)}, bf16[256,2048]{1,0:T(8,128)(2,1)S(1)}, u32[]{:S(2)}, u32[]{:S(2)}) collective-permute-start(bf16[256,2048]{1,0:T(8,128)(2,1)S(1)} %get-tuple-element.328), channel_id=1, source_target_pairs={{0,1},{1,0},{2,3},{3,2},{4,5},{5,4},{6,7},{7,6},{8,9},{9,8},{10,11... | collective-permute-start | bytes 3145736 | tf_op jit(solution)/shard_map/ppermute | solution.py:79
  465.0 19.4 %collective-permute-start.48 = (bf16[256,2048]{1,0:T(8,128)(2,1)S(1)}, bf16[256,2048]{1,0:T(8,128)(2,1)S(1)}, u32[]{:S(2)}, u32[]{:S(2)}) collective-permute-start(bf16[256,2048]{1,0:T(8,128)(2,1)S(1)} %get-tuple-element.327), channel_id=1, source_target_pairs={{0,2},{1,3},{2,0},{3,1},{4,6},{5,7},{6,4},{7,5},{8,10},{9,11},{10,... | collective-permute-start | bytes 3145736 | tf_op jit(solution)/shard_map/ppermute | solution.py:79
  488.4 40.0 %collective-permute-start.49 = (bf16[512,2048]{1,0:T(8,128)(2,1)}, bf16[512,2048]{1,0:T(8,128)(2,1)S(1)}, u32[]{:S(2)}, u32[]{:S(2)}) collective-permute-start(bf16[512,2048]{1,0:T(8,128)(2,1)} %pad_maximum_fusion.5), channel_id=1, source_target_pairs={{0,2},{1,3},{2,0},{3,1},{4,6},{5,7},{6,4},{7,5},{8,10},{9,11},{10,... | collective-permute-start | bytes 6291464 | tf_op jit(solution)/shard_map/ppermute | solution.py:79
  489.8 39.5 %collective-permute-start.50 = (bf16[512,2048]{1,0:T(8,128)(2,1)}, bf16[512,2048]{1,0:T(8,128)(2,1)}, u32[]{:S(2)}, u32[]{:S(2)}) collective-permute-start(bf16[512,2048]{1,0:T(8,128)(2,1)} %pad_maximum_fusion.4), channel_id=1, source_target_pairs={{0,1},{1,0},{2,3},{3,2},{4,5},{5,4},{6,7},{7,6},{8,9},{9,8},{10,11... | collective-permute-start | bytes 6291464 | tf_op jit(solution)/shard_map/ppermute | solution.py:79
  529.8 245.0 %reduce-scatter.14.cloned.1.call-start = ((), (), s32[]{:S(2)}) async-start(), calls=%async_computation.15 | async-start | bytes 6488064 | tf_op jit(solution)/shard_map/reduce_scatter | solution.py:627
  550.1 26.8 %all-to-all-start = ((bf16[4,512,512]{2,1,0:T(8,128)(2,1)}), bf16[4,512,512]{2,1,0:T(8,128)(2,1)}, u32[]{:S(2)}, u32[]{:S(2)}) async-start(bf16[4,512,512]{2,1,0:T(8,128)(2,1)} %bitcast.325), calls=%async_computation | async-start | bytes 4194304 | tf_op jit(solution)/shard_map/all_to_all | solution.py:70
  554.7 250.3 %reduce-scatter.12.cloned.1.call-start = ((), (), s32[]{:S(2)}) async-start(), calls=%async_computation.14 | async-start | bytes 4718592 | tf_op jit(solution)/shard_map/reduce_scatter | solution.py:645
  585.1 32.6 %collective-permute-start.57 = (bf16[512,1024]{1,0:T(8,128)(2,1)}, bf16[512,1024]{1,0:T(8,128)(2,1)}, u32[]{:S(2)}, u32[]{:S(2)}) collective-permute-start(bf16[512,1024]{1,0:T(8,128)(2,1)} %get-tuple-element.307), channel_id=1, source_target_pairs={{0,1},{1,0},{2,3},{3,2},{4,5},{5,4},{6,7},{7,6},{8,9},{9,8},{10,11... | collective-permute-start | bytes 3145736 | tf_op jit(solution)/shard_map/ppermute | solution.py:79
  585.4 43.9 %collective-permute-start.58 = (bf16[512,1024]{1,0:T(8,128)(2,1)}, bf16[512,1024]{1,0:T(8,128)(2,1)}, u32[]{:S(2)}, u32[]{:S(2)}) collective-permute-start(bf16[512,1024]{1,0:T(8,128)(2,1)} %get-tuple-element.306), channel_id=1, source_target_pairs={{0,2},{1,3},{2,0},{3,1},{4,6},{5,7},{6,4},{7,5},{8,10},{9,11},{10,... | collective-permute-start | bytes 3145736 | tf_op jit(solution)/shard_map/ppermute | solution.py:79
  586.1 45.5 %collective-permute-start.59 = (bf16[512,1024]{1,0:T(8,128)(2,1)}, bf16[512,1024]{1,0:T(8,128)(2,1)}, u32[]{:S(2)}, u32[]{:S(2)}) collective-permute-start(bf16[512,1024]{1,0:T(8,128)(2,1)} %get-tuple-element.305), channel_id=1, source_target_pairs={{0,3},{1,2},{2,1},{3,0},{4,7},{5,6},{6,5},{7,4},{8,11},{9,10},{10,... | collective-permute-start | bytes 3145736 | tf_op jit(solution)/shard_map/ppermute | solution.py:79
  616.5 20.1 %collective-permute-start.54 = (bf16[64,1408]{1,0:T(8,128)(2,1)S(1)}, bf16[64,1408]{1,0:T(8,128)(2,1)S(1)}, u32[]{:S(2)}, u32[]{:S(2)}) collective-permute-start(bf16[64,1408]{1,0:T(8,128)(2,1)S(1)} %get-tuple-element.357), channel_id=1, source_target_pairs={{0,1},{1,0},{2,3},{3,2},{4,5},{5,4},{6,7},{7,6},{8,9},{9,8},{10,11... | collective-permute-start | bytes 540680 | tf_op jit(solution)/shard_map/ppermute | solution.py:79
  616.9 25.8 %collective-permute-start.55 = (bf16[64,1408]{1,0:T(8,128)(2,1)S(1)}, bf16[64,1408]{1,0:T(8,128)(2,1)S(1)}, u32[]{:S(2)}, u32[]{:S(2)}) collective-permute-start(bf16[64,1408]{1,0:T(8,128)(2,1)S(1)} %get-tuple-element.356), channel_id=1, source_target_pairs={{0,2},{1,3},{2,0},{3,1},{4,6},{5,7},{6,4},{7,5},{8,10},{9,11},{10,... | collective-permute-start | bytes 540680 | tf_op jit(solution)/shard_map/ppermute | solution.py:79
  617.7 25.0 %collective-permute-start.56 = (bf16[64,1408]{1,0:T(8,128)(2,1)S(1)}, bf16[64,1408]{1,0:T(8,128)(2,1)S(1)}, u32[]{:S(2)}, u32[]{:S(2)}) collective-permute-start(bf16[64,1408]{1,0:T(8,128)(2,1)S(1)} %get-tuple-element.355), channel_id=1, source_target_pairs={{0,3},{1,2},{2,1},{3,0},{4,7},{5,6},{6,5},{7,4},{8,11},{9,10},{10,... | collective-permute-start | bytes 540680 | tf_op jit(solution)/shard_map/ppermute | solution.py:79
  644.0 30.9 %collective-permute-start.60 = (bf16[256,2048]{1,0:T(8,128)(2,1)S(1)}, bf16[256,2048]{1,0:T(8,128)(2,1)S(1)}, u32[]{:S(2)}, u32[]{:S(2)}) collective-permute-start(bf16[256,2048]{1,0:T(8,128)(2,1)S(1)} %get-tuple-element.303), channel_id=1, source_target_pairs={{0,1},{1,0},{2,3},{3,2},{4,5},{5,4},{6,7},{7,6},{8,9},{9,8},{10,11... | collective-permute-start | bytes 3145736 | tf_op jit(solution)/shard_map/ppermute | solution.py:79
  644.5 30.4 %collective-permute-start.61 = (bf16[256,2048]{1,0:T(8,128)(2,1)S(1)}, bf16[256,2048]{1,0:T(8,128)(2,1)S(1)}, u32[]{:S(2)}, u32[]{:S(2)}) collective-permute-start(bf16[256,2048]{1,0:T(8,128)(2,1)S(1)} %get-tuple-element.302), channel_id=1, source_target_pairs={{0,2},{1,3},{2,0},{3,1},{4,6},{5,7},{6,4},{7,5},{8,10},{9,11},{10,... | collective-permute-start | bytes 3145736 | tf_op jit(solution)/shard_map/ppermute | solution.py:79
  645.4 44.2 %collective-permute-start.62 = (bf16[256,2048]{1,0:T(8,128)(2,1)S(1)}, bf16[256,2048]{1,0:T(8,128)(2,1)S(1)}, u32[]{:S(2)}, u32[]{:S(2)}) collective-permute-start(bf16[256,2048]{1,0:T(8,128)(2,1)S(1)} %get-tuple-element.301), channel_id=1, source_target_pairs={{0,3},{1,2},{2,1},{3,0},{4,7},{5,6},{6,5},{7,4},{8,11},{9,10},{10,... | collective-permute-start | bytes 3145736 | tf_op jit(solution)/shard_map/ppermute | solution.py:79
  702.3 69.7 %collective-permute-start.67 = (bf16[256,2048]{1,0:T(8,128)(2,1)}, bf16[256,2048]{1,0:T(8,128)(2,1)}, u32[]{:S(2)}, u32[]{:S(2)}) collective-permute-start(bf16[256,2048]{1,0:T(8,128)(2,1)} %get-tuple-element.299), channel_id=1, source_target_pairs={{0,1},{1,0},{2,3},{3,2},{4,5},{5,4},{6,7},{7,6},{8,9},{9,8},{10,11... | collective-permute-start | bytes 3145736 | tf_op jit(solution)/shard_map/ppermute | solution.py:79
  702.4 69.6 %collective-permute-start.68 = (bf16[256,2048]{1,0:T(8,128)(2,1)}, bf16[256,2048]{1,0:T(8,128)(2,1)}, u32[]{:S(2)}, u32[]{:S(2)}) collective-permute-start(bf16[256,2048]{1,0:T(8,128)(2,1)} %get-tuple-element.298), channel_id=1, source_target_pairs={{0,2},{1,3},{2,0},{3,1},{4,6},{5,7},{6,4},{7,5},{8,10},{9,11},{10,... | collective-permute-start | bytes 3145736 | tf_op jit(solution)/shard_map/ppermute | solution.py:79
  702.7 69.4 %collective-permute-start.69 = (bf16[256,2048]{1,0:T(8,128)(2,1)}, bf16[256,2048]{1,0:T(8,128)(2,1)}, u32[]{:S(2)}, u32[]{:S(2)}) collective-permute-start(bf16[256,2048]{1,0:T(8,128)(2,1)} %get-tuple-element.297), channel_id=1, source_target_pairs={{0,3},{1,2},{2,1},{3,0},{4,7},{5,6},{6,5},{7,4},{8,11},{9,10},{10,... | collective-permute-start | bytes 3145736 | tf_op jit(solution)/shard_map/ppermute | solution.py:79
  706.4 22.8 %collective-permute-start.63 = (f32[4,16,1536]{2,1,0:T(8,128)}, f32[4,16,1536]{2,1,0:T(8,128)S(1)}, u32[]{:S(2)}, u32[]{:S(2)}) collective-permute-start(f32[4,16,1536]{2,1,0:T(8,128)} %bitcast.87), channel_id=1, source_target_pairs={{0,4},{4,0},{8,12},{12,8},{16,20},{20,16},{24,28},{28,24},{1,5},{5... | collective-permute-start | bytes 1179656 | tf_op jit(solution)/shard_map/ppermute | solution.py:83
  715.9 74.7 %all-to-all-start.1 = ((bf16[32,5,2048]{2,1,0:T(8,128)(2,1)}), bf16[32,5,2048]{2,1,0:T(8,128)(2,1)S(1)}, u32[]{:S(2)}, u32[]{:S(2)}) async-start(bf16[32,5,2048]{2,1,0:T(8,128)(2,1)} %pad_maximum_fusion.8), calls=%async_computation.3 | async-start | bytes 2097152 | tf_op jit(solution)/shard_map/all_to_all | solution.py:70
  729.2 85.7 %reduce-scatter.10.cloned.1.call-start = ((), (), s32[]{:S(2)}) async-start(), calls=%async_computation.13 | async-start | bytes 1179648 | tf_op jit(solution)/shard_map/reduce_scatter | solution.py:675
  731.7 20.7 %collective-permute-start.64 = (f32[16,1536]{1,0:T(8,128)S(1)}, f32[16,1536]{1,0:T(8,128)S(1)}, u32[]{:S(2)}, u32[]{:S(2)}) collective-permute-start(f32[16,1536]{1,0:T(8,128)S(1)} %get-tuple-element.370), channel_id=1, source_target_pairs={{0,8},{4,12},{8,0},{12,4},{16,24},{20,28},{24,16},{28,20},{1,9},{5... | collective-permute-start | bytes 294920 | tf_op jit(solution)/shard_map/ppermute | solution.py:83
  735.6 30.0 %collective-permute-start.65 = (f32[16,1536]{1,0:T(8,128)}, f32[16,1536]{1,0:T(8,128)S(1)}, u32[]{:S(2)}, u32[]{:S(2)}) collective-permute-start(f32[16,1536]{1,0:T(8,128)} %get-tuple-element.368), channel_id=1, source_target_pairs={{0,16},{4,20},{8,24},{12,28},{16,0},{20,4},{24,8},{28,12},{1,17},{... | collective-permute-start | bytes 294920 | tf_op jit(solution)/shard_map/ppermute | solution.py:83
  753.0 18.3 %collective-permute-start.66 = (f32[16,1536]{1,0:T(8,128)}, f32[16,1536]{1,0:T(8,128)S(1)}, u32[]{:S(2)}, u32[]{:S(2)}) collective-permute-start(f32[16,1536]{1,0:T(8,128)} %get-tuple-element.369), channel_id=1, source_target_pairs={{0,24},{4,28},{8,16},{12,20},{16,8},{20,12},{24,0},{28,4},{1,25},{... | collective-permute-start | bytes 294920 | tf_op jit(solution)/shard_map/ppermute | solution.py:83
  776.0 13.3 %collective-permute-start.77 = (bf16[64,1408]{1,0:T(8,128)(2,1)S(1)}, bf16[64,1408]{1,0:T(8,128)(2,1)S(1)}, u32[]{:S(2)}, u32[]{:S(2)}) collective-permute-start(bf16[64,1408]{1,0:T(8,128)(2,1)S(1)} %get-tuple-element.353), channel_id=1, source_target_pairs={{0,1},{1,0},{2,3},{3,2},{4,5},{5,4},{6,7},{7,6},{8,9},{9,8},{10,11... | collective-permute-start | bytes 540680 | tf_op jit(solution)/shard_map/ppermute | solution.py:79
  777.2 12.0 %collective-permute-start.78 = (bf16[64,1408]{1,0:T(8,128)(2,1)S(1)}, bf16[64,1408]{1,0:T(8,128)(2,1)S(1)}, u32[]{:S(2)}, u32[]{:S(2)}) collective-permute-start(bf16[64,1408]{1,0:T(8,128)(2,1)S(1)} %get-tuple-element.352), channel_id=1, source_target_pairs={{0,2},{1,3},{2,0},{3,1},{4,6},{5,7},{6,4},{7,5},{8,10},{9,11},{10,... | collective-permute-start | bytes 540680 | tf_op jit(solution)/shard_map/ppermute | solution.py:79
  (173 other events, 1850.4 us)
Sparse Core Ops, SparseCore 0:
  87.9 62.7 all-gather.4
  152.8 59.0 all-gather.6
  214.2 59.0 all-gather.8
  275.4 63.3 all-gather.10
  463.5 73.3 reduce-scatter.5
  539.1 66.9 reduce-scatter.7
  608.4 63.0 reduce-scatter.13
  673.8 48.4 reduce-scatter.11
  735.7 38.6 reduce-scatter.9

commit v4 on v3

--- a/solution.py
+++ b/solution.py
@@ -131,66 +131,51 @@
     )(place("seq"), *blocks)
 
 
-def take_rows(field, groups):
-    rows, columns = field.shape[0] // groups, field.shape[1]
-
-    def kernel(place_ref, field_ref, out_ref):
+def take_rows(fields, groups):
+    rows = fields[0].shape[0] // groups
+    columns = [field.shape[1] for field in fields]
+
+    def kernel(place_ref, *refs):
         for g in range(groups):
-            out_ref[lax.bitwise_xor(place_ref[0], g)] = field_ref[g * rows : (g + 1) * rows]
+            first = 0
+            for field_ref, size in zip(refs, columns):
+                block = field_ref[g * rows : (g + 1) * rows]
+                refs[-1][lax.bitwise_xor(place_ref[0], g), :, first : first + size] = block
+                first += size
 
     return pl.pallas_call(
         kernel,
-        in_specs=[pl.BlockSpec(memory_space=pltpu.SMEM), pl.BlockSpec(memory_space=pltpu.VMEM)],
+        in_specs=[pl.BlockSpec(memory_space=pltpu.SMEM)]
+        + [pl.BlockSpec(memory_space=pltpu.VMEM)] * len(fields),
         out_specs=pl.BlockSpec(memory_space=pltpu.VMEM),
-        out_shape=jax.ShapeDtypeStruct((groups, rows, columns), field.dtype),
-        compiler_params=pltpu.CompilerParams(vmem_limit_bytes=16 << 20),
-    )(place("seq"), field)
-
-
-def take_groups(field, groups, rows):
-    dps = field.shape[0] // (groups * rows)
-    columns = field.shape[1]
-
-    def kernel(place_ref, field_ref, out_ref):
-        for d in range(dps):
-            out_ref[0, d * rows : (d + 1) * rows] = field_ref[d, 0]
-
-    return pl.pallas_call(
-        kernel,
-        grid_spec=pltpu.PrefetchScalarGridSpec(
-            num_scalar_prefetch=1,
-            grid=(groups,),
-            in_specs=[
-                pl.BlockSpec((dps, 1, rows, columns), lambda k, at: (0, lax.bitwise_xor(at[0], k), 0, 0))
-            ],
-            out_specs=pl.BlockSpec((1, dps * rows, columns), lambda k, at: (k, 0, 0)),
-        ),
-        out_shape=jax.ShapeDtypeStruct((groups, dps * rows, columns), field.dtype),
-    )(place("seq"), field.reshape(dps, groups, rows, columns))
-
-
-def join_columns(blocks, columns, pieces):
+        out_shape=jax.ShapeDtypeStruct((groups, rows, sum(columns)), fields[0].dtype),
+        compiler_params=pltpu.CompilerParams(vmem_limit_bytes=24 << 20),
+    )(place("seq"), *fields)
+
+
+def join_columns(blocks, columns, pieces, fields):
     rows, size = blocks[0].shape
-    size //= pieces
+    size //= pieces * fields
     groups = len(blocks)
 
     def kernel(place_ref, *refs):
         for g in range(groups):
             source = lax.bitwise_xor(place_ref[0], g)
-            for i in range(pieces):
+            for i in range(pieces * fields):
                 block = refs[0][:, i * size : (i + 1) * size]
                 for k in range(1, groups):
                     block = jnp.where(source == k, refs[k][:, i * size : (i + 1) * size], block)
-                first = (i * groups + g) * size
+                out_ref = refs[groups + i // pieces]
+                first = (i % pieces * groups + g) * size
                 end = min(first + size, columns)
-                refs[-1][:, first:end] = block[:, : end - first].astype(f32)
+                out_ref[:, first:end] = block[:, : end - first].astype(f32)
 
     return pl.pallas_call(
         kernel,
         in_specs=[pl.BlockSpec(memory_space=pltpu.SMEM)] + [pl.BlockSpec(memory_space=pltpu.VMEM)] * groups,
-        out_specs=pl.BlockSpec(memory_space=pltpu.VMEM),
-        out_shape=jax.ShapeDtypeStruct((rows, columns), f32),
-        compiler_params=pltpu.CompilerParams(vmem_limit_bytes=16 << 20),
+        out_specs=[pl.BlockSpec(memory_space=pltpu.VMEM)] * fields,
+        out_shape=[jax.ShapeDtypeStruct((rows, columns), f32)] * fields,
+        compiler_params=pltpu.CompilerParams(vmem_limit_bytes=24 << 20),
     )(place("seq"), *blocks)
 
 
@@ -350,18 +335,27 @@
         out_ref[lax.bitwise_xor(place_ref[0], b), 0] = (dot(expo.astype(bf16), values) * (1.0 / total)).astype(bf16)
 
 
-def attend_back_kernel(place_ref, prefix_ref, hot_ref, table_ref, cos_ref, sin_ref, grad_ref, out_ref, query_ref, key_sum, value_sum):
+def probs_kernel(prefix_ref, hot_ref, table_ref, cos_ref, sin_ref, field_ref, probs_ref):
     prefix = prefix_ref[pl.program_id(0)]
-    head = pl.program_id(1)
     queries, keys, values = head_fields(hot_ref, table_ref, cos_ref, sin_ref)
-    query_ref[...] = queries
-    keys_t = keys.T
+    field_ref[0, 0, 0], field_ref[0, 0, 1], field_ref[0, 0, 2] = queries, keys, values
+    _, _, blocks, _, size = probs_ref.shape
+    for b in range(blocks):
+        block = field_ref[0, 0, 0, b * size : (b + 1) * size]
+        expo, total = softmax_columns(keys, block, b * size, prefix)
+        probs_ref[0, 0, b] = (expo * (1.0 / total)).astype(bf16)
+
+
+def attend_back_kernel(place_ref, field_ref, probs_ref, cos_ref, sin_ref, grad_ref, out_ref, key_sum, value_sum):
+    head = pl.program_id(0)
+    keys_t = field_ref[0, 0, 1].T
+    values = field_ref[0, 0, 2]
     blocks, _, size, _ = grad_ref.shape
     width = out_ref.shape[-1] // 3
 
     def store(b, part, block):
         column = pl.multiple_of(part * width + head * HEAD, HEAD)
-        out_ref[lax.bitwise_xor(place_ref[0], b), 0, :, pl.ds(column, HEAD)] = block.astype(bf16)
+        out_ref[lax.bitwise_xor(place_ref[0], b), :, pl.ds(column, HEAD)] = block.astype(bf16)
 
     def unrotated(block, b):
         rows = slice(b * size, (b + 1) * size)
@@ -369,15 +363,15 @@
         return block * cos_ref[rows] - pltpu.roll(block, HEAD // 2, 1) * sin_ref[rows]
 
     for b in range(blocks):
-        block = query_ref[b * size : (b + 1) * size]
+        block = field_ref[0, 0, 0, b * size : (b + 1) * size]
         grad = grad_ref[b, 0]
-        expo, total = softmax_columns(keys, block, b * size, prefix)
-        probs = expo * (1.0 / total)
+        probs_low = probs_ref[0, 0, b]
+        probs = probs_low.astype(f32)
         d_probs = dot(values, grad, LAST)
         inner = jnp.sum(probs * d_probs, axis=0, keepdims=True)
         d_scores = (probs * (d_probs - inner)).astype(bf16)
         key_part = dot(d_scores, block)
-        value_part = dot(probs.astype(bf16), grad)
+        value_part = dot(probs_low, grad)
         if b == 0:
             key_sum[...] = key_part
             value_sum[...] = value_part
@@ -423,30 +417,56 @@
     )(place("seq"), prefix, hot, table, cosine, sine)
 
 
-def attend_back(prefix, hot, table, cosine, sine, grad):
+def probabilities(prefix, hot, table, cosine, sine):
     groups, seqs, size, vocab = hot.shape
     heads = table.shape[2] // HEAD
     length = groups * size
     return pl.pallas_call(
-        attend_back_kernel,
+        probs_kernel,
         grid=(seqs, heads),
-        in_specs=[pl.BlockSpec(memory_space=pltpu.SMEM)]
-        + attention_specs(groups, size, vocab, table.shape[0])
-        + [pl.BlockSpec((groups, 1, size, HEAD), lambda s, h: (0, s, 0, h))],
-        out_specs=pl.BlockSpec((groups, 1, size, 3 * heads * HEAD), lambda s, h: (0, s, 0, 0)),
-        out_shape=jax.ShapeDtypeStruct((groups, seqs, size, 3 * heads * HEAD), bf16),
-        scratch_shapes=[
-            pltpu.VMEM((length, HEAD), bf16),
-            pltpu.VMEM((length, HEAD), f32),
-            pltpu.VMEM((length, HEAD), f32),
+        in_specs=attention_specs(groups, size, vocab, table.shape[0]),
+        out_specs=[
+            pl.BlockSpec((1, 1, 3, length, HEAD), lambda s, h: (s, h, 0, 0, 0)),
+            pl.BlockSpec((1, 1, groups, length, size), lambda s, h: (s, h, 0, 0, 0)),
+        ],
+        out_shape=[
+            jax.ShapeDtypeStruct((seqs, heads, 3, length, HEAD), bf16),
+            jax.ShapeDtypeStruct((seqs, heads, groups, length, size), bf16),
         ],
         compiler_params=pltpu.CompilerParams(vmem_limit_bytes=48 << 20),
         cost_estimate=pl.CostEstimate(
-            flops=10 * seqs * heads * length * length * HEAD,
-            bytes_accessed=10 * length * heads * HEAD * seqs,
+            flops=2 * seqs * heads * length * length * HEAD,
+            bytes_accessed=2 * length * length * heads * seqs,
             transcendentals=seqs * heads * length * length,
         ),
-    )(place("seq"), prefix, hot, table, cosine, sine, grad)
+    )(prefix, hot, table, cosine, sine)
+
+
+def attend_back(s, fields, probs, cosine, sine, grad):
+    groups, _, size, _ = grad.shape
+    heads = fields.shape[1]
+    length = groups * size
+    return pl.pallas_call(
+        attend_back_kernel,
+        grid=(heads,),
+        in_specs=[
+            pl.BlockSpec(memory_space=pltpu.SMEM),
+            pl.BlockSpec((1, 1, 3, length, HEAD), lambda h: (s, h, 0, 0, 0)),
+            pl.BlockSpec((1, 1, groups, length, size), lambda h: (s, h, 0, 0, 0)),
+            pl.BlockSpec((length, HEAD), lambda h: (0, 0)),
+            pl.BlockSpec((length, HEAD), lambda h: (0, 0)),
+            pl.BlockSpec((groups, 1, size, HEAD), lambda h: (0, s, 0, h)),
+        ],
+        out_specs=pl.BlockSpec((groups, size, 3 * heads * HEAD), lambda h: (0, 0, 0)),
+        out_shape=jax.ShapeDtypeStruct((groups, size, 3 * heads * HEAD), bf16),
+        scratch_shapes=[pltpu.VMEM((length, HEAD), f32), pltpu.VMEM((length, HEAD), f32)],
+        compiler_params=pltpu.CompilerParams(vmem_limit_bytes=48 << 20),
+        cost_estimate=pl.CostEstimate(
+            flops=8 * heads * length * length * HEAD,
+            bytes_accessed=2 * length * length * heads,
+            transcendentals=0,
+        ),
+    )(place("seq"), fields, probs, cosine, sine, grad)
 
 
 def on_device(
@@ -563,7 +583,14 @@
         hidden.astype(bf16), forward, lambda block: forward(0, block)
     )
     products, gate_slopes, up_slopes = zip(own_values, *values[1:])
-    branch = scatter_tokens(lambda product: dot(product, down_w, LAST), products)[0]
+    branch, _, (fields, probs) = scatter_tokens(
+        lambda product: dot(product, down_w, LAST),
+        products,
+        None,
+        lambda table: probabilities(prefix_lengths, all_hot, table, cosine, sine),
+        (),
+        (qkv_table,),
+    )
     normed, norm_two_pull = jax.vjp(layer_norm, deep_alpha * hidden + branch, gain_two, bias_two)
     activations = normed.astype(bf16)
 
@@ -634,45 +661,27 @@
     d_context = d_context.reshape(count, groups, head_cols).transpose(1, 0, 2)
     d_context = exchange(d_context, "seq").reshape(groups, seqs, local_len, head_cols)
 
-    half = width // 2
-    out_left = dot(context, d_attention[:, :half], ROWS).astype(bf16)
-    out_right = dot(context, d_attention[:, half:], ROWS).astype(bf16)
+    out_part = dot(context, d_attention, ROWS).astype(bf16)
     first_low = halves(d_first)
     lookup_first = dot(token_hot, first_low[0], ROWS) + dot(token_hot, first_low[1], ROWS)
     embed_part = head_grad + (lookup_scale * deep_alpha) * lookup_first
-    out_left = take_groups(out_left, groups, rows)
-    out_left, out_right, embed_part, d_context = together(out_left, out_right, embed_part, d_context)
-    out_right = lax.psum_scatter(out_right, "dp", scatter_dimension=0, tiled=True)
-    out_left = swap_all(out_left)
-
-    def back(s, *before):
-        grad = together(d_context[:, s : s + 1], *before)[0]
-        block = attend_back(
-            prefix_lengths[s : s + 1], all_hot[:, s : s + 1], qkv_table, cosine, sine, grad
-        )
-        return block.reshape(seq_len, 3 * head_cols)
-
-    def own_rows(mine, *before):
-        mine = together(mine, *before)[0]
-        return swap_all(take_rows(mine, groups))
-
-    gate_blocks = own_rows(gate_rows, d_first)
-    d_context, gate_blocks = together(d_context, gate_blocks)
+    d_context, out_part = together(d_context, out_part)
+    out_rows = lax.psum_scatter(out_part, "dp", scatter_dimension=0, tiled=True)
+
+    def own_rows(fields, *before):
+        fields = together(fields, *before)[0]
+        return swap_all(take_rows(fields, groups))
+
     d_qkv, input_blocks = [], []
     for s in range(seqs):
-        block = back(s, *input_blocks[-1][:1]) if s else back(s)
+        grad = together(d_context, *input_blocks[-1][:1])[0] if s else d_context
+        block = attend_back(s, fields, probs, cosine, sine, grad).reshape(seq_len, 3 * head_cols)
+        part = dot(block, qkv_w, LAST).astype(bf16).reshape(groups, local_len, width)
         if s:
-            block, input_blocks[-1] = together(block, input_blocks[-1])
-        part = dot(block, qkv_w, LAST).astype(bf16).reshape(groups, local_len, width)
-        if s == 0:
-            up_blocks = own_rows(up_rows, block)
-            part, up_blocks, out_left = together(part, up_blocks, out_left)
+            part, input_blocks[-1] = together(part, input_blocks[-1])
         block, part = together(block, part)
         d_qkv.append(block)
         input_blocks.append(swap_all(part))
-    out_left, _ = together(out_left, d_qkv[-1])
-    out_left = sum(block.astype(f32) for block in out_left).astype(bf16)
-    out_left = lax.psum_scatter(out_left, "dp", scatter_dimension=0, tiled=True)
 
     tokens_near = jnp.stack(
         [lax.dynamic_index_in_dim(tokens_all, lax.bitwise_xor(my_seq, k), 0, False) for k in range(groups)]
@@ -694,21 +703,17 @@
     norm_grads = norm_grads[0] + norm_grads[1]
 
     sums_mine = sum_dp(qkv_sums.reshape(2, chips, piece, 3 * head_cols))
-    sums_mine, input_blocks[-1] = together(sums_mine, input_blocks[-1])
+    ff_blocks = own_rows([gate_rows, up_rows, down_rows], qkv_sums)
+    sums_mine, input_blocks[-1], ff_blocks = together(sums_mine, input_blocks[-1], ff_blocks)
     input_grad = deep_alpha * d_first + jnp.concatenate(
         [sum(block.astype(f32) for block in blocks) for blocks in input_blocks]
     )
     sums_all = spread_dp(sums_mine.astype(bf16))[0].reshape(vocab, 3 * head_cols)
     qkv_rows = dot(embed_dp, sums_all, ROWS).astype(bf16)
-    qkv_grad = join_columns(own_rows(qkv_rows), 3 * width, 3)
-
-    down_blocks = own_rows(down_rows, sums_mine)
-    gate_grad = join_columns(gate_blocks, hidden_units, 1)
-    up_grad = join_columns(up_blocks, hidden_units, 1)
-    out_blocks = own_rows(out_right, qkv_grad, *down_blocks)
-    down_grad = join_columns(down_blocks, hidden_units, 1)
-    out_right = sum(block.astype(f32) for block in out_blocks)
-    out_grad = jnp.concatenate([out_left.astype(f32), out_right], axis=1)
+    (qkv_grad,) = join_columns(own_rows([qkv_rows]), 3 * width, 3, 1)
+
+    gate_grad, up_grad, down_grad = join_columns(ff_blocks, hidden_units, 1, 3)
+    out_grad = sum(block.astype(f32) for block in own_rows([out_rows], sums_mine))
 
     return (
         activations.reshape(seqs, local_len, width),

time: 836 us -> 819 us (0.980)
  matrix products: 245 us -> 257 us
  starting transfers between devices: 115 us -> 103 us
  local copies, waits for them, and re-layouts: 51.3 us -> 39.9 us
    ppermute x59 -> x50, waiting for transfers between devices: 154 us -> 119 us  [swap(): lax.ppermute(block, 'seq', [(s, s ^ bits) for s in range(lax.axis_size('s...]
    ppermute x24, waiting for transfers between devices: 64.2 us -> 78.9 us  [swap_dp(): lax.ppermute(block, 'dp', [(d, d ^ bits) for d in range(lax.axis_size('dp...]
    reduce_scatter x2 -> x1, waiting for transfers between devices: 0.02 us -> 14.5 us  [on_device(): out_rows = lax.psum_scatter(out_part, 'dp', scatter_dimension=0, tiled=True)]
    dot_general x51 -> x50, matrix products: 245 us -> 257 us  [dot(): return lax.dot_general(left, right, dims, preferred_element_type=f32)]
    all_to_all x2, waiting for transfers between devices: 1.69 us -> 10.1 us  [exchange(): return lax.all_to_all(blocks, axes, split_axis=0, concat_axis=0, tiled=True)]
    ppermute x59 -> x50, starting transfers between devices: 52.8 us -> 44.8 us  [swap(): lax.ppermute(block, 'seq', [(s, s ^ bits) for s in range(lax.axis_size('s...]
    pallas_call x8 -> x6, Pallas kernels: 53.6 us -> 58.8 us  [the longest x2 36.7 us: attend_back(): pl.pallas_call(attend_back_kernel, grid=(heads,), in_specs=[pl.BlockSpec(...]
    unnamed x289 -> x221, local copies, waits for them, and re-layouts: 17.9 us -> 13.7 us
  transfers between devices with their start and end apart: 94 -> 84, of which waited for: 42 -> 36; matrix products, arithmetic and copies ran while one was open for 36% -> 37% of each run, Pallas kernels for 11% -> 12%
where the time goes in v4:
time: 819 us; the launch traced here: 813 us
  matrix products  257 us (31%)
  waiting for transfers between devices  237 us (29%)
  starting transfers between devices  103 us (13%)
  Pallas kernels  96.9 us (12%)
  other arithmetic  62.9 us (8%)
  local copies, waits for them, and re-layouts  39.9 us (5%)
  between operations  16.4 us (2%)
    dot_general x50, matrix products, dot(): return lax.dot_general(left, right, dims, preferred_element_type=f32)  257 us
    ppermute x50, waiting for transfers between devices, swap(): lax.ppermute(block, 'seq', [(s, s ^ bits) for s in range(lax.axis_size('s...  119 us
    ppermute x24, waiting for transfers between devices, swap_dp(): lax.ppermute(block, 'dp', [(d, d ^ bits) for d in range(lax.axis_size('dp...  78.9 us
    ppermute x24, starting transfers between devices, swap_dp(): lax.ppermute(block, 'dp', [(d, d ^ bits) for d in range(lax.axis_size('dp...  47.2 us
    ppermute x50, starting transfers between devices, swap(): lax.ppermute(block, 'seq', [(s, s ^ bits) for s in range(lax.axis_size('s...  44.8 us
    pallas_call x2, Pallas kernels, attend_back(): pl.pallas_call(attend_back_kernel, grid=(heads,), in_specs=[pl.BlockSpec(...  36.7 us
    pallas_call x2, Pallas kernels, attend(): pl.pallas_call(attend_kernel, grid=(seqs, heads), in_specs=[pl.BlockSpec(...  25.3 us
    pallas_call x1, Pallas kernels, probabilities(): pl.pallas_call(probs_kernel, grid=(seqs, heads), in_specs=attention_specs...  21.8 us
  transfers between devices with their start and end apart: 84, of which 36 were waited for; matrix products, arithmetic and copies ran while one was open for 37% of the time, Pallas kernels for 12%

profile of v4, /device:TPU:9, one launch (start us, length us, event | category | flops | bytes accessed | tf_op | source)
XLA Modules:
  0.0 812.6 jit_solution(17154264549243573219)
XLA Ops:
  26.3 7.1 collective-permute-done.5
  46.8 7.1 collective-permute-done.14
  57.9 13.4 %collective-permute-done.16 = bf16[64,2048]{1,0:T(8,128)(2,1)S(1)} collective-permute-done((bf16[64,2048]{1,0:T(8,128)(2,1)S(1)}, bf16[64,2048]{1,0:T(8,128)(2,1)S(1)}, u32[]{:S(2)}, u32[]{:S(2)}) %collective-permute-start.16) | collective-permute-done | bytes 262176 | tf_op jit(solution)/shard_map/ppermute | solution.py:83
  80.0 4.6 collective-permute-done.36.refs_3_
  94.2 5.7 collective-permute-start.22
  103.2 8.2 %collective-permute-done.17 = bf16[4,64,2048]{2,1,0:T(8,128)(2,1)} collective-permute-done((bf16[4,64,2048]{2,1,0:T(8,128)(2,1)}, bf16[4,64,2048]{2,1,0:T(8,128)(2,1)}, u32[]{:S(2)}, u32[]{:S(2)}) %collective-permute-start.17) | collective-permute-done | bytes 1048608 | tf_op jit(solution)/shard_map/ppermute | solution.py:79
  117.7 12.7 %shard_map.241 = bf16[4,1,256,512]{3,2,1,0:T(8,128)(2,1)S(1)} custom-call(s32[1]{0:T(128)} %bitcast.12.place_ref.seq_ref, s32[1]{0:T(128)} %get-tuple-element.371.prefix_ref, bf16[4,1,256,128]{3,2,1,0:T(8,128)(2,1)S(1)} %get-tuple-element.334.hot_ref, bf16[256,3,512]{2,1,0:T(4,128)(2,1)S(1)} %reshape.514.table_ref, ...), custom_call_target="tpu_custom_call" | custom-call | flops 2147483648 | bytes 2097152 | tf_op jit(solution)/shard_map/pallas_call | solution.py:403
  130.5 3.9 pad_maximum_fusion.mine_ref
  134.4 8.7 %collective-permute-start.31 = (bf16[4,4,64,2048]{3,2,1,0:T(8,128)(2,1)}, bf16[4,4,64,2048]{3,2,1,0:T(8,128)(2,1)}, u32[]{:S(2)}, u32[]{:S(2)}) collective-permute-start(bf16[4,4,64,2048]{3,2,1,0:T(8,128)(2,1)} %pad_maximum_fusion.mine_ref), channel_id=1, source_target_pairs={{0,4},{4,0},{8,12},{12,8},{16,20},{20,16},{24,28},{28,24},{1,5},{5... | collective-permute-start | bytes 12582920 | tf_op jit(solution)/shard_map/ppermute | solution.py:83
  147.5 12.6 %shard_map.240 = bf16[4,1,256,512]{3,2,1,0:T(8,128)(2,1)S(1)} custom-call(s32[1]{0:T(128)} %bitcast.12.place_ref.seq_ref, s32[1]{0:T(128)} %get-tuple-element.372.prefix_ref, bf16[4,1,256,128]{3,2,1,0:T(8,128)(2,1)S(1)} %get-tuple-element.335.hot_ref, bf16[256,3,512]{2,1,0:T(4,128)(2,1)S(1)} %reshape.514.table_ref, ...), custom_call_target="tpu_custom_call" | custom-call | flops 2147483648 | bytes 2097152 | tf_op jit(solution)/shard_map/pallas_call | solution.py:403
  168.7 4.7 collective-permute-done.25.refs_3_
  173.6 7.7 shard_map.243
  181.3 4.7 fusion.129
  190.7 8.3 %fusion.132 = f32[512,1408]{1,0:T(8,128)} fusion(bf16[512,2048]{1,0:T(8,128)(2,1)} %fusion.31, bf16[2048,1408]{1,0:T(8,128)(2,1)} %all-gather.5.cloned.1.call-done), kind=kOutput, calls=%fused_computation.331 | convolution fusion | flops 2952790016 | bytes 10747904 | tf_op jit(solution)/shard_map/dot_general | solution.py:29
  199.0 13.1 %all-gather.7.cloned.1.call-done = bf16[2048,1408]{1,0:T(8,128)(2,1)} async-done(((bf16[256,1408]{1,0:T(8,128)(2,1)}), bf16[2048,1408]{1,0:T(8,128)(2,1)}) %all-gather.7.cloned.1.call-update) | async-done | bytes 5767184 | tf_op jit(solution)/shard_map/all_gather | solution.py:554
  212.1 10.8 %fusion.37 = (bf16[512,1408]{1,0:T(8,128)(2,1)}, bf16[512,1408]{1,0:T(8,128)(2,1)}, bf16[512,1408]{1,0:T(8,128)(2,1)}) fusion(f32[512,1408]{1,0:T(8,128)} %fusion.132, bf16[512,2048]{1,0:T(8,128)(2,1)} %fusion.31, bf16[2048,1408]{1,0:T(8,128)(2,1)} %all-gather.7.cloned.1.call-done), kind=kOutput, calls=%fused_computation.78 | convolution fusion | flops 2966487040 | bytes 15073280 | tf_op jit(solution)/shard_map/dot_general | solution.py:29
  222.9 10.9 %collective-permute-done.32 = bf16[512,2048]{1,0:T(8,128)(2,1)} collective-permute-done((bf16[512,2048]{1,0:T(8,128)(2,1)}, bf16[512,2048]{1,0:T(8,128)(2,1)}, u32[]{:S(2)}, u32[]{:S(2)}) %collective-permute-start.32) | collective-permute-done | bytes 2097184 | tf_op jit(solution)/shard_map/ppermute | solution.py:79
  239.1 5.2 fusion.134
  244.3 5.2 fusion.133
  249.5 7.9 fusion.49
  257.4 7.8 fusion.43
  270.7 5.1 multiply_convert_fusion.8
  275.8 6.7 convolution_convert_fusion.7
  284.2 5.4 fusion.138
  296.4 7.5 collective-permute-done.39
  309.8 21.8 %shard_map.248 = (bf16[2,4,3,1024,128]{4,3,2,1,0:T(8,128)(2,1)}, bf16[2,4,4,1024,256]{4,3,2,1,0:T(8,128)(2,1)}) custom-call(s32[2]{0:T(128)S(1)} %copy-done.15, bf16[4,2,256,128]{3,2,1,0:T(8,128)(2,1)S(1)} %get-tuple-element.370.hot_ref, bf16[256,3,512]{2,1,0:T(4,128)(2,1)S(1)} %reshape.514.table_ref, f32[1024,128]{1,0:T(8,128)S(1)} %get-tuple-element.382.cos_ref, ...), custom_call_target="tpu_custom_call" | custom-call | flops 2147483648 | bytes 16777216 | tf_op jit(solution)/shard_map/pallas_call | solution.py:424
  331.6 19.8 %collective-permute-done.41 = bf16[512,2048]{1,0:T(8,128)(2,1)} collective-permute-done((bf16[512,2048]{1,0:T(8,128)(2,1)}, bf16[512,2048]{1,0:T(8,128)(2,1)}, u32[]{:S(2)}, u32[]{:S(2)}) %collective-permute-start.41) | collective-permute-done | bytes 2097184 | tf_op jit(solution)/shard_map/ppermute | solution.py:79
  365.8 5.6 convolution_convert_fusion.1
  377.1 7.6 convolution_convert_fusion.2
  384.8 7.7 convolution_convert_fusion.3
  392.5 5.0 fusion.140
  397.5 6.7 convolution_add_fusion.2
  404.2 8.5 %collective-permute-done.43 = bf16[512,2048]{1,0:T(8,128)(2,1)S(1)} collective-permute-done((bf16[512,2048]{1,0:T(8,128)(2,1)S(1)}, bf16[512,2048]{1,0:T(8,128)(2,1)S(1)}, u32[]{:S(2)}, u32[]{:S(2)}) %collective-permute-start.43) | collective-permute-done | bytes 2097184 | tf_op jit(solution)/shard_map/ppermute | solution.py:79
  415.3 4.9 multiply_convert_fusion.2
  420.2 4.9 multiply_convert_fusion.4
  425.1 9.5 %collective-permute-done.45 = bf16[256,2048]{1,0:T(8,128)(2,1)S(1)} collective-permute-done((bf16[256,2048]{1,0:T(8,128)(2,1)S(1)}, bf16[256,2048]{1,0:T(8,128)(2,1)S(1)}, u32[]{:S(2)}, u32[]{:S(2)}) %collective-permute-start.45) | collective-permute-done | bytes 1048608 | tf_op jit(solution)/shard_map/ppermute | solution.py:79
  434.9 4.6 multiply_convert_fusion
  443.0 3.7 add_convert_fusion.3
  446.7 16.1 %add_convert_fusion.2 = bf16[2048,1408]{1,0:T(8,128)(2,1)} fusion(bf16[2048,1408]{1,0:T(8,128)(2,1)} %convolution_convert_fusion.3, bf16[512,2048]{1,0:T(8,128)(2,1)S(1)} %copy-done.44, bf16[512,2048]{1,0:T(8,128)(2,1)} %collective-permute-done.33, bf16[512,2048]{1,0:T(8,128)(2,1)} %collective-permute-done.32, bf16[512,1408]{1,0:T(8,128)(2,1)} %copy-done.87, ...), kind=kOutput, calls=%fused_computation.2 | convolution fusion | flops 8898871296 | bytes 22151168 | tf_op jit(solution)/shard_map/dot_general | solution.py:29
  465.2 6.0 fusion.143
  474.8 4.8 fusion.142
  479.6 4.8 convolution_add_fusion.1
  490.9 15.1 %add_convert_fusion = bf16[2048,1408]{1,0:T(8,128)(2,1)} fusion(bf16[2048,1408]{1,0:T(8,128)(2,1)} %convolution_convert_fusion.1, bf16[512,2048]{1,0:T(8,128)(2,1)S(1)} %copy-done.46, bf16[512,2048]{1,0:T(8,128)(2,1)S(1)} %copy-done.42, bf16[512,2048]{1,0:T(8,128)(2,1)S(1)} %copy-done.40, bf16[512,1408]{1,0:T(8,128)(2,1)S(1)} %copy-done.80, ...), kind=kOutput, calls=%fused_computation | convolution fusion | flops 8898871296 | bytes 22151168 | tf_op jit(solution)/shard_map/dot_general | solution.py:29
  506.0 15.5 %add_convert_fusion.1 = bf16[2048,1408]{1,0:T(8,128)(2,1)} fusion(bf16[2048,1408]{1,0:T(8,128)(2,1)} %convolution_convert_fusion.2, bf16[512,2048]{1,0:T(8,128)(2,1)} %copy-done.43, bf16[512,2048]{1,0:T(8,128)(2,1)} %collective-permute-done.33, bf16[512,2048]{1,0:T(8,128)(2,1)} %collective-permute-done.32, bf16[512,1408]{1,0:T(8,128)(2,1)} %copy-done.83, ...), kind=kOutput, calls=%fused_computation.1 | convolution fusion | flops 8898871296 | bytes 22151168 | tf_op jit(solution)/shard_map/dot_general | solution.py:29
  521.6 5.8 collective-permute-done.49
  528.2 7.9 multiply_reduce_fusion.1
  537.3 9.9 %convolution_convert_fusion.6 = bf16[512,2048]{1,0:T(8,128)(2,1)S(1)} fusion(bf16[2048,2048]{1,0:T(8,128)(2,1)} %bitcast.296, f32[512,2048]{1,0:T(8,128)S(1)} %get-tuple-element.265, f32[512]{0:T(512)S(1)} %negate_multiply_fusion), kind=kOutput, calls=%fused_computation.71 | convolution fusion | flops 4298113024 | bytes 14682112 | tf_op jit(solution)/shard_map/dot_general | solution.py:29
  552.4 10.9 %convolution_convert_fusion = bf16[2048,2048]{1,0:T(8,128)(2,1)} fusion(bf16[512,2048]{1,0:T(8,128)(2,1)} %copy-done.5, f32[512,2048]{1,0:T(8,128)} %copy-done.19, f32[512]{0:T(512)S(1)} %negate_multiply_fusion), kind=kOutput, calls=%fused_computation.3 | convolution fusion | flops 4301258752 | bytes 14682112 | tf_op jit(solution)/shard_map/dot_general | solution.py:29
  563.3 10.1 %all-to-all-done = bf16[4,512,512]{2,1,0:T(8,128)(2,1)S(1)} async-done(((bf16[4,512,512]{2,1,0:T(8,128)(2,1)}), bf16[4,512,512]{2,1,0:T(8,128)(2,1)S(1)}, u32[]{:S(2)}, u32[]{:S(2)}) %all-to-all-start) | async-done | bytes 2097184 | tf_op jit(solution)/shard_map/all_to_all | solution.py:70
  580.8 18.7 %shard_map.249 = bf16[4,256,1536]{2,1,0:T(8,128)(2,1)} custom-call(s32[1]{0:T(128)} %bitcast.12.place_ref.seq_ref, bf16[2,4,3,1024,128]{4,3,2,1,0:T(8,128)(2,1)} %get-tuple-element.221.field_ref, bf16[2,4,4,1024,256]{4,3,2,1,0:T(8,128)(2,1)} %get-tuple-element.222.probs_ref, f32[1024,128]{1,0:T(8,128)S(1)} %copy-done.2, f32[1024,128]{1,0:T(8,128)S(1)} %copy-done.4, ...), custom_call_target="tpu_custom_call" | custom-call | flops 4294967296 | bytes 8388608 | tf_op jit(solution)/shard_map/pallas_call | solution.py:449
  599.5 8.4 %convolution_convert_fusion.5 = bf16[1024,2048]{1,0:T(8,128)(2,1)S(1)} fusion(bf16[1024,1536]{1,0:T(8,128)(2,1)} %bitcast.300, bf16[2048,1536]{1,0:T(8,128)(2,1)S(1)} %bitcast.352), kind=kOutput, calls=%fused_computation.65 | convolution fusion | flops 6444548096 | bytes 13631488 | tf_op jit(solution)/shard_map/dot_general | solution.py:29
  612.1 18.0 %shard_map.250 = bf16[4,256,1536]{2,1,0:T(8,128)(2,1)} custom-call(s32[1]{0:T(128)} %bitcast.12.place_ref.seq_ref, bf16[2,4,3,1024,128]{4,3,2,1,0:T(8,128)(2,1)} %get-tuple-element.221.field_ref, bf16[2,4,4,1024,256]{4,3,2,1,0:T(8,128)(2,1)} %get-tuple-element.222.probs_ref, f32[1024,128]{1,0:T(8,128)S(1)} %copy-done.2, f32[1024,128]{1,0:T(8,128)S(1)} %copy-done.4, ...), custom_call_target="tpu_custom_call" | custom-call | flops 4294967296 | bytes 8388608 | tf_op jit(solution)/shard_map/pallas_call | solution.py:449
  630.1 10.2 %convolution_convert_fusion.4 = bf16[1024,2048]{1,0:T(8,128)(2,1)S(1)} fusion(bf16[1024,1536]{1,0:T(8,128)(2,1)} %bitcast.298, bf16[2048,1536]{1,0:T(8,128)(2,1)} %all-gather.11.cloned.1.call-done), kind=kOutput, calls=%fused_computation.64 | convolution fusion | flops 6444548096 | bytes 13631488 | tf_op jit(solution)/shard_map/dot_general | solution.py:29
  640.9 9.9 %collective-permute-done.53 = bf16[256,2048]{1,0:T(8,128)(2,1)S(1)} collective-permute-done((bf16[256,2048]{1,0:T(8,128)(2,1)S(1)}, bf16[256,2048]{1,0:T(8,128)(2,1)S(1)}, u32[]{:S(2)}, u32[]{:S(2)}) %collective-permute-start.53) | collective-permute-done | bytes 1048608 | tf_op jit(solution)/shard_map/ppermute | solution.py:79
  658.2 7.1 collective-permute-start.54
  670.9 6.6 all-to-all-start.1
  678.8 3.9 convert_add_fusion.1
  688.5 28.2 %collective-permute-done.55 = f32[16,1536]{1,0:T(8,128)S(1)} collective-permute-done((f32[16,1536]{1,0:T(8,128)S(1)}, f32[16,1536]{1,0:T(8,128)S(1)}, u32[]{:S(2)}, u32[]{:S(2)}) %collective-permute-start.55) | collective-permute-done | bytes 98336 | tf_op jit(solution)/shard_map/ppermute | solution.py:83
  720.4 4.2 collective-permute-done.56
  725.6 8.4 %collective-permute-done.57 = f32[16,1536]{1,0:T(8,128)S(1)} collective-permute-done((f32[16,1536]{1,0:T(8,128)S(1)}, f32[16,1536]{1,0:T(8,128)S(1)}, u32[]{:S(2)}, u32[]{:S(2)}) %collective-permute-start.57) | collective-permute-done | bytes 98336 | tf_op jit(solution)/shard_map/ppermute | solution.py:83
  737.6 21.3 %collective-permute-done.62.refs_2_ = bf16[64,4224]{1,0:T(8,128)(2,1)S(1)} collective-permute-done((bf16[64,4224]{1,0:T(8,128)(2,1)}, bf16[64,4224]{1,0:T(8,128)(2,1)S(1)}, u32[]{:S(2)}, u32[]{:S(2)}) %collective-permute-start.62) | collective-permute-done | bytes 540704 | tf_op jit(solution)/shard_map/ppermute | solution.py:79
  769.2 4.3 convert_add_fusion
  776.8 14.5 %reduce-scatter.11.cloned.1.call-done.refs_0_ = bf16[256,2048]{1,0:T(8,128)(2,1)} async-done(((bf16[2048,2048]{1,0:T(8,128)(2,1)}), bf16[256,2048]{1,0:T(8,128)(2,1)}) %reduce-scatter.11.cloned.1.call-update) | async-done | bytes 1048592 | tf_op jit(solution)/shard_map/reduce_scatter | solution.py:669
  795.4 5.4 maximum_add_fusion
  (543 shorter events, 215.1 us)
Async XLA Ops:
  7.2 183.5 %all-gather.5.cloned.1.call-start = ((), (), s32[]{:S(2)}) async-start(), calls=%async_computation.6 | async-start | bytes 6488064 | tf_op jit(solution)/shard_map/all_gather | solution.py:554
  16.7 19.0 %collective-permute-start.7 = (bf16[64,1536]{1,0:T(8,128)(2,1)}, bf16[64,1536]{1,0:T(8,128)(2,1)S(1)}, u32[]{:S(2)}, u32[]{:S(2)}) collective-permute-start(bf16[64,1536]{1,0:T(8,128)(2,1)} %get-tuple-element.332), channel_id=1, source_target_pairs={{0,1},{1,0},{2,3},{3,2},{4,5},{5,4},{6,7},{7,6},{8,9},{9,8},{10,11... | collective-permute-start | bytes 589832 | tf_op jit(solution)/shard_map/ppermute | solution.py:79
  17.9 17.8 %collective-permute-start.8 = (bf16[64,1536]{1,0:T(8,128)(2,1)}, bf16[64,1536]{1,0:T(8,128)(2,1)S(1)}, u32[]{:S(2)}, u32[]{:S(2)}) collective-permute-start(bf16[64,1536]{1,0:T(8,128)(2,1)} %get-tuple-element.331), channel_id=1, source_target_pairs={{0,2},{1,3},{2,0},{3,1},{4,6},{5,7},{6,4},{7,5},{8,10},{9,11},{10,... | collective-permute-start | bytes 589832 | tf_op jit(solution)/shard_map/ppermute | solution.py:79
  22.2 11.1 %collective-permute-start.5 = (bf16[4,5,2048]{2,1,0:T(8,128)(2,1)S(1)}, bf16[4,5,2048]{2,1,0:T(8,128)(2,1)S(1)}, u32[]{:S(2)}, u32[]{:S(2)}) collective-permute-start(bf16[4,5,2048]{2,1,0:T(8,128)(2,1)S(1)} %get-tuple-element.349), channel_id=1, source_target_pairs={{0,24},{4,28},{8,16},{12,20},{16,8},{20,12},{24,0},{28,4},{1,25},{... | collective-permute-start | bytes 245768 | tf_op jit(solution)/shard_map/ppermute | solution.py:83
  23.8 12.0 %collective-permute-start.9 = (bf16[64,1536]{1,0:T(8,128)(2,1)}, bf16[64,1536]{1,0:T(8,128)(2,1)S(1)}, u32[]{:S(2)}, u32[]{:S(2)}) collective-permute-start(bf16[64,1536]{1,0:T(8,128)(2,1)} %get-tuple-element.330), channel_id=1, source_target_pairs={{0,3},{1,2},{2,1},{3,0},{4,7},{5,6},{6,5},{7,4},{8,11},{9,10},{10,... | collective-permute-start | bytes 589832 | tf_op jit(solution)/shard_map/ppermute | solution.py:79
  43.3 36.5 %collective-permute-start.34 = (bf16[64,4224]{1,0:T(8,128)(2,1)S(1)}, bf16[64,4224]{1,0:T(8,128)(2,1)S(1)}, u32[]{:S(2)}, u32[]{:S(2)}) collective-permute-start(bf16[64,4224]{1,0:T(8,128)(2,1)S(1)} %get-tuple-element.305), channel_id=1, source_target_pairs={{0,1},{1,0},{2,3},{3,2},{4,5},{5,4},{6,7},{7,6},{8,9},{9,8},{10,11... | collective-permute-start | bytes 1622024 | tf_op jit(solution)/shard_map/ppermute | solution.py:79
  43.6 36.4 %collective-permute-start.35 = (bf16[64,4224]{1,0:T(8,128)(2,1)S(1)}, bf16[64,4224]{1,0:T(8,128)(2,1)S(1)}, u32[]{:S(2)}, u32[]{:S(2)}) collective-permute-start(bf16[64,4224]{1,0:T(8,128)(2,1)S(1)} %get-tuple-element.304), channel_id=1, source_target_pairs={{0,2},{1,3},{2,0},{3,1},{4,6},{5,7},{6,4},{7,5},{8,10},{9,11},{10,... | collective-permute-start | bytes 1622024 | tf_op jit(solution)/shard_map/ppermute | solution.py:79
  44.1 13.8 %collective-permute-start.15 = (bf16[64,2048]{1,0:T(8,128)(2,1)S(1)}, bf16[64,2048]{1,0:T(8,128)(2,1)S(1)}, u32[]{:S(2)}, u32[]{:S(2)}) collective-permute-start(bf16[64,2048]{1,0:T(8,128)(2,1)S(1)} %copy-done.49), channel_id=1, source_target_pairs={{0,16},{4,20},{8,24},{12,28},{16,0},{20,4},{24,8},{28,12},{1,17},{... | collective-permute-start | bytes 786440 | tf_op jit(solution)/shard_map/ppermute | solution.py:83
  46.5 24.7 %collective-permute-start.16 = (bf16[64,2048]{1,0:T(8,128)(2,1)S(1)}, bf16[64,2048]{1,0:T(8,128)(2,1)S(1)}, u32[]{:S(2)}, u32[]{:S(2)}) collective-permute-start(bf16[64,2048]{1,0:T(8,128)(2,1)S(1)} %copy-done.49), channel_id=1, source_target_pairs={{0,24},{4,28},{8,16},{12,20},{16,8},{20,12},{24,0},{28,4},{1,25},{... | collective-permute-start | bytes 786440 | tf_op jit(solution)/shard_map/ppermute | solution.py:83
  54.0 20.7 %collective-permute-start.11 = (f32[16,1536]{1,0:T(8,128)S(1)}, f32[16,1536]{1,0:T(8,128)S(1)}, u32[]{:S(2)}, u32[]{:S(2)}) collective-permute-start(f32[16,1536]{1,0:T(8,128)S(1)} %get-tuple-element.343), channel_id=1, source_target_pairs={{0,8},{4,12},{8,0},{12,4},{16,24},{20,28},{24,16},{28,20},{1,9},{5... | collective-permute-start | bytes 294920 | tf_op jit(solution)/shard_map/ppermute | solution.py:83
  57.9 18.7 %collective-permute-start.12 = (f32[16,1536]{1,0:T(8,128)S(1)}, f32[16,1536]{1,0:T(8,128)S(1)}, u32[]{:S(2)}, u32[]{:S(2)}) collective-permute-start(f32[16,1536]{1,0:T(8,128)S(1)} %get-tuple-element.341), channel_id=1, source_target_pairs={{0,16},{4,20},{8,24},{12,28},{16,0},{20,4},{24,8},{28,12},{1,17},{... | collective-permute-start | bytes 294920 | tf_op jit(solution)/shard_map/ppermute | solution.py:83
  74.6 10.0 %collective-permute-start.36 = (bf16[64,4224]{1,0:T(8,128)(2,1)S(1)}, bf16[64,4224]{1,0:T(8,128)(2,1)S(1)}, u32[]{:S(2)}, u32[]{:S(2)}) collective-permute-start(bf16[64,4224]{1,0:T(8,128)(2,1)S(1)} %get-tuple-element.303), channel_id=1, source_target_pairs={{0,3},{1,2},{2,1},{3,0},{4,7},{5,6},{6,5},{7,4},{8,11},{9,10},{10,... | collective-permute-start | bytes 1622024 | tf_op jit(solution)/shard_map/ppermute | solution.py:79
  87.8 124.3 %all-gather.7.cloned.1.call-start = ((), (), s32[]{:S(2)}) async-start(), calls=%async_computation.7 | async-start | bytes 6488064 | tf_op jit(solution)/shard_map/all_gather | solution.py:554
  88.6 187.2 %all-gather.9.cloned.1.call-start = ((), (), s32[]{:S(2)}) async-start(), calls=%async_computation.8 | async-start | bytes 6488064 | tf_op jit(solution)/shard_map/all_gather | solution.py:554
  89.3 273.8 %all-gather.11.cloned.1.call-start = ((), (), s32[]{:S(2)}) async-start(), calls=%async_computation.9 | async-start | bytes 7077888 | tf_op jit(solution)/shard_map/all_gather | solution.py:554
  91.8 19.6 %collective-permute-start.17 = (bf16[4,64,2048]{2,1,0:T(8,128)(2,1)}, bf16[4,64,2048]{2,1,0:T(8,128)(2,1)}, u32[]{:S(2)}, u32[]{:S(2)}) collective-permute-start(bf16[4,64,2048]{2,1,0:T(8,128)(2,1)} %pad_maximum_fusion.7), channel_id=1, source_target_pairs={{0,1},{1,0},{2,3},{3,2},{4,5},{5,4},{6,7},{7,6},{8,9},{9,8},{10,11... | collective-permute-start | bytes 3145736 | tf_op jit(solution)/shard_map/ppermute | solution.py:79
  92.9 19.6 %collective-permute-start.18 = (bf16[4,64,2048]{2,1,0:T(8,128)(2,1)}, bf16[4,64,2048]{2,1,0:T(8,128)(2,1)}, u32[]{:S(2)}, u32[]{:S(2)}) collective-permute-start(bf16[4,64,2048]{2,1,0:T(8,128)(2,1)} %pad_maximum_fusion.7), channel_id=1, source_target_pairs={{0,2},{1,3},{2,0},{3,1},{4,6},{5,7},{6,4},{7,5},{8,10},{9,11},{10,... | collective-permute-start | bytes 3145736 | tf_op jit(solution)/shard_map/ppermute | solution.py:79
  113.5 16.8 %collective-permute-start.29 = (bf16[2,64,2048]{2,1,0:T(8,128)(2,1)S(1)}, bf16[2,64,2048]{2,1,0:T(8,128)(2,1)S(1)}, u32[]{:S(2)}, u32[]{:S(2)}) collective-permute-start(bf16[2,64,2048]{2,1,0:T(8,128)(2,1)S(1)} %slice.331), channel_id=1, source_target_pairs={{0,2},{1,3},{2,0},{3,1},{4,6},{5,7},{6,4},{7,5},{8,10},{9,11},{10,... | collective-permute-start | bytes 1572872 | tf_op jit(solution)/shard_map/ppermute | solution.py:79
  116.0 14.4 %collective-permute-start.30 = (bf16[2,64,2048]{2,1,0:T(8,128)(2,1)S(1)}, bf16[2,64,2048]{2,1,0:T(8,128)(2,1)S(1)}, u32[]{:S(2)}, u32[]{:S(2)}) collective-permute-start(bf16[2,64,2048]{2,1,0:T(8,128)(2,1)S(1)} %slice.332), channel_id=1, source_target_pairs={{0,1},{1,0},{2,3},{3,2},{4,5},{5,4},{6,7},{7,6},{8,9},{9,8},{10,11... | collective-permute-start | bytes 1572872 | tf_op jit(solution)/shard_map/ppermute | solution.py:79
  134.4 39.2 %collective-permute-start.31 = (bf16[4,4,64,2048]{3,2,1,0:T(8,128)(2,1)}, bf16[4,4,64,2048]{3,2,1,0:T(8,128)(2,1)}, u32[]{:S(2)}, u32[]{:S(2)}) collective-permute-start(bf16[4,4,64,2048]{3,2,1,0:T(8,128)(2,1)} %pad_maximum_fusion.mine_ref), channel_id=1, source_target_pairs={{0,4},{4,0},{8,12},{12,8},{16,20},{20,16},{24,28},{28,24},{1,5},{5... | collective-permute-start | bytes 12582920 | tf_op jit(solution)/shard_map/ppermute | solution.py:83
  144.8 16.7 %collective-permute-start.26 = (bf16[256,512]{1,0:T(8,128)(2,1)S(1)}, bf16[256,512]{1,0:T(8,128)(2,1)S(1)}, u32[]{:S(2)}, u32[]{:S(2)}) collective-permute-start(bf16[256,512]{1,0:T(8,128)(2,1)S(1)} %get-tuple-element.316), channel_id=1, source_target_pairs={{0,1},{1,0},{2,3},{3,2},{4,5},{5,4},{6,7},{7,6},{8,9},{9,8},{10,11... | collective-permute-start | bytes 786440 | tf_op jit(solution)/shard_map/ppermute | solution.py:79
  146.1 15.7 %collective-permute-start.27 = (bf16[256,512]{1,0:T(8,128)(2,1)S(1)}, bf16[256,512]{1,0:T(8,128)(2,1)S(1)}, u32[]{:S(2)}, u32[]{:S(2)}) collective-permute-start(bf16[256,512]{1,0:T(8,128)(2,1)S(1)} %get-tuple-element.315), channel_id=1, source_target_pairs={{0,2},{1,3},{2,0},{3,1},{4,6},{5,7},{6,4},{7,5},{8,10},{9,11},{10,... | collective-permute-start | bytes 786440 | tf_op jit(solution)/shard_map/ppermute | solution.py:79
  146.4 17.4 %collective-permute-start.28 = (bf16[256,512]{1,0:T(8,128)(2,1)S(1)}, bf16[256,512]{1,0:T(8,128)(2,1)S(1)}, u32[]{:S(2)}, u32[]{:S(2)}) collective-permute-start(bf16[256,512]{1,0:T(8,128)(2,1)S(1)} %get-tuple-element.314), channel_id=1, source_target_pairs={{0,3},{1,2},{2,1},{3,0},{4,7},{5,6},{6,5},{7,4},{8,11},{9,10},{10,... | collective-permute-start | bytes 786440 | tf_op jit(solution)/shard_map/ppermute | solution.py:79
  161.8 11.6 %collective-permute-start.25 = (bf16[256,512]{1,0:T(8,128)(2,1)S(1)}, bf16[256,512]{1,0:T(8,128)(2,1)S(1)}, u32[]{:S(2)}, u32[]{:S(2)}) collective-permute-start(bf16[256,512]{1,0:T(8,128)(2,1)S(1)} %get-tuple-element.318), channel_id=1, source_target_pairs={{0,3},{1,2},{2,1},{3,0},{4,7},{5,6},{6,5},{7,4},{8,11},{9,10},{10,... | collective-permute-start | bytes 786440 | tf_op jit(solution)/shard_map/ppermute | solution.py:79
  188.8 45.1 %collective-permute-start.32 = (bf16[512,2048]{1,0:T(8,128)(2,1)}, bf16[512,2048]{1,0:T(8,128)(2,1)}, u32[]{:S(2)}, u32[]{:S(2)}) collective-permute-start(bf16[512,2048]{1,0:T(8,128)(2,1)} %fusion.31), channel_id=1, source_target_pairs={{0,1},{1,0},{2,3},{3,2},{4,5},{5,4},{6,7},{7,6},{8,9},{9,8},{10,11... | collective-permute-start | bytes 6291464 | tf_op jit(solution)/shard_map/ppermute | solution.py:79
  189.5 45.2 %collective-permute-start.33 = (bf16[512,2048]{1,0:T(8,128)(2,1)}, bf16[512,2048]{1,0:T(8,128)(2,1)}, u32[]{:S(2)}, u32[]{:S(2)}) collective-permute-start(bf16[512,2048]{1,0:T(8,128)(2,1)} %fusion.31), channel_id=1, source_target_pairs={{0,2},{1,3},{2,0},{3,1},{4,6},{5,7},{6,4},{7,5},{8,10},{9,11},{10,... | collective-permute-start | bytes 6291464 | tf_op jit(solution)/shard_map/ppermute | solution.py:79
  190.6 494.4 %reduce-scatter.5.cloned.1.call-start = ((), (), s32[]{:S(2)}) async-start(), calls=%async_computation.10 | async-start | bytes 6488064 | tf_op jit(solution)/shard_map/reduce_scatter | solution.py:654
  236.0 29.2 %collective-permute-start.37 = (bf16[256,2048]{1,0:T(8,128)(2,1)S(1)}, bf16[256,2048]{1,0:T(8,128)(2,1)S(1)}, u32[]{:S(2)}, u32[]{:S(2)}) collective-permute-start(bf16[256,2048]{1,0:T(8,128)(2,1)S(1)} %slice.342), channel_id=1, source_target_pairs={{0,2},{1,3},{2,0},{3,1},{4,6},{5,7},{6,4},{7,5},{8,10},{9,11},{10,... | collective-permute-start | bytes 3145736 | tf_op jit(solution)/shard_map/ppermute | solution.py:79
  238.7 26.6 %collective-permute-start.38 = (bf16[256,2048]{1,0:T(8,128)(2,1)S(1)}, bf16[256,2048]{1,0:T(8,128)(2,1)S(1)}, u32[]{:S(2)}, u32[]{:S(2)}) collective-permute-start(bf16[256,2048]{1,0:T(8,128)(2,1)S(1)} %slice.343), channel_id=1, source_target_pairs={{0,1},{1,0},{2,3},{3,2},{4,5},{5,4},{6,7},{7,6},{8,9},{9,8},{10,11... | collective-permute-start | bytes 3145736 | tf_op jit(solution)/shard_map/ppermute | solution.py:79
  282.7 21.2 %collective-permute-start.39 = (bf16[256,2048]{1,0:T(8,128)(2,1)S(1)}, bf16[256,2048]{1,0:T(8,128)(2,1)S(1)}, u32[]{:S(2)}, u32[]{:S(2)}) collective-permute-start(bf16[256,2048]{1,0:T(8,128)(2,1)S(1)} %get-tuple-element.310), channel_id=1, source_target_pairs={{0,1},{1,0},{2,3},{3,2},{4,5},{5,4},{6,7},{7,6},{8,9},{9,8},{10,11... | collective-permute-start | bytes 3145736 | tf_op jit(solution)/shard_map/ppermute | solution.py:79
  283.9 20.8 %collective-permute-start.40 = (bf16[256,2048]{1,0:T(8,128)(2,1)S(1)}, bf16[256,2048]{1,0:T(8,128)(2,1)S(1)}, u32[]{:S(2)}, u32[]{:S(2)}) collective-permute-start(bf16[256,2048]{1,0:T(8,128)(2,1)S(1)} %get-tuple-element.309), channel_id=1, source_target_pairs={{0,2},{1,3},{2,0},{3,1},{4,6},{5,7},{6,4},{7,5},{8,10},{9,11},{10,... | collective-permute-start | bytes 3145736 | tf_op jit(solution)/shard_map/ppermute | solution.py:79
  308.8 42.7 %collective-permute-start.41 = (bf16[512,2048]{1,0:T(8,128)(2,1)}, bf16[512,2048]{1,0:T(8,128)(2,1)}, u32[]{:S(2)}, u32[]{:S(2)}) collective-permute-start(bf16[512,2048]{1,0:T(8,128)(2,1)} %pad_maximum_fusion.3), channel_id=1, source_target_pairs={{0,2},{1,3},{2,0},{3,1},{4,6},{5,7},{6,4},{7,5},{8,10},{9,11},{10,... | collective-permute-start | bytes 6291464 | tf_op jit(solution)/shard_map/ppermute | solution.py:79
  309.0 42.5 %collective-permute-start.42 = (bf16[512,2048]{1,0:T(8,128)(2,1)}, bf16[512,2048]{1,0:T(8,128)(2,1)}, u32[]{:S(2)}, u32[]{:S(2)}) collective-permute-start(bf16[512,2048]{1,0:T(8,128)(2,1)} %pad_maximum_fusion.2), channel_id=1, source_target_pairs={{0,1},{1,0},{2,3},{3,2},{4,5},{5,4},{6,7},{7,6},{8,9},{9,8},{10,11... | collective-permute-start | bytes 6291464 | tf_op jit(solution)/shard_map/ppermute | solution.py:79
  371.4 41.3 %collective-permute-start.43 = (bf16[512,2048]{1,0:T(8,128)(2,1)S(1)}, bf16[512,2048]{1,0:T(8,128)(2,1)S(1)}, u32[]{:S(2)}, u32[]{:S(2)}) collective-permute-start(bf16[512,2048]{1,0:T(8,128)(2,1)S(1)} %convert_element_type.343), channel_id=1, source_target_pairs={{0,1},{1,0},{2,3},{3,2},{4,5},{5,4},{6,7},{7,6},{8,9},{9,8},{10,11... | collective-permute-start | bytes 6291464 | tf_op jit(solution)/shard_map/ppermute | solution.py:79
  371.9 41.1 %collective-permute-start.44 = (bf16[512,2048]{1,0:T(8,128)(2,1)S(1)}, bf16[512,2048]{1,0:T(8,128)(2,1)S(1)}, u32[]{:S(2)}, u32[]{:S(2)}) collective-permute-start(bf16[512,2048]{1,0:T(8,128)(2,1)S(1)} %convert_element_type.343), channel_id=1, source_target_pairs={{0,2},{1,3},{2,0},{3,1},{4,6},{5,7},{6,4},{7,5},{8,10},{9,11},{10,... | collective-permute-start | bytes 6291464 | tf_op jit(solution)/shard_map/ppermute | solution.py:79
  413.1 21.5 %collective-permute-start.45 = (bf16[256,2048]{1,0:T(8,128)(2,1)S(1)}, bf16[256,2048]{1,0:T(8,128)(2,1)S(1)}, u32[]{:S(2)}, u32[]{:S(2)}) collective-permute-start(bf16[256,2048]{1,0:T(8,128)(2,1)S(1)} %slice.353), channel_id=1, source_target_pairs={{0,2},{1,3},{2,0},{3,1},{4,6},{5,7},{6,4},{7,5},{8,10},{9,11},{10,... | collective-permute-start | bytes 3145736 | tf_op jit(solution)/shard_map/ppermute | solution.py:79
  414.3 20.3 %collective-permute-start.46 = (bf16[256,2048]{1,0:T(8,128)(2,1)S(1)}, bf16[256,2048]{1,0:T(8,128)(2,1)S(1)}, u32[]{:S(2)}, u32[]{:S(2)}) collective-permute-start(bf16[256,2048]{1,0:T(8,128)(2,1)S(1)} %slice.354), channel_id=1, source_target_pairs={{0,1},{1,0},{2,3},{3,2},{4,5},{5,4},{6,7},{7,6},{8,9},{9,8},{10,11... | collective-permute-start | bytes 3145736 | tf_op jit(solution)/shard_map/ppermute | solution.py:79
  462.9 222.1 %reduce-scatter.7.cloned.1.call-start = ((), (), s32[]{:S(2)}) async-start(), calls=%async_computation.11 | async-start | bytes 6488064 | tf_op jit(solution)/shard_map/reduce_scatter | solution.py:654
  463.2 21.2 %collective-permute-start.47 = (bf16[256,2048]{1,0:T(8,128)(2,1)S(1)}, bf16[256,2048]{1,0:T(8,128)(2,1)S(1)}, u32[]{:S(2)}, u32[]{:S(2)}) collective-permute-start(bf16[256,2048]{1,0:T(8,128)(2,1)S(1)} %get-tuple-element.308), channel_id=1, source_target_pairs={{0,1},{1,0},{2,3},{3,2},{4,5},{5,4},{6,7},{7,6},{8,9},{9,8},{10,11... | collective-permute-start | bytes 3145736 | tf_op jit(solution)/shard_map/ppermute | solution.py:79
  464.1 20.3 %collective-permute-start.48 = (bf16[256,2048]{1,0:T(8,128)(2,1)S(1)}, bf16[256,2048]{1,0:T(8,128)(2,1)S(1)}, u32[]{:S(2)}, u32[]{:S(2)}) collective-permute-start(bf16[256,2048]{1,0:T(8,128)(2,1)S(1)} %get-tuple-element.307), channel_id=1, source_target_pairs={{0,2},{1,3},{2,0},{3,1},{4,6},{5,7},{6,4},{7,5},{8,10},{9,11},{10,... | collective-permute-start | bytes 3145736 | tf_op jit(solution)/shard_map/ppermute | solution.py:79
  488.6 38.8 %collective-permute-start.49 = (bf16[512,2048]{1,0:T(8,128)(2,1)}, bf16[512,2048]{1,0:T(8,128)(2,1)S(1)}, u32[]{:S(2)}, u32[]{:S(2)}) collective-permute-start(bf16[512,2048]{1,0:T(8,128)(2,1)} %pad_maximum_fusion.5), channel_id=1, source_target_pairs={{0,2},{1,3},{2,0},{3,1},{4,6},{5,7},{6,4},{7,5},{8,10},{9,11},{10,... | collective-permute-start | bytes 6291464 | tf_op jit(solution)/shard_map/ppermute | solution.py:79
  488.6 38.8 %collective-permute-start.50 = (bf16[512,2048]{1,0:T(8,128)(2,1)}, bf16[512,2048]{1,0:T(8,128)(2,1)}, u32[]{:S(2)}, u32[]{:S(2)}) collective-permute-start(bf16[512,2048]{1,0:T(8,128)(2,1)} %pad_maximum_fusion.4), channel_id=1, source_target_pairs={{0,1},{1,0},{2,3},{3,2},{4,5},{5,4},{6,7},{7,6},{8,9},{9,8},{10,11... | collective-permute-start | bytes 6291464 | tf_op jit(solution)/shard_map/ppermute | solution.py:79
  527.4 157.5 %reduce-scatter.9.cloned.1.call-start = ((), (), s32[]{:S(2)}) async-start(), calls=%async_computation.12 | async-start | bytes 6488064 | tf_op jit(solution)/shard_map/reduce_scatter | solution.py:654
  548.7 24.6 %all-to-all-start = ((bf16[4,512,512]{2,1,0:T(8,128)(2,1)}), bf16[4,512,512]{2,1,0:T(8,128)(2,1)S(1)}, u32[]{:S(2)}, u32[]{:S(2)}) async-start(bf16[4,512,512]{2,1,0:T(8,128)(2,1)} %bitcast.302), calls=%async_computation | async-start | bytes 4194304 | tf_op jit(solution)/shard_map/all_to_all | solution.py:70
  552.4 239.0 %reduce-scatter.11.cloned.1.call-start = ((), (), s32[]{:S(2)}) async-start(), calls=%async_computation.13 | async-start | bytes 9437184 | tf_op jit(solution)/shard_map/reduce_scatter | solution.py:669
  609.4 31.5 %collective-permute-start.51 = (bf16[256,2048]{1,0:T(8,128)(2,1)S(1)}, bf16[256,2048]{1,0:T(8,128)(2,1)S(1)}, u32[]{:S(2)}, u32[]{:S(2)}) collective-permute-start(bf16[256,2048]{1,0:T(8,128)(2,1)S(1)} %get-tuple-element.285), channel_id=1, source_target_pairs={{0,1},{1,0},{2,3},{3,2},{4,5},{5,4},{6,7},{7,6},{8,9},{9,8},{10,11... | collective-permute-start | bytes 3145736 | tf_op jit(solution)/shard_map/ppermute | solution.py:79
  609.4 31.5 %collective-permute-start.52 = (bf16[256,2048]{1,0:T(8,128)(2,1)S(1)}, bf16[256,2048]{1,0:T(8,128)(2,1)S(1)}, u32[]{:S(2)}, u32[]{:S(2)}) collective-permute-start(bf16[256,2048]{1,0:T(8,128)(2,1)S(1)} %get-tuple-element.284), channel_id=1, source_target_pairs={{0,2},{1,3},{2,0},{3,1},{4,6},{5,7},{6,4},{7,5},{8,10},{9,11},{10,... | collective-permute-start | bytes 3145736 | tf_op jit(solution)/shard_map/ppermute | solution.py:79
  609.7 41.1 %collective-permute-start.53 = (bf16[256,2048]{1,0:T(8,128)(2,1)S(1)}, bf16[256,2048]{1,0:T(8,128)(2,1)S(1)}, u32[]{:S(2)}, u32[]{:S(2)}) collective-permute-start(bf16[256,2048]{1,0:T(8,128)(2,1)S(1)} %get-tuple-element.283), channel_id=1, source_target_pairs={{0,3},{1,2},{2,1},{3,0},{4,7},{5,6},{6,5},{7,4},{8,11},{9,10},{10,... | collective-permute-start | bytes 3145736 | tf_op jit(solution)/shard_map/ppermute | solution.py:79
  653.4 81.8 %collective-permute-start.58 = (bf16[256,2048]{1,0:T(8,128)(2,1)}, bf16[256,2048]{1,0:T(8,128)(2,1)}, u32[]{:S(2)}, u32[]{:S(2)}) collective-permute-start(bf16[256,2048]{1,0:T(8,128)(2,1)} %get-tuple-element.281), channel_id=1, source_target_pairs={{0,1},{1,0},{2,3},{3,2},{4,5},{5,4},{6,7},{7,6},{8,9},{9,8},{10,11... | collective-permute-start | bytes 3145736 | tf_op jit(solution)/shard_map/ppermute | solution.py:79
  653.6 83.9 %collective-permute-start.59 = (bf16[256,2048]{1,0:T(8,128)(2,1)}, bf16[256,2048]{1,0:T(8,128)(2,1)}, u32[]{:S(2)}, u32[]{:S(2)}) collective-permute-start(bf16[256,2048]{1,0:T(8,128)(2,1)} %get-tuple-element.280), channel_id=1, source_target_pairs={{0,2},{1,3},{2,0},{3,1},{4,6},{5,7},{6,4},{7,5},{8,10},{9,11},{10,... | collective-permute-start | bytes 3145736 | tf_op jit(solution)/shard_map/ppermute | solution.py:79
  655.5 82.0 %collective-permute-start.60 = (bf16[256,2048]{1,0:T(8,128)(2,1)}, bf16[256,2048]{1,0:T(8,128)(2,1)}, u32[]{:S(2)}, u32[]{:S(2)}) collective-permute-start(bf16[256,2048]{1,0:T(8,128)(2,1)} %get-tuple-element.279), channel_id=1, source_target_pairs={{0,3},{1,2},{2,1},{3,0},{4,7},{5,6},{6,5},{7,4},{8,11},{9,10},{10,... | collective-permute-start | bytes 3145736 | tf_op jit(solution)/shard_map/ppermute | solution.py:79
  658.2 19.3 %collective-permute-start.54 = (f32[4,16,1536]{2,1,0:T(8,128)}, f32[4,16,1536]{2,1,0:T(8,128)}, u32[]{:S(2)}, u32[]{:S(2)}) collective-permute-start(f32[4,16,1536]{2,1,0:T(8,128)} %bitcast.74), channel_id=1, source_target_pairs={{0,4},{4,0},{8,12},{12,8},{16,20},{20,16},{24,28},{28,24},{1,5},{5... | collective-permute-start | bytes 1179656 | tf_op jit(solution)/shard_map/ppermute | solution.py:83
  670.9 66.4 %all-to-all-start.1 = ((bf16[32,5,2048]{2,1,0:T(8,128)(2,1)}), bf16[32,5,2048]{2,1,0:T(8,128)(2,1)S(1)}, u32[]{:S(2)}, u32[]{:S(2)}) async-start(bf16[32,5,2048]{2,1,0:T(8,128)(2,1)} %pad_maximum_fusion.8), calls=%async_computation.4 | async-start | bytes 2097152 | tf_op jit(solution)/shard_map/all_to_all | solution.py:70
  678.6 38.1 %collective-permute-start.55 = (f32[16,1536]{1,0:T(8,128)S(1)}, f32[16,1536]{1,0:T(8,128)S(1)}, u32[]{:S(2)}, u32[]{:S(2)}) collective-permute-start(f32[16,1536]{1,0:T(8,128)S(1)} %get-tuple-element.338), channel_id=1, source_target_pairs={{0,8},{4,12},{8,0},{12,4},{16,24},{20,28},{24,16},{28,20},{1,9},{5... | collective-permute-start | bytes 294920 | tf_op jit(solution)/shard_map/ppermute | solution.py:83
  682.7 41.8 %collective-permute-start.56 = (f32[16,1536]{1,0:T(8,128)S(1)}, f32[16,1536]{1,0:T(8,128)S(1)}, u32[]{:S(2)}, u32[]{:S(2)}) collective-permute-start(f32[16,1536]{1,0:T(8,128)S(1)} %get-tuple-element.336), channel_id=1, source_target_pairs={{0,16},{4,20},{8,24},{12,28},{16,0},{20,4},{24,8},{28,12},{1,17},{... | collective-permute-start | bytes 294920 | tf_op jit(solution)/shard_map/ppermute | solution.py:83
  716.7 17.3 %collective-permute-start.57 = (f32[16,1536]{1,0:T(8,128)S(1)}, f32[16,1536]{1,0:T(8,128)S(1)}, u32[]{:S(2)}, u32[]{:S(2)}) collective-permute-start(f32[16,1536]{1,0:T(8,128)S(1)} %get-tuple-element.337), channel_id=1, source_target_pairs={{0,24},{4,28},{8,16},{12,20},{16,8},{20,12},{24,0},{28,4},{1,25},{... | collective-permute-start | bytes 294920 | tf_op jit(solution)/shard_map/ppermute | solution.py:83
  724.6 13.0 %collective-permute-start.61 = (bf16[64,4224]{1,0:T(8,128)(2,1)}, bf16[64,4224]{1,0:T(8,128)(2,1)S(1)}, u32[]{:S(2)}, u32[]{:S(2)}) collective-permute-start(bf16[64,4224]{1,0:T(8,128)(2,1)} %get-tuple-element.298), channel_id=1, source_target_pairs={{0,1},{1,0},{2,3},{3,2},{4,5},{5,4},{6,7},{7,6},{8,9},{9,8},{10,11... | collective-permute-start | bytes 1622024 | tf_op jit(solution)/shard_map/ppermute | solution.py:79
  734.0 24.9 %collective-permute-start.62 = (bf16[64,4224]{1,0:T(8,128)(2,1)}, bf16[64,4224]{1,0:T(8,128)(2,1)S(1)}, u32[]{:S(2)}, u32[]{:S(2)}) collective-permute-start(bf16[64,4224]{1,0:T(8,128)(2,1)} %get-tuple-element.297), channel_id=1, source_target_pairs={{0,2},{1,3},{2,0},{3,1},{4,6},{5,7},{6,4},{7,5},{8,10},{9,11},{10,... | collective-permute-start | bytes 1622024 | tf_op jit(solution)/shard_map/ppermute | solution.py:79
  735.2 23.7 %collective-permute-start.63 = (bf16[64,4224]{1,0:T(8,128)(2,1)}, bf16[64,4224]{1,0:T(8,128)(2,1)S(1)}, u32[]{:S(2)}, u32[]{:S(2)}) collective-permute-start(bf16[64,4224]{1,0:T(8,128)(2,1)} %get-tuple-element.296), channel_id=1, source_target_pairs={{0,3},{1,2},{2,1},{3,0},{4,7},{5,6},{6,5},{7,4},{8,11},{9,10},{10,... | collective-permute-start | bytes 1622024 | tf_op jit(solution)/shard_map/ppermute | solution.py:79
  774.1 21.1 %collective-permute-start.68 = (bf16[64,1536]{1,0:T(8,128)(2,1)S(1)}, bf16[64,1536]{1,0:T(8,128)(2,1)S(1)}, u32[]{:S(2)}, u32[]{:S(2)}) collective-permute-start(bf16[64,1536]{1,0:T(8,128)(2,1)S(1)} %get-tuple-element.324), channel_id=1, source_target_pairs={{0,1},{1,0},{2,3},{3,2},{4,5},{5,4},{6,7},{7,6},{8,9},{9,8},{10,11... | collective-permute-start | bytes 589832 | tf_op jit(solution)/shard_map/ppermute | solution.py:79
  775.3 27.9 %collective-permute-start.69 = (bf16[64,1536]{1,0:T(8,128)(2,1)S(1)}, bf16[64,1536]{1,0:T(8,128)(2,1)S(1)}, u32[]{:S(2)}, u32[]{:S(2)}) collective-permute-start(bf16[64,1536]{1,0:T(8,128)(2,1)S(1)} %get-tuple-element.323), channel_id=1, source_target_pairs={{0,2},{1,3},{2,0},{3,1},{4,6},{5,7},{6,4},{7,5},{8,10},{9,11},{10,... | collective-permute-start | bytes 589832 | tf_op jit(solution)/shard_map/ppermute | solution.py:79
  776.5 26.7 %collective-permute-start.70 = (bf16[64,1536]{1,0:T(8,128)(2,1)S(1)}, bf16[64,1536]{1,0:T(8,128)(2,1)S(1)}, u32[]{:S(2)}, u32[]{:S(2)}) collective-permute-start(bf16[64,1536]{1,0:T(8,128)(2,1)S(1)} %get-tuple-element.322), channel_id=1, source_target_pairs={{0,3},{1,2},{2,1},{3,0},{4,7},{5,6},{6,5},{7,4},{8,11},{9,10},{10,... | collective-permute-start | bytes 589832 | tf_op jit(solution)/shard_map/ppermute | solution.py:79
  792.7 11.8 %collective-permute-start.71 = (bf16[64,2048]{1,0:T(8,128)(2,1)S(1)}, bf16[64,2048]{1,0:T(8,128)(2,1)S(1)}, u32[]{:S(2)}, u32[]{:S(2)}) collective-permute-start(bf16[64,2048]{1,0:T(8,128)(2,1)S(1)} %get-tuple-element.311), channel_id=1, source_target_pairs={{0,1},{1,0},{2,3},{3,2},{4,5},{5,4},{6,7},{7,6},{8,9},{9,8},{10,11... | collective-permute-start | bytes 786440 | tf_op jit(solution)/shard_map/ppermute | solution.py:79
  794.0 10.7 %collective-permute-start.72 = (bf16[64,2048]{1,0:T(8,128)(2,1)S(1)}, bf16[64,2048]{1,0:T(8,128)(2,1)S(1)}, u32[]{:S(2)}, u32[]{:S(2)}) collective-permute-start(bf16[64,2048]{1,0:T(8,128)(2,1)S(1)} %get-tuple-element.313), channel_id=1, source_target_pairs={{0,2},{1,3},{2,0},{3,1},{4,6},{5,7},{6,4},{7,5},{8,10},{9,11},{10,... | collective-permute-start | bytes 786440 | tf_op jit(solution)/shard_map/ppermute | solution.py:79
  (129 other events, 1994.4 us)
Sparse Core Ops, SparseCore 0:
  87.9 62.7 all-gather.4
  152.9 59.1 all-gather.6
  214.3 59.0 all-gather.8
  275.5 63.2 all-gather.10
  463.0 71.0 reduce-scatter.4
  536.3 63.7 reduce-scatter.6
  602.4 63.5 reduce-scatter.8
  668.2 123.0 reduce-scatter.10

commit v5 on v4

--- a/solution.py
+++ b/solution.py
@@ -238,9 +238,10 @@
     )(place("seq"), *blocks)
 
 
-def sum_dp(parts):
-    kept = parts[0] + swap_dp(parts[1], 1)
-    return kept[0] + sum(swap_dp(kept[j], 2 * j) for j in range(1, kept.shape[0]))
+def sum_dp(parts, kind):
+    kept = parts[0] + swap_dp(parts[1].astype(kind), 1).astype(f32)
+    sent = kept.astype(kind)
+    return kept[0] + sum(swap_dp(sent[j], 2 * j).astype(f32) for j in range(1, kept.shape[0]))
 
 
 def spread_dp(block):
@@ -543,7 +544,7 @@
     embed_dp = lax.dynamic_slice_in_dim(embed_table, my_dp * groups * rows, groups * rows, 1)
     embed_dp = dot(row_hot, embed_dp).astype(bf16)
     qkv_part = dot(embed_dp, qkv_cols)
-    qkv_rows = sum_dp(qkv_part.reshape(2, chips, piece, 3 * head_cols))
+    qkv_rows = sum_dp(qkv_part.reshape(2, chips, piece, 3 * head_cols), f32)
 
     qkv_rows, out_blocks = together(qkv_rows, out_blocks)
     qkv_table, chip_rows = spread_dp(halves(qkv_rows))
@@ -697,12 +698,13 @@
     norm_part = jnp.pad(norm_part, ((0, 0), (0, width - 8 * rows))).reshape(devices, 1, width)
     small = embed_part.astype(bf16).reshape(devices, vocab_here, width)
     small = jnp.concatenate([small, norm_part], axis=1)
+    sums_mine = sum_dp(qkv_sums.reshape(2, chips, piece, 3 * head_cols), bf16)
+    small, _ = together(small, sums_mine)
     small = jnp.sum(exchange(small, BOTH).astype(f32), axis=0)
     embedding_grad = small[:vocab_here]
     norm_grads = small[vocab_here, : 8 * rows].reshape(2, 4, rows)
     norm_grads = norm_grads[0] + norm_grads[1]
 
-    sums_mine = sum_dp(qkv_sums.reshape(2, chips, piece, 3 * head_cols))
     ff_blocks = own_rows([gate_rows, up_rows, down_rows], qkv_sums)
     sums_mine, input_blocks[-1], ff_blocks = together(sums_mine, input_blocks[-1], ff_blocks)
     input_grad = deep_alpha * d_first + jnp.concatenate(

time: 819 us -> 812 us (level)
    ppermute x24, waiting for transfers between devices: 78.9 us -> 43.4 us  [swap_dp(): lax.ppermute(block, 'dp', [(d, d ^ bits) for d in range(lax.axis_size('dp...]
    all_to_all x2, waiting for transfers between devices: 10.1 us -> 41.8 us  [exchange(): return lax.all_to_all(blocks, axes, split_axis=0, concat_axis=0, tiled=True)]
    ppermute x50, waiting for transfers between devices: 119 us -> 109 us  [swap(): lax.ppermute(block, 'seq', [(s, s ^ bits) for s in range(lax.axis_size('s...]
    reduce_scatter x1, waiting for transfers between devices: 14.5 us -> 23.9 us  [on_device(): out_rows = lax.psum_scatter(out_part, 'dp', scatter_dimension=0, tiled=True)]
  transfers between devices with their start and end apart: 84 -> 84, of which waited for: 36 -> 37; matrix products, arithmetic and copies ran while one was open for 37% -> 36% of each run, Pallas kernels for 12% -> 12%
where the time goes in v5:
time: 812 us; the launch traced here: 806 us
  matrix products  256 us (32%)
  waiting for transfers between devices  232 us (29%)
  starting transfers between devices  106 us (13%)
  Pallas kernels  96.9 us (12%)
  other arithmetic  59.1 us (7%)
  local copies, waits for them, and re-layouts  38.9 us (5%)
  between operations  16.5 us (2%)
    dot_general x50, matrix products, dot(): return lax.dot_general(left, right, dims, preferred_element_type=f32)  256 us
    ppermute x50, waiting for transfers between devices, swap(): lax.ppermute(block, 'seq', [(s, s ^ bits) for s in range(lax.axis_size('s...  109 us
    ppermute x24, starting transfers between devices, swap_dp(): lax.ppermute(block, 'dp', [(d, d ^ bits) for d in range(lax.axis_size('dp...  53.5 us
    ppermute x24, waiting for transfers between devices, swap_dp(): lax.ppermute(block, 'dp', [(d, d ^ bits) for d in range(lax.axis_size('dp...  43.4 us
    ppermute x50, starting transfers between devices, swap(): lax.ppermute(block, 'seq', [(s, s ^ bits) for s in range(lax.axis_size('s...  43.2 us
    all_to_all x2, waiting for transfers between devices, exchange(): return lax.all_to_all(blocks, axes, split_axis=0, concat_axis=0, tiled=True)  41.8 us
    pallas_call x2, Pallas kernels, attend_back(): pl.pallas_call(attend_back_kernel, grid=(heads,), in_specs=[pl.BlockSpec(...  36.7 us
    pallas_call x2, Pallas kernels, attend(): pl.pallas_call(attend_kernel, grid=(seqs, heads), in_specs=[pl.BlockSpec(...  25.3 us
  transfers between devices with their start and end apart: 84, of which 37 were waited for; matrix products, arithmetic and copies ran while one was open for 36% of the time, Pallas kernels for 12%

profile of v5, /device:TPU:9, one launch (start us, length us, event | category | flops | bytes accessed | tf_op | source)
XLA Modules:
  0.0 806.3 jit_solution(1465729911709909934)
XLA Ops:
  26.3 7.1 collective-permute-done.5
  46.8 7.1 collective-permute-done.14
  57.9 13.4 %collective-permute-done.16 = bf16[64,2048]{1,0:T(8,128)(2,1)S(1)} collective-permute-done((bf16[64,2048]{1,0:T(8,128)(2,1)S(1)}, bf16[64,2048]{1,0:T(8,128)(2,1)S(1)}, u32[]{:S(2)}, u32[]{:S(2)}) %collective-permute-start.16) | collective-permute-done | bytes 262176 | tf_op jit(solution)/shard_map/ppermute | solution.py:83
  80.0 4.7 collective-permute-done.36.refs_3_
  94.1 5.7 collective-permute-start.22
  103.2 8.2 %collective-permute-done.17 = bf16[4,64,2048]{2,1,0:T(8,128)(2,1)} collective-permute-done((bf16[4,64,2048]{2,1,0:T(8,128)(2,1)}, bf16[4,64,2048]{2,1,0:T(8,128)(2,1)}, u32[]{:S(2)}, u32[]{:S(2)}) %collective-permute-start.17) | collective-permute-done | bytes 1048608 | tf_op jit(solution)/shard_map/ppermute | solution.py:79
  117.6 12.7 %shard_map.241 = bf16[4,1,256,512]{3,2,1,0:T(8,128)(2,1)S(1)} custom-call(s32[1]{0:T(128)} %bitcast.12.place_ref.seq_ref, s32[1]{0:T(128)} %get-tuple-element.373.prefix_ref, bf16[4,1,256,128]{3,2,1,0:T(8,128)(2,1)S(1)} %get-tuple-element.336.hot_ref, bf16[256,3,512]{2,1,0:T(4,128)(2,1)S(1)} %reshape.515.table_ref, ...), custom_call_target="tpu_custom_call" | custom-call | flops 2147483648 | bytes 2097152 | tf_op jit(solution)/shard_map/pallas_call | solution.py:404
  130.4 3.9 pad_maximum_fusion.mine_ref
  134.3 8.8 %collective-permute-start.31 = (bf16[4,4,64,2048]{3,2,1,0:T(8,128)(2,1)}, bf16[4,4,64,2048]{3,2,1,0:T(8,128)(2,1)}, u32[]{:S(2)}, u32[]{:S(2)}) collective-permute-start(bf16[4,4,64,2048]{3,2,1,0:T(8,128)(2,1)} %pad_maximum_fusion.mine_ref), channel_id=1, source_target_pairs={{0,4},{4,0},{8,12},{12,8},{16,20},{20,16},{24,28},{28,24},{1,5},{5... | collective-permute-start | bytes 12582920 | tf_op jit(solution)/shard_map/ppermute | solution.py:83
  147.5 12.6 %shard_map.240 = bf16[4,1,256,512]{3,2,1,0:T(8,128)(2,1)S(1)} custom-call(s32[1]{0:T(128)} %bitcast.12.place_ref.seq_ref, s32[1]{0:T(128)} %get-tuple-element.374.prefix_ref, bf16[4,1,256,128]{3,2,1,0:T(8,128)(2,1)S(1)} %get-tuple-element.337.hot_ref, bf16[256,3,512]{2,1,0:T(4,128)(2,1)S(1)} %reshape.515.table_ref, ...), custom_call_target="tpu_custom_call" | custom-call | flops 2147483648 | bytes 2097152 | tf_op jit(solution)/shard_map/pallas_call | solution.py:404
  163.8 3.7 collective-permute-done.23.refs_1_
  168.7 4.7 collective-permute-done.25.refs_3_
  173.6 7.7 shard_map.243
  181.3 4.7 fusion.129
  190.7 8.3 %fusion.132 = f32[512,1408]{1,0:T(8,128)} fusion(bf16[512,2048]{1,0:T(8,128)(2,1)} %fusion.31, bf16[2048,1408]{1,0:T(8,128)(2,1)} %all-gather.5.cloned.1.call-done), kind=kOutput, calls=%fused_computation.333 | convolution fusion | flops 2952790016 | bytes 10747904 | tf_op jit(solution)/shard_map/dot_general | solution.py:29
  199.0 13.1 %all-gather.7.cloned.1.call-done = bf16[2048,1408]{1,0:T(8,128)(2,1)} async-done(((bf16[256,1408]{1,0:T(8,128)(2,1)}), bf16[2048,1408]{1,0:T(8,128)(2,1)}) %all-gather.7.cloned.1.call-update) | async-done | bytes 5767184 | tf_op jit(solution)/shard_map/all_gather | solution.py:555
  212.1 10.8 %fusion.37 = (bf16[512,1408]{1,0:T(8,128)(2,1)}, bf16[512,1408]{1,0:T(8,128)(2,1)}, bf16[512,1408]{1,0:T(8,128)(2,1)}) fusion(f32[512,1408]{1,0:T(8,128)} %fusion.132, bf16[512,2048]{1,0:T(8,128)(2,1)} %fusion.31, bf16[2048,1408]{1,0:T(8,128)(2,1)} %all-gather.7.cloned.1.call-done), kind=kOutput, calls=%fused_computation.78 | convolution fusion | flops 2966487040 | bytes 15073280 | tf_op jit(solution)/shard_map/dot_general | solution.py:29
  222.9 10.8 %collective-permute-done.32 = bf16[512,2048]{1,0:T(8,128)(2,1)} collective-permute-done((bf16[512,2048]{1,0:T(8,128)(2,1)}, bf16[512,2048]{1,0:T(8,128)(2,1)}, u32[]{:S(2)}, u32[]{:S(2)}) %collective-permute-start.32) | collective-permute-done | bytes 2097184 | tf_op jit(solution)/shard_map/ppermute | solution.py:79
  239.1 5.2 fusion.134
  244.3 5.2 fusion.133
  249.5 8.0 fusion.49
  257.5 7.7 fusion.43
  270.6 5.1 multiply_convert_fusion.8
  275.7 6.7 convolution_convert_fusion.7
  284.0 5.4 fusion.138
  296.3 7.5 collective-permute-done.39
  309.7 21.8 %shard_map.248 = (bf16[2,4,3,1024,128]{4,3,2,1,0:T(8,128)(2,1)}, bf16[2,4,4,1024,256]{4,3,2,1,0:T(8,128)(2,1)}) custom-call(s32[2]{0:T(128)S(1)} %copy-done.15, bf16[4,2,256,128]{3,2,1,0:T(8,128)(2,1)S(1)} %get-tuple-element.372.hot_ref, bf16[256,3,512]{2,1,0:T(4,128)(2,1)S(1)} %reshape.515.table_ref, f32[1024,128]{1,0:T(8,128)S(1)} %get-tuple-element.384.cos_ref, ...), custom_call_target="tpu_custom_call" | custom-call | flops 2147483648 | bytes 16777216 | tf_op jit(solution)/shard_map/pallas_call | solution.py:425
  331.5 20.0 %collective-permute-done.41 = bf16[512,2048]{1,0:T(8,128)(2,1)} collective-permute-done((bf16[512,2048]{1,0:T(8,128)(2,1)}, bf16[512,2048]{1,0:T(8,128)(2,1)}, u32[]{:S(2)}, u32[]{:S(2)}) %collective-permute-start.41) | collective-permute-done | bytes 2097184 | tf_op jit(solution)/shard_map/ppermute | solution.py:79
  365.8 5.6 convolution_convert_fusion.1
  377.0 7.6 convolution_convert_fusion.2
  384.7 7.7 convolution_convert_fusion.3
  392.4 5.0 fusion.140
  397.4 6.6 convolution_add_fusion.2
  404.1 8.8 %collective-permute-done.43 = bf16[512,2048]{1,0:T(8,128)(2,1)S(1)} collective-permute-done((bf16[512,2048]{1,0:T(8,128)(2,1)S(1)}, bf16[512,2048]{1,0:T(8,128)(2,1)S(1)}, u32[]{:S(2)}, u32[]{:S(2)}) %collective-permute-start.43) | collective-permute-done | bytes 2097184 | tf_op jit(solution)/shard_map/ppermute | solution.py:79
  415.3 4.9 multiply_convert_fusion.2
  420.3 4.9 multiply_convert_fusion.4
  425.2 9.4 %collective-permute-done.45 = bf16[256,2048]{1,0:T(8,128)(2,1)S(1)} collective-permute-done((bf16[256,2048]{1,0:T(8,128)(2,1)S(1)}, bf16[256,2048]{1,0:T(8,128)(2,1)S(1)}, u32[]{:S(2)}, u32[]{:S(2)}) %collective-permute-start.45) | collective-permute-done | bytes 1048608 | tf_op jit(solution)/shard_map/ppermute | solution.py:79
  434.8 4.6 multiply_convert_fusion
  442.9 3.7 add_convert_fusion.3
  446.7 16.1 %add_convert_fusion.2 = bf16[2048,1408]{1,0:T(8,128)(2,1)} fusion(bf16[2048,1408]{1,0:T(8,128)(2,1)} %convolution_convert_fusion.3, bf16[512,2048]{1,0:T(8,128)(2,1)S(1)} %copy-done.47, bf16[512,2048]{1,0:T(8,128)(2,1)} %collective-permute-done.33, bf16[512,2048]{1,0:T(8,128)(2,1)} %collective-permute-done.32, bf16[512,1408]{1,0:T(8,128)(2,1)} %copy-done.90, ...), kind=kOutput, calls=%fused_computation.2 | convolution fusion | flops 8898871296 | bytes 22151168 | tf_op jit(solution)/shard_map/dot_general | solution.py:29
  465.2 6.0 fusion.143
  474.8 4.8 fusion.142
  479.6 4.8 convolution_add_fusion.1
  490.9 15.1 %add_convert_fusion = bf16[2048,1408]{1,0:T(8,128)(2,1)} fusion(bf16[2048,1408]{1,0:T(8,128)(2,1)} %convolution_convert_fusion.1, bf16[512,2048]{1,0:T(8,128)(2,1)S(1)} %copy-done.49, bf16[512,2048]{1,0:T(8,128)(2,1)S(1)} %copy-done.45, bf16[512,2048]{1,0:T(8,128)(2,1)S(1)} %copy-done.43, bf16[512,1408]{1,0:T(8,128)(2,1)S(1)} %copy-done.83, ...), kind=kOutput, calls=%fused_computation | convolution fusion | flops 8898871296 | bytes 22151168 | tf_op jit(solution)/shard_map/dot_general | solution.py:29
  506.0 15.6 %add_convert_fusion.1 = bf16[2048,1408]{1,0:T(8,128)(2,1)} fusion(bf16[2048,1408]{1,0:T(8,128)(2,1)} %convolution_convert_fusion.2, bf16[512,2048]{1,0:T(8,128)(2,1)} %copy-done.46, bf16[512,2048]{1,0:T(8,128)(2,1)} %collective-permute-done.33, bf16[512,2048]{1,0:T(8,128)(2,1)} %collective-permute-done.32, bf16[512,1408]{1,0:T(8,128)(2,1)} %copy-done.86, ...), kind=kOutput, calls=%fused_computation.1 | convolution fusion | flops 8898871296 | bytes 22151168 | tf_op jit(solution)/shard_map/dot_general | solution.py:29
  521.6 5.8 collective-permute-done.49
  528.5 7.9 multiply_reduce_fusion.1
  537.6 9.9 %convolution_convert_fusion.6 = bf16[512,2048]{1,0:T(8,128)(2,1)S(1)} fusion(bf16[2048,2048]{1,0:T(8,128)(2,1)} %bitcast.296, f32[512,2048]{1,0:T(8,128)S(1)} %get-tuple-element.269, f32[512]{0:T(512)S(1)} %negate_multiply_fusion), kind=kOutput, calls=%fused_computation.71 | convolution fusion | flops 4298113024 | bytes 14682112 | tf_op jit(solution)/shard_map/dot_general | solution.py:29
  552.7 10.9 %convolution_convert_fusion = bf16[2048,2048]{1,0:T(8,128)(2,1)} fusion(bf16[512,2048]{1,0:T(8,128)(2,1)} %copy-done.5, f32[512,2048]{1,0:T(8,128)} %copy-done.19, f32[512]{0:T(512)S(1)} %negate_multiply_fusion), kind=kOutput, calls=%fused_computation.3 | convolution fusion | flops 4301258752 | bytes 14682112 | tf_op jit(solution)/shard_map/dot_general | solution.py:29
  563.6 10.0 %all-to-all-done = bf16[4,512,512]{2,1,0:T(8,128)(2,1)S(1)} async-done(((bf16[4,512,512]{2,1,0:T(8,128)(2,1)}), bf16[4,512,512]{2,1,0:T(8,128)(2,1)S(1)}, u32[]{:S(2)}, u32[]{:S(2)}) %all-to-all-start) | async-done | bytes 2097184 | tf_op jit(solution)/shard_map/all_to_all | solution.py:70
  581.0 18.7 %shard_map.249 = bf16[4,256,1536]{2,1,0:T(8,128)(2,1)} custom-call(s32[1]{0:T(128)} %bitcast.12.place_ref.seq_ref, bf16[2,4,3,1024,128]{4,3,2,1,0:T(8,128)(2,1)} %get-tuple-element.222.field_ref, bf16[2,4,4,1024,256]{4,3,2,1,0:T(8,128)(2,1)} %get-tuple-element.223.probs_ref, f32[1024,128]{1,0:T(8,128)S(1)} %copy-done.2, f32[1024,128]{1,0:T(8,128)S(1)} %copy-done.4, ...), custom_call_target="tpu_custom_call" | custom-call | flops 4294967296 | bytes 8388608 | tf_op jit(solution)/shard_map/pallas_call | solution.py:450
  599.7 8.3 %convolution_convert_fusion.5 = bf16[1024,2048]{1,0:T(8,128)(2,1)S(1)} fusion(bf16[1024,1536]{1,0:T(8,128)(2,1)} %bitcast.300, bf16[2048,1536]{1,0:T(8,128)(2,1)S(1)} %bitcast.353), kind=kOutput, calls=%fused_computation.65 | convolution fusion | flops 6444548096 | bytes 13631488 | tf_op jit(solution)/shard_map/dot_general | solution.py:29
  612.3 18.0 %shard_map.250 = bf16[4,256,1536]{2,1,0:T(8,128)(2,1)} custom-call(s32[1]{0:T(128)} %bitcast.12.place_ref.seq_ref, bf16[2,4,3,1024,128]{4,3,2,1,0:T(8,128)(2,1)} %get-tuple-element.222.field_ref, bf16[2,4,4,1024,256]{4,3,2,1,0:T(8,128)(2,1)} %get-tuple-element.223.probs_ref, f32[1024,128]{1,0:T(8,128)S(1)} %copy-done.2, f32[1024,128]{1,0:T(8,128)S(1)} %copy-done.4, ...), custom_call_target="tpu_custom_call" | custom-call | flops 4294967296 | bytes 8388608 | tf_op jit(solution)/shard_map/pallas_call | solution.py:450
  630.3 10.2 %convolution_convert_fusion.4 = bf16[1024,2048]{1,0:T(8,128)(2,1)S(1)} fusion(bf16[1024,1536]{1,0:T(8,128)(2,1)} %bitcast.298, bf16[2048,1536]{1,0:T(8,128)(2,1)} %all-gather.11.cloned.1.call-done), kind=kOutput, calls=%fused_computation.64 | convolution fusion | flops 6444548096 | bytes 13631488 | tf_op jit(solution)/shard_map/dot_general | solution.py:29
  641.1 10.0 %collective-permute-done.53 = bf16[256,2048]{1,0:T(8,128)(2,1)S(1)} collective-permute-done((bf16[256,2048]{1,0:T(8,128)(2,1)S(1)}, bf16[256,2048]{1,0:T(8,128)(2,1)S(1)}, u32[]{:S(2)}, u32[]{:S(2)}) %collective-permute-start.53) | collective-permute-done | bytes 1048608 | tf_op jit(solution)/shard_map/ppermute | solution.py:79
  656.1 7.4 collective-permute-start.54
  667.9 4.1 collective-permute-start.55
  679.4 5.1 all-to-all-start.1
  693.9 31.8 %all-to-all-done.1 = bf16[32,5,2048]{2,1,0:T(8,128)(2,1)S(1)} async-done(((bf16[32,5,2048]{2,1,0:T(8,128)(2,1)}), bf16[32,5,2048]{2,1,0:T(8,128)(2,1)S(1)}, u32[]{:S(2)}, u32[]{:S(2)}) %all-to-all-start.1) | async-done | bytes 655392 | tf_op jit(solution)/shard_map/all_to_all | solution.py:70
  728.2 8.3 %collective-permute-done.63.refs_3_ = bf16[64,4224]{1,0:T(8,128)(2,1)S(1)} collective-permute-done((bf16[64,4224]{1,0:T(8,128)(2,1)}, bf16[64,4224]{1,0:T(8,128)(2,1)S(1)}, u32[]{:S(2)}, u32[]{:S(2)}) %collective-permute-start.63) | collective-permute-done | bytes 540704 | tf_op jit(solution)/shard_map/ppermute | solution.py:79
  747.5 6.1 collective-permute-start.67
  753.6 4.3 convert_add_fusion
  761.2 23.9 %reduce-scatter.11.cloned.1.call-done.refs_0_ = bf16[256,2048]{1,0:T(8,128)(2,1)} async-done(((bf16[2048,2048]{1,0:T(8,128)(2,1)}), bf16[256,2048]{1,0:T(8,128)(2,1)}) %reduce-scatter.11.cloned.1.call-update) | async-done | bytes 1048592 | tf_op jit(solution)/shard_map/reduce_scatter | solution.py:670
  789.2 5.4 maximum_add_fusion
  (551 shorter events, 212.2 us)
Async XLA Ops:
  7.2 183.5 %all-gather.5.cloned.1.call-start = ((), (), s32[]{:S(2)}) async-start(), calls=%async_computation.6 | async-start | bytes 6488064 | tf_op jit(solution)/shard_map/all_gather | solution.py:555
  16.7 19.0 %collective-permute-start.7 = (bf16[64,1536]{1,0:T(8,128)(2,1)}, bf16[64,1536]{1,0:T(8,128)(2,1)S(1)}, u32[]{:S(2)}, u32[]{:S(2)}) collective-permute-start(bf16[64,1536]{1,0:T(8,128)(2,1)} %get-tuple-element.334), channel_id=1, source_target_pairs={{0,1},{1,0},{2,3},{3,2},{4,5},{5,4},{6,7},{7,6},{8,9},{9,8},{10,11... | collective-permute-start | bytes 589832 | tf_op jit(solution)/shard_map/ppermute | solution.py:79
  18.0 17.8 %collective-permute-start.8 = (bf16[64,1536]{1,0:T(8,128)(2,1)}, bf16[64,1536]{1,0:T(8,128)(2,1)S(1)}, u32[]{:S(2)}, u32[]{:S(2)}) collective-permute-start(bf16[64,1536]{1,0:T(8,128)(2,1)} %get-tuple-element.333), channel_id=1, source_target_pairs={{0,2},{1,3},{2,0},{3,1},{4,6},{5,7},{6,4},{7,5},{8,10},{9,11},{10,... | collective-permute-start | bytes 589832 | tf_op jit(solution)/shard_map/ppermute | solution.py:79
  22.2 11.1 %collective-permute-start.5 = (bf16[4,5,2048]{2,1,0:T(8,128)(2,1)S(1)}, bf16[4,5,2048]{2,1,0:T(8,128)(2,1)S(1)}, u32[]{:S(2)}, u32[]{:S(2)}) collective-permute-start(bf16[4,5,2048]{2,1,0:T(8,128)(2,1)S(1)} %get-tuple-element.351), channel_id=1, source_target_pairs={{0,24},{4,28},{8,16},{12,20},{16,8},{20,12},{24,0},{28,4},{1,25},{... | collective-permute-start | bytes 245768 | tf_op jit(solution)/shard_map/ppermute | solution.py:83
  23.9 12.0 %collective-permute-start.9 = (bf16[64,1536]{1,0:T(8,128)(2,1)}, bf16[64,1536]{1,0:T(8,128)(2,1)S(1)}, u32[]{:S(2)}, u32[]{:S(2)}) collective-permute-start(bf16[64,1536]{1,0:T(8,128)(2,1)} %get-tuple-element.332), channel_id=1, source_target_pairs={{0,3},{1,2},{2,1},{3,0},{4,7},{5,6},{6,5},{7,4},{8,11},{9,10},{10,... | collective-permute-start | bytes 589832 | tf_op jit(solution)/shard_map/ppermute | solution.py:79
  43.3 36.6 %collective-permute-start.34 = (bf16[64,4224]{1,0:T(8,128)(2,1)S(1)}, bf16[64,4224]{1,0:T(8,128)(2,1)S(1)}, u32[]{:S(2)}, u32[]{:S(2)}) collective-permute-start(bf16[64,4224]{1,0:T(8,128)(2,1)S(1)} %get-tuple-element.309), channel_id=1, source_target_pairs={{0,1},{1,0},{2,3},{3,2},{4,5},{5,4},{6,7},{7,6},{8,9},{9,8},{10,11... | collective-permute-start | bytes 1622024 | tf_op jit(solution)/shard_map/ppermute | solution.py:79
  43.6 36.4 %collective-permute-start.35 = (bf16[64,4224]{1,0:T(8,128)(2,1)S(1)}, bf16[64,4224]{1,0:T(8,128)(2,1)S(1)}, u32[]{:S(2)}, u32[]{:S(2)}) collective-permute-start(bf16[64,4224]{1,0:T(8,128)(2,1)S(1)} %get-tuple-element.308), channel_id=1, source_target_pairs={{0,2},{1,3},{2,0},{3,1},{4,6},{5,7},{6,4},{7,5},{8,10},{9,11},{10,... | collective-permute-start | bytes 1622024 | tf_op jit(solution)/shard_map/ppermute | solution.py:79
  44.1 9.9 %collective-permute-start.14 = (bf16[64,2048]{1,0:T(8,128)(2,1)S(1)}, bf16[64,2048]{1,0:T(8,128)(2,1)S(1)}, u32[]{:S(2)}, u32[]{:S(2)}) collective-permute-start(bf16[64,2048]{1,0:T(8,128)(2,1)S(1)} %copy-done.52), channel_id=1, source_target_pairs={{0,8},{4,12},{8,0},{12,4},{16,24},{20,28},{24,16},{28,20},{1,9},{5... | collective-permute-start | bytes 786440 | tf_op jit(solution)/shard_map/ppermute | solution.py:83
  44.1 13.8 %collective-permute-start.15 = (bf16[64,2048]{1,0:T(8,128)(2,1)S(1)}, bf16[64,2048]{1,0:T(8,128)(2,1)S(1)}, u32[]{:S(2)}, u32[]{:S(2)}) collective-permute-start(bf16[64,2048]{1,0:T(8,128)(2,1)S(1)} %copy-done.52), channel_id=1, source_target_pairs={{0,16},{4,20},{8,24},{12,28},{16,0},{20,4},{24,8},{28,12},{1,17},{... | collective-permute-start | bytes 786440 | tf_op jit(solution)/shard_map/ppermute | solution.py:83
  46.6 24.8 %collective-permute-start.16 = (bf16[64,2048]{1,0:T(8,128)(2,1)S(1)}, bf16[64,2048]{1,0:T(8,128)(2,1)S(1)}, u32[]{:S(2)}, u32[]{:S(2)}) collective-permute-start(bf16[64,2048]{1,0:T(8,128)(2,1)S(1)} %copy-done.52), channel_id=1, source_target_pairs={{0,24},{4,28},{8,16},{12,20},{16,8},{20,12},{24,0},{28,4},{1,25},{... | collective-permute-start | bytes 786440 | tf_op jit(solution)/shard_map/ppermute | solution.py:83
  54.0 20.7 %collective-permute-start.11 = (f32[16,1536]{1,0:T(8,128)S(1)}, f32[16,1536]{1,0:T(8,128)S(1)}, u32[]{:S(2)}, u32[]{:S(2)}) collective-permute-start(f32[16,1536]{1,0:T(8,128)S(1)} %get-tuple-element.342), channel_id=1, source_target_pairs={{0,8},{4,12},{8,0},{12,4},{16,24},{20,28},{24,16},{28,20},{1,9},{5... | collective-permute-start | bytes 294920 | tf_op jit(solution)/shard_map/ppermute | solution.py:83
  57.9 18.7 %collective-permute-start.12 = (f32[16,1536]{1,0:T(8,128)S(1)}, f32[16,1536]{1,0:T(8,128)S(1)}, u32[]{:S(2)}, u32[]{:S(2)}) collective-permute-start(f32[16,1536]{1,0:T(8,128)S(1)} %get-tuple-element.340), channel_id=1, source_target_pairs={{0,16},{4,20},{8,24},{12,28},{16,0},{20,4},{24,8},{28,12},{1,17},{... | collective-permute-start | bytes 294920 | tf_op jit(solution)/shard_map/ppermute | solution.py:83
  74.6 10.0 %collective-permute-start.36 = (bf16[64,4224]{1,0:T(8,128)(2,1)S(1)}, bf16[64,4224]{1,0:T(8,128)(2,1)S(1)}, u32[]{:S(2)}, u32[]{:S(2)}) collective-permute-start(bf16[64,4224]{1,0:T(8,128)(2,1)S(1)} %get-tuple-element.307), channel_id=1, source_target_pairs={{0,3},{1,2},{2,1},{3,0},{4,7},{5,6},{6,5},{7,4},{8,11},{9,10},{10,... | collective-permute-start | bytes 1622024 | tf_op jit(solution)/shard_map/ppermute | solution.py:79
  87.8 124.3 %all-gather.7.cloned.1.call-start = ((), (), s32[]{:S(2)}) async-start(), calls=%async_computation.7 | async-start | bytes 6488064 | tf_op jit(solution)/shard_map/all_gather | solution.py:555
  88.6 187.2 %all-gather.9.cloned.1.call-start = ((), (), s32[]{:S(2)}) async-start(), calls=%async_computation.8 | async-start | bytes 6488064 | tf_op jit(solution)/shard_map/all_gather | solution.py:555
  89.3 273.8 %all-gather.11.cloned.1.call-start = ((), (), s32[]{:S(2)}) async-start(), calls=%async_computation.9 | async-start | bytes 7077888 | tf_op jit(solution)/shard_map/all_gather | solution.py:555
  91.8 19.6 %collective-permute-start.17 = (bf16[4,64,2048]{2,1,0:T(8,128)(2,1)}, bf16[4,64,2048]{2,1,0:T(8,128)(2,1)}, u32[]{:S(2)}, u32[]{:S(2)}) collective-permute-start(bf16[4,64,2048]{2,1,0:T(8,128)(2,1)} %pad_maximum_fusion.7), channel_id=1, source_target_pairs={{0,1},{1,0},{2,3},{3,2},{4,5},{5,4},{6,7},{7,6},{8,9},{9,8},{10,11... | collective-permute-start | bytes 3145736 | tf_op jit(solution)/shard_map/ppermute | solution.py:79
  92.9 19.6 %collective-permute-start.18 = (bf16[4,64,2048]{2,1,0:T(8,128)(2,1)}, bf16[4,64,2048]{2,1,0:T(8,128)(2,1)}, u32[]{:S(2)}, u32[]{:S(2)}) collective-permute-start(bf16[4,64,2048]{2,1,0:T(8,128)(2,1)} %pad_maximum_fusion.7), channel_id=1, source_target_pairs={{0,2},{1,3},{2,0},{3,1},{4,6},{5,7},{6,4},{7,5},{8,10},{9,11},{10,... | collective-permute-start | bytes 3145736 | tf_op jit(solution)/shard_map/ppermute | solution.py:79
  113.5 16.8 %collective-permute-start.29 = (bf16[2,64,2048]{2,1,0:T(8,128)(2,1)S(1)}, bf16[2,64,2048]{2,1,0:T(8,128)(2,1)S(1)}, u32[]{:S(2)}, u32[]{:S(2)}) collective-permute-start(bf16[2,64,2048]{2,1,0:T(8,128)(2,1)S(1)} %slice.332), channel_id=1, source_target_pairs={{0,2},{1,3},{2,0},{3,1},{4,6},{5,7},{6,4},{7,5},{8,10},{9,11},{10,... | collective-permute-start | bytes 1572872 | tf_op jit(solution)/shard_map/ppermute | solution.py:79
  115.9 14.4 %collective-permute-start.30 = (bf16[2,64,2048]{2,1,0:T(8,128)(2,1)S(1)}, bf16[2,64,2048]{2,1,0:T(8,128)(2,1)S(1)}, u32[]{:S(2)}, u32[]{:S(2)}) collective-permute-start(bf16[2,64,2048]{2,1,0:T(8,128)(2,1)S(1)} %slice.333), channel_id=1, source_target_pairs={{0,1},{1,0},{2,3},{3,2},{4,5},{5,4},{6,7},{7,6},{8,9},{9,8},{10,11... | collective-permute-start | bytes 1572872 | tf_op jit(solution)/shard_map/ppermute | solution.py:79
  134.3 39.2 %collective-permute-start.31 = (bf16[4,4,64,2048]{3,2,1,0:T(8,128)(2,1)}, bf16[4,4,64,2048]{3,2,1,0:T(8,128)(2,1)}, u32[]{:S(2)}, u32[]{:S(2)}) collective-permute-start(bf16[4,4,64,2048]{3,2,1,0:T(8,128)(2,1)} %pad_maximum_fusion.mine_ref), channel_id=1, source_target_pairs={{0,4},{4,0},{8,12},{12,8},{16,20},{20,16},{24,28},{28,24},{1,5},{5... | collective-permute-start | bytes 12582920 | tf_op jit(solution)/shard_map/ppermute | solution.py:83
  144.8 16.7 %collective-permute-start.26 = (bf16[256,512]{1,0:T(8,128)(2,1)S(1)}, bf16[256,512]{1,0:T(8,128)(2,1)S(1)}, u32[]{:S(2)}, u32[]{:S(2)}) collective-permute-start(bf16[256,512]{1,0:T(8,128)(2,1)S(1)} %get-tuple-element.320), channel_id=1, source_target_pairs={{0,1},{1,0},{2,3},{3,2},{4,5},{5,4},{6,7},{7,6},{8,9},{9,8},{10,11... | collective-permute-start | bytes 786440 | tf_op jit(solution)/shard_map/ppermute | solution.py:79
  146.1 15.7 %collective-permute-start.27 = (bf16[256,512]{1,0:T(8,128)(2,1)S(1)}, bf16[256,512]{1,0:T(8,128)(2,1)S(1)}, u32[]{:S(2)}, u32[]{:S(2)}) collective-permute-start(bf16[256,512]{1,0:T(8,128)(2,1)S(1)} %get-tuple-element.319), channel_id=1, source_target_pairs={{0,2},{1,3},{2,0},{3,1},{4,6},{5,7},{6,4},{7,5},{8,10},{9,11},{10,... | collective-permute-start | bytes 786440 | tf_op jit(solution)/shard_map/ppermute | solution.py:79
  146.4 17.4 %collective-permute-start.28 = (bf16[256,512]{1,0:T(8,128)(2,1)S(1)}, bf16[256,512]{1,0:T(8,128)(2,1)S(1)}, u32[]{:S(2)}, u32[]{:S(2)}) collective-permute-start(bf16[256,512]{1,0:T(8,128)(2,1)S(1)} %get-tuple-element.318), channel_id=1, source_target_pairs={{0,3},{1,2},{2,1},{3,0},{4,7},{5,6},{6,5},{7,4},{8,11},{9,10},{10,... | collective-permute-start | bytes 786440 | tf_op jit(solution)/shard_map/ppermute | solution.py:79
  161.8 11.6 %collective-permute-start.25 = (bf16[256,512]{1,0:T(8,128)(2,1)S(1)}, bf16[256,512]{1,0:T(8,128)(2,1)S(1)}, u32[]{:S(2)}, u32[]{:S(2)}) collective-permute-start(bf16[256,512]{1,0:T(8,128)(2,1)S(1)} %get-tuple-element.322), channel_id=1, source_target_pairs={{0,3},{1,2},{2,1},{3,0},{4,7},{5,6},{6,5},{7,4},{8,11},{9,10},{10,... | collective-permute-start | bytes 786440 | tf_op jit(solution)/shard_map/ppermute | solution.py:79
  188.7 45.0 %collective-permute-start.32 = (bf16[512,2048]{1,0:T(8,128)(2,1)}, bf16[512,2048]{1,0:T(8,128)(2,1)}, u32[]{:S(2)}, u32[]{:S(2)}) collective-permute-start(bf16[512,2048]{1,0:T(8,128)(2,1)} %fusion.31), channel_id=1, source_target_pairs={{0,1},{1,0},{2,3},{3,2},{4,5},{5,4},{6,7},{7,6},{8,9},{9,8},{10,11... | collective-permute-start | bytes 6291464 | tf_op jit(solution)/shard_map/ppermute | solution.py:79
  189.5 45.2 %collective-permute-start.33 = (bf16[512,2048]{1,0:T(8,128)(2,1)}, bf16[512,2048]{1,0:T(8,128)(2,1)}, u32[]{:S(2)}, u32[]{:S(2)}) collective-permute-start(bf16[512,2048]{1,0:T(8,128)(2,1)} %fusion.31), channel_id=1, source_target_pairs={{0,2},{1,3},{2,0},{3,1},{4,6},{5,7},{6,4},{7,5},{8,10},{9,11},{10,... | collective-permute-start | bytes 6291464 | tf_op jit(solution)/shard_map/ppermute | solution.py:79
  190.6 493.8 %reduce-scatter.5.cloned.1.call-start = ((), (), s32[]{:S(2)}) async-start(), calls=%async_computation.10 | async-start | bytes 6488064 | tf_op jit(solution)/shard_map/reduce_scatter | solution.py:655
  235.9 29.2 %collective-permute-start.37 = (bf16[256,2048]{1,0:T(8,128)(2,1)S(1)}, bf16[256,2048]{1,0:T(8,128)(2,1)S(1)}, u32[]{:S(2)}, u32[]{:S(2)}) collective-permute-start(bf16[256,2048]{1,0:T(8,128)(2,1)S(1)} %slice.343), channel_id=1, source_target_pairs={{0,2},{1,3},{2,0},{3,1},{4,6},{5,7},{6,4},{7,5},{8,10},{9,11},{10,... | collective-permute-start | bytes 3145736 | tf_op jit(solution)/shard_map/ppermute | solution.py:79
  238.6 26.5 %collective-permute-start.38 = (bf16[256,2048]{1,0:T(8,128)(2,1)S(1)}, bf16[256,2048]{1,0:T(8,128)(2,1)S(1)}, u32[]{:S(2)}, u32[]{:S(2)}) collective-permute-start(bf16[256,2048]{1,0:T(8,128)(2,1)S(1)} %slice.344), channel_id=1, source_target_pairs={{0,1},{1,0},{2,3},{3,2},{4,5},{5,4},{6,7},{7,6},{8,9},{9,8},{10,11... | collective-permute-start | bytes 3145736 | tf_op jit(solution)/shard_map/ppermute | solution.py:79
  282.6 21.2 %collective-permute-start.39 = (bf16[256,2048]{1,0:T(8,128)(2,1)S(1)}, bf16[256,2048]{1,0:T(8,128)(2,1)S(1)}, u32[]{:S(2)}, u32[]{:S(2)}) collective-permute-start(bf16[256,2048]{1,0:T(8,128)(2,1)S(1)} %get-tuple-element.314), channel_id=1, source_target_pairs={{0,1},{1,0},{2,3},{3,2},{4,5},{5,4},{6,7},{7,6},{8,9},{9,8},{10,11... | collective-permute-start | bytes 3145736 | tf_op jit(solution)/shard_map/ppermute | solution.py:79
  283.8 20.8 %collective-permute-start.40 = (bf16[256,2048]{1,0:T(8,128)(2,1)S(1)}, bf16[256,2048]{1,0:T(8,128)(2,1)S(1)}, u32[]{:S(2)}, u32[]{:S(2)}) collective-permute-start(bf16[256,2048]{1,0:T(8,128)(2,1)S(1)} %get-tuple-element.313), channel_id=1, source_target_pairs={{0,2},{1,3},{2,0},{3,1},{4,6},{5,7},{6,4},{7,5},{8,10},{9,11},{10,... | collective-permute-start | bytes 3145736 | tf_op jit(solution)/shard_map/ppermute | solution.py:79
  308.8 42.7 %collective-permute-start.41 = (bf16[512,2048]{1,0:T(8,128)(2,1)}, bf16[512,2048]{1,0:T(8,128)(2,1)}, u32[]{:S(2)}, u32[]{:S(2)}) collective-permute-start(bf16[512,2048]{1,0:T(8,128)(2,1)} %pad_maximum_fusion.3), channel_id=1, source_target_pairs={{0,2},{1,3},{2,0},{3,1},{4,6},{5,7},{6,4},{7,5},{8,10},{9,11},{10,... | collective-permute-start | bytes 6291464 | tf_op jit(solution)/shard_map/ppermute | solution.py:79
  308.9 42.6 %collective-permute-start.42 = (bf16[512,2048]{1,0:T(8,128)(2,1)}, bf16[512,2048]{1,0:T(8,128)(2,1)}, u32[]{:S(2)}, u32[]{:S(2)}) collective-permute-start(bf16[512,2048]{1,0:T(8,128)(2,1)} %pad_maximum_fusion.2), channel_id=1, source_target_pairs={{0,1},{1,0},{2,3},{3,2},{4,5},{5,4},{6,7},{7,6},{8,9},{9,8},{10,11... | collective-permute-start | bytes 6291464 | tf_op jit(solution)/shard_map/ppermute | solution.py:79
  371.4 41.5 %collective-permute-start.43 = (bf16[512,2048]{1,0:T(8,128)(2,1)S(1)}, bf16[512,2048]{1,0:T(8,128)(2,1)S(1)}, u32[]{:S(2)}, u32[]{:S(2)}) collective-permute-start(bf16[512,2048]{1,0:T(8,128)(2,1)S(1)} %convert_element_type.362), channel_id=1, source_target_pairs={{0,1},{1,0},{2,3},{3,2},{4,5},{5,4},{6,7},{7,6},{8,9},{9,8},{10,11... | collective-permute-start | bytes 6291464 | tf_op jit(solution)/shard_map/ppermute | solution.py:79
  371.8 41.1 %collective-permute-start.44 = (bf16[512,2048]{1,0:T(8,128)(2,1)S(1)}, bf16[512,2048]{1,0:T(8,128)(2,1)S(1)}, u32[]{:S(2)}, u32[]{:S(2)}) collective-permute-start(bf16[512,2048]{1,0:T(8,128)(2,1)S(1)} %convert_element_type.362), channel_id=1, source_target_pairs={{0,2},{1,3},{2,0},{3,1},{4,6},{5,7},{6,4},{7,5},{8,10},{9,11},{10,... | collective-permute-start | bytes 6291464 | tf_op jit(solution)/shard_map/ppermute | solution.py:79
  413.0 21.5 %collective-permute-start.45 = (bf16[256,2048]{1,0:T(8,128)(2,1)S(1)}, bf16[256,2048]{1,0:T(8,128)(2,1)S(1)}, u32[]{:S(2)}, u32[]{:S(2)}) collective-permute-start(bf16[256,2048]{1,0:T(8,128)(2,1)S(1)} %slice.354), channel_id=1, source_target_pairs={{0,2},{1,3},{2,0},{3,1},{4,6},{5,7},{6,4},{7,5},{8,10},{9,11},{10,... | collective-permute-start | bytes 3145736 | tf_op jit(solution)/shard_map/ppermute | solution.py:79
  414.2 20.4 %collective-permute-start.46 = (bf16[256,2048]{1,0:T(8,128)(2,1)S(1)}, bf16[256,2048]{1,0:T(8,128)(2,1)S(1)}, u32[]{:S(2)}, u32[]{:S(2)}) collective-permute-start(bf16[256,2048]{1,0:T(8,128)(2,1)S(1)} %slice.355), channel_id=1, source_target_pairs={{0,1},{1,0},{2,3},{3,2},{4,5},{5,4},{6,7},{7,6},{8,9},{9,8},{10,11... | collective-permute-start | bytes 3145736 | tf_op jit(solution)/shard_map/ppermute | solution.py:79
  462.8 221.7 %reduce-scatter.7.cloned.1.call-start = ((), (), s32[]{:S(2)}) async-start(), calls=%async_computation.11 | async-start | bytes 6488064 | tf_op jit(solution)/shard_map/reduce_scatter | solution.py:655
  463.1 21.3 %collective-permute-start.47 = (bf16[256,2048]{1,0:T(8,128)(2,1)S(1)}, bf16[256,2048]{1,0:T(8,128)(2,1)S(1)}, u32[]{:S(2)}, u32[]{:S(2)}) collective-permute-start(bf16[256,2048]{1,0:T(8,128)(2,1)S(1)} %get-tuple-element.312), channel_id=1, source_target_pairs={{0,1},{1,0},{2,3},{3,2},{4,5},{5,4},{6,7},{7,6},{8,9},{9,8},{10,11... | collective-permute-start | bytes 3145736 | tf_op jit(solution)/shard_map/ppermute | solution.py:79
  464.3 20.1 %collective-permute-start.48 = (bf16[256,2048]{1,0:T(8,128)(2,1)S(1)}, bf16[256,2048]{1,0:T(8,128)(2,1)S(1)}, u32[]{:S(2)}, u32[]{:S(2)}) collective-permute-start(bf16[256,2048]{1,0:T(8,128)(2,1)S(1)} %get-tuple-element.311), channel_id=1, source_target_pairs={{0,2},{1,3},{2,0},{3,1},{4,6},{5,7},{6,4},{7,5},{8,10},{9,11},{10,... | collective-permute-start | bytes 3145736 | tf_op jit(solution)/shard_map/ppermute | solution.py:79
  488.5 38.8 %collective-permute-start.49 = (bf16[512,2048]{1,0:T(8,128)(2,1)}, bf16[512,2048]{1,0:T(8,128)(2,1)S(1)}, u32[]{:S(2)}, u32[]{:S(2)}) collective-permute-start(bf16[512,2048]{1,0:T(8,128)(2,1)} %pad_maximum_fusion.5), channel_id=1, source_target_pairs={{0,2},{1,3},{2,0},{3,1},{4,6},{5,7},{6,4},{7,5},{8,10},{9,11},{10,... | collective-permute-start | bytes 6291464 | tf_op jit(solution)/shard_map/ppermute | solution.py:79
  488.9 38.8 %collective-permute-start.50 = (bf16[512,2048]{1,0:T(8,128)(2,1)}, bf16[512,2048]{1,0:T(8,128)(2,1)}, u32[]{:S(2)}, u32[]{:S(2)}) collective-permute-start(bf16[512,2048]{1,0:T(8,128)(2,1)} %pad_maximum_fusion.4), channel_id=1, source_target_pairs={{0,1},{1,0},{2,3},{3,2},{4,5},{5,4},{6,7},{7,6},{8,9},{9,8},{10,11... | collective-permute-start | bytes 6291464 | tf_op jit(solution)/shard_map/ppermute | solution.py:79
  527.7 156.8 %reduce-scatter.9.cloned.1.call-start = ((), (), s32[]{:S(2)}) async-start(), calls=%async_computation.12 | async-start | bytes 6488064 | tf_op jit(solution)/shard_map/reduce_scatter | solution.py:655
  549.0 24.6 %all-to-all-start = ((bf16[4,512,512]{2,1,0:T(8,128)(2,1)}), bf16[4,512,512]{2,1,0:T(8,128)(2,1)S(1)}, u32[]{:S(2)}, u32[]{:S(2)}) async-start(bf16[4,512,512]{2,1,0:T(8,128)(2,1)} %bitcast.303), calls=%async_computation | async-start | bytes 4194304 | tf_op jit(solution)/shard_map/all_to_all | solution.py:70
  552.6 232.4 %reduce-scatter.11.cloned.1.call-start = ((), (), s32[]{:S(2)}) async-start(), calls=%async_computation.13 | async-start | bytes 9437184 | tf_op jit(solution)/shard_map/reduce_scatter | solution.py:670
  609.6 31.5 %collective-permute-start.51 = (bf16[256,2048]{1,0:T(8,128)(2,1)S(1)}, bf16[256,2048]{1,0:T(8,128)(2,1)S(1)}, u32[]{:S(2)}, u32[]{:S(2)}) collective-permute-start(bf16[256,2048]{1,0:T(8,128)(2,1)S(1)} %get-tuple-element.289), channel_id=1, source_target_pairs={{0,1},{1,0},{2,3},{3,2},{4,5},{5,4},{6,7},{7,6},{8,9},{9,8},{10,11... | collective-permute-start | bytes 3145736 | tf_op jit(solution)/shard_map/ppermute | solution.py:79
  609.6 31.5 %collective-permute-start.52 = (bf16[256,2048]{1,0:T(8,128)(2,1)S(1)}, bf16[256,2048]{1,0:T(8,128)(2,1)S(1)}, u32[]{:S(2)}, u32[]{:S(2)}) collective-permute-start(bf16[256,2048]{1,0:T(8,128)(2,1)S(1)} %get-tuple-element.288), channel_id=1, source_target_pairs={{0,2},{1,3},{2,0},{3,1},{4,6},{5,7},{6,4},{7,5},{8,10},{9,11},{10,... | collective-permute-start | bytes 3145736 | tf_op jit(solution)/shard_map/ppermute | solution.py:79
  610.0 41.2 %collective-permute-start.53 = (bf16[256,2048]{1,0:T(8,128)(2,1)S(1)}, bf16[256,2048]{1,0:T(8,128)(2,1)S(1)}, u32[]{:S(2)}, u32[]{:S(2)}) collective-permute-start(bf16[256,2048]{1,0:T(8,128)(2,1)S(1)} %get-tuple-element.287), channel_id=1, source_target_pairs={{0,3},{1,2},{2,1},{3,0},{4,7},{5,6},{6,5},{7,4},{8,11},{9,10},{10,... | collective-permute-start | bytes 3145736 | tf_op jit(solution)/shard_map/ppermute | solution.py:79
  654.3 37.4 %collective-permute-start.58 = (bf16[256,2048]{1,0:T(8,128)(2,1)}, bf16[256,2048]{1,0:T(8,128)(2,1)}, u32[]{:S(2)}, u32[]{:S(2)}) collective-permute-start(bf16[256,2048]{1,0:T(8,128)(2,1)} %get-tuple-element.285), channel_id=1, source_target_pairs={{0,1},{1,0},{2,3},{3,2},{4,5},{5,4},{6,7},{7,6},{8,9},{9,8},{10,11... | collective-permute-start | bytes 3145736 | tf_op jit(solution)/shard_map/ppermute | solution.py:79
  654.3 71.7 %collective-permute-start.59 = (bf16[256,2048]{1,0:T(8,128)(2,1)}, bf16[256,2048]{1,0:T(8,128)(2,1)}, u32[]{:S(2)}, u32[]{:S(2)}) collective-permute-start(bf16[256,2048]{1,0:T(8,128)(2,1)} %get-tuple-element.284), channel_id=1, source_target_pairs={{0,2},{1,3},{2,0},{3,1},{4,6},{5,7},{6,4},{7,5},{8,10},{9,11},{10,... | collective-permute-start | bytes 3145736 | tf_op jit(solution)/shard_map/ppermute | solution.py:79
  656.1 11.6 %collective-permute-start.54 = (bf16[4,16,1536]{2,1,0:T(8,128)(2,1)S(1)}, bf16[4,16,1536]{2,1,0:T(8,128)(2,1)S(1)}, u32[]{:S(2)}, u32[]{:S(2)}) collective-permute-start(bf16[4,16,1536]{2,1,0:T(8,128)(2,1)S(1)} %bitcast.324), channel_id=1, source_target_pairs={{0,4},{4,0},{8,12},{12,8},{16,20},{20,16},{24,28},{28,24},{1,5},{5... | collective-permute-start | bytes 589832 | tf_op jit(solution)/shard_map/ppermute | solution.py:83
  674.7 51.2 %collective-permute-start.60 = (bf16[256,2048]{1,0:T(8,128)(2,1)}, bf16[256,2048]{1,0:T(8,128)(2,1)}, u32[]{:S(2)}, u32[]{:S(2)}) collective-permute-start(bf16[256,2048]{1,0:T(8,128)(2,1)} %get-tuple-element.283), channel_id=1, source_target_pairs={{0,3},{1,2},{2,1},{3,0},{4,7},{5,6},{6,5},{7,4},{8,11},{9,10},{10,... | collective-permute-start | bytes 3145736 | tf_op jit(solution)/shard_map/ppermute | solution.py:79
  679.4 46.4 %all-to-all-start.1 = ((bf16[32,5,2048]{2,1,0:T(8,128)(2,1)}), bf16[32,5,2048]{2,1,0:T(8,128)(2,1)S(1)}, u32[]{:S(2)}, u32[]{:S(2)}) async-start(bf16[32,5,2048]{2,1,0:T(8,128)(2,1)} %pad_maximum_fusion.8), calls=%async_computation.4 | async-start | bytes 2097152 | tf_op jit(solution)/shard_map/all_to_all | solution.py:70
  689.3 36.7 %collective-permute-start.61 = (bf16[64,4224]{1,0:T(8,128)(2,1)}, bf16[64,4224]{1,0:T(8,128)(2,1)S(1)}, u32[]{:S(2)}, u32[]{:S(2)}) collective-permute-start(bf16[64,4224]{1,0:T(8,128)(2,1)} %get-tuple-element.302), channel_id=1, source_target_pairs={{0,1},{1,0},{2,3},{3,2},{4,5},{5,4},{6,7},{7,6},{8,9},{9,8},{10,11... | collective-permute-start | bytes 1622024 | tf_op jit(solution)/shard_map/ppermute | solution.py:79
  690.5 37.7 %collective-permute-start.62 = (bf16[64,4224]{1,0:T(8,128)(2,1)}, bf16[64,4224]{1,0:T(8,128)(2,1)S(1)}, u32[]{:S(2)}, u32[]{:S(2)}) collective-permute-start(bf16[64,4224]{1,0:T(8,128)(2,1)} %get-tuple-element.301), channel_id=1, source_target_pairs={{0,2},{1,3},{2,0},{3,1},{4,6},{5,7},{6,4},{7,5},{8,10},{9,11},{10,... | collective-permute-start | bytes 1622024 | tf_op jit(solution)/shard_map/ppermute | solution.py:79
  691.7 44.8 %collective-permute-start.63 = (bf16[64,4224]{1,0:T(8,128)(2,1)}, bf16[64,4224]{1,0:T(8,128)(2,1)S(1)}, u32[]{:S(2)}, u32[]{:S(2)}) collective-permute-start(bf16[64,4224]{1,0:T(8,128)(2,1)} %get-tuple-element.300), channel_id=1, source_target_pairs={{0,3},{1,2},{2,1},{3,0},{4,7},{5,6},{6,5},{7,4},{8,11},{9,10},{10,... | collective-permute-start | bytes 1622024 | tf_op jit(solution)/shard_map/ppermute | solution.py:79
  747.5 10.4 %collective-permute-start.67 = (bf16[4,16,1536]{2,1,0:T(8,128)(2,1)S(1)}, bf16[4,16,1536]{2,1,0:T(8,128)(2,1)S(1)}, u32[]{:S(2)}, u32[]{:S(2)}) collective-permute-start(bf16[4,16,1536]{2,1,0:T(8,128)(2,1)S(1)} %get-tuple-element.346), channel_id=1, source_target_pairs={{0,4},{4,0},{8,12},{12,8},{16,20},{20,16},{24,28},{28,24},{1,5},{5... | collective-permute-start | bytes 589832 | tf_op jit(solution)/shard_map/ppermute | solution.py:83
  758.5 29.3 %collective-permute-start.68 = (bf16[64,1536]{1,0:T(8,128)(2,1)S(1)}, bf16[64,1536]{1,0:T(8,128)(2,1)S(1)}, u32[]{:S(2)}, u32[]{:S(2)}) collective-permute-start(bf16[64,1536]{1,0:T(8,128)(2,1)S(1)} %get-tuple-element.328), channel_id=1, source_target_pairs={{0,1},{1,0},{2,3},{3,2},{4,5},{5,4},{6,7},{7,6},{8,9},{9,8},{10,11... | collective-permute-start | bytes 589832 | tf_op jit(solution)/shard_map/ppermute | solution.py:79
  758.6 38.4 %collective-permute-start.69 = (bf16[64,1536]{1,0:T(8,128)(2,1)S(1)}, bf16[64,1536]{1,0:T(8,128)(2,1)S(1)}, u32[]{:S(2)}, u32[]{:S(2)}) collective-permute-start(bf16[64,1536]{1,0:T(8,128)(2,1)S(1)} %get-tuple-element.327), channel_id=1, source_target_pairs={{0,2},{1,3},{2,0},{3,1},{4,6},{5,7},{6,4},{7,5},{8,10},{9,11},{10,... | collective-permute-start | bytes 589832 | tf_op jit(solution)/shard_map/ppermute | solution.py:79
  758.6 38.3 %collective-permute-start.70 = (bf16[64,1536]{1,0:T(8,128)(2,1)S(1)}, bf16[64,1536]{1,0:T(8,128)(2,1)S(1)}, u32[]{:S(2)}, u32[]{:S(2)}) collective-permute-start(bf16[64,1536]{1,0:T(8,128)(2,1)S(1)} %get-tuple-element.326), channel_id=1, source_target_pairs={{0,3},{1,2},{2,1},{3,0},{4,7},{5,6},{6,5},{7,4},{8,11},{9,10},{10,... | collective-permute-start | bytes 589832 | tf_op jit(solution)/shard_map/ppermute | solution.py:79
  786.4 11.8 %collective-permute-start.71 = (bf16[64,2048]{1,0:T(8,128)(2,1)S(1)}, bf16[64,2048]{1,0:T(8,128)(2,1)S(1)}, u32[]{:S(2)}, u32[]{:S(2)}) collective-permute-start(bf16[64,2048]{1,0:T(8,128)(2,1)S(1)} %get-tuple-element.315), channel_id=1, source_target_pairs={{0,1},{1,0},{2,3},{3,2},{4,5},{5,4},{6,7},{7,6},{8,9},{9,8},{10,11... | collective-permute-start | bytes 786440 | tf_op jit(solution)/shard_map/ppermute | solution.py:79
  787.4 10.9 %collective-permute-start.72 = (bf16[64,2048]{1,0:T(8,128)(2,1)S(1)}, bf16[64,2048]{1,0:T(8,128)(2,1)S(1)}, u32[]{:S(2)}, u32[]{:S(2)}) collective-permute-start(bf16[64,2048]{1,0:T(8,128)(2,1)S(1)} %get-tuple-element.317), channel_id=1, source_target_pairs={{0,2},{1,3},{2,0},{3,1},{4,6},{5,7},{6,4},{7,5},{8,10},{9,11},{10,... | collective-permute-start | bytes 786440 | tf_op jit(solution)/shard_map/ppermute | solution.py:79
  787.8 10.5 %collective-permute-start.73 = (bf16[64,2048]{1,0:T(8,128)(2,1)S(1)}, bf16[64,2048]{1,0:T(8,128)(2,1)S(1)}, u32[]{:S(2)}, u32[]{:S(2)}) collective-permute-start(bf16[64,2048]{1,0:T(8,128)(2,1)S(1)} %get-tuple-element.316), channel_id=1, source_target_pairs={{0,3},{1,2},{2,1},{3,0},{4,7},{5,6},{6,5},{7,4},{8,11},{9,10},{10,... | collective-permute-start | bytes 786440 | tf_op jit(solution)/shard_map/ppermute | solution.py:79
  (133 other events, 2012.4 us)
Sparse Core Ops, SparseCore 0:
  87.9 62.7 all-gather.4
  152.9 59.1 all-gather.6
  214.3 59.0 all-gather.8
  275.5 63.2 all-gather.10
  463.0 70.9 reduce-scatter.4
  536.1 63.8 reduce-scatter.6
  602.3 63.5 reduce-scatter.8
  668.1 116.8 reduce-scatter.10
